TPU v7x, 32 devices: a whole 2x2x4 slice. The times are simulated.
32 devices in a mesh: ctx: 8 (over z, y), shard: 4 (over x, core).
Axes of the slice: x: 2, y: 2, z: 4, core: 2. Of those that a mesh axis runs over, the one named last changes fastest.
Arguments:
- tokens: bfloat16 [8, 1024, 1024], P('shard', 'ctx'), may hold values from -6 to 6
- cotangent: bfloat16 [8, 1024, 1024], P('shard', 'ctx'), may hold values from -6 to 6
- lengths: int32 [8], P('shard'), may hold values from 256 to 1024, as said below
- unit_owner: int32 [187], replicated, may hold values from 0 to 3, as said below
- master: float32 [280, 64, 1024], P('shard'), as said below
- first_moment: float32 [280, 64, 1024], P('shard')
- second_moment: float32 [280, 64, 1024], P('shard'), as said below
- norm_gains: float32 [2, 1024], replicated, may hold values from 0.5 to 1.5
- gain_first: float32 [2, 1024], replicated
- gain_second: float32 [2, 1024], replicated, as said below
Outputs:
- output: bfloat16 [8, 1024, 1024], P('shard', 'ctx')
- token_grad: bfloat16 [8, 1024, 1024], P('shard', 'ctx')
- new_master: float32 [280, 64, 1024], P('shard')
- new_first: float32 [280, 64, 1024], P('shard')
- new_second: float32 [280, 64, 1024], P('shard')
- new_gains: float32 [2, 1024], replicated
- new_gain_first: float32 [2, 1024], replicated
- new_gain_second: float32 [2, 1024], replicated
Inputs may be any that keep to these rules, and one draw needn't show every extreme that they name: Slot s holds lengths[s] real tokens, then padding; in each aligned group of 2 slots one slot is full. `unit_owner`: no owner holds more than 70 units; one owner holds exactly 70. `master`: slots that no unit maps to are unused. `second_moment`: all entries positive. `gain_second`: all entries positive.
All inputs are finite; a program needn't handle non-finite values.
Results may differ from a plain program's by a relative error of at most 0.018.
The roundings to bfloat16 on the way count: a program that leaves them out, or rounds other values in their place, can miss the bound.
Values may be sent and summed in bfloat16 or wider, within the bound.
A program may use at most 384 MiB of HBM per device.

v0:
```python
import jax
import jax.numpy as jnp
from jax import lax
from jax.sharding import PartitionSpec as P

HEADS = 16
HEAD_DIM = 64
FF = 2624
STEP = 10


eps_norm = 1e-05
rope_base = 160000.0
mask_fill = -1e30
beta_one = 0.9
beta_two = 0.98
adam_eps = 1e-06
rate_matrix = 0.03
rate_gain = 0.6
decay_matrix = 0.01


def passed_along(block, axis, distance):
    devices = range(lax.axis_size(axis))
    route = [((i - distance) % len(devices), i) for i in devices]
    return lax.ppermute(block, axis, route)


def transposed(left, right):
    return lax.dot_general(
        left, right, (((1,), (1,)), ((), ())), preferred_element_type=jnp.float32
    )


def leading(left, right):
    return lax.dot_general(
        left, right, (((0,), (0,)), ((), ())), preferred_element_type=jnp.float32
    )


def layer_norm(values, gain):
    row_mean = jnp.mean(values, axis=-1, keepdims=True)
    centred = values - row_mean
    variance = jnp.mean(centred * centred, axis=-1, keepdims=True)
    return centred * lax.rsqrt(variance + eps_norm) * gain


def rope_tables(positions):
    half_dim = HEAD_DIM // 2
    inverse = rope_base ** (-2.0 * jnp.arange(half_dim, dtype=jnp.float32) / HEAD_DIM)
    angles = positions.astype(jnp.float32)[:, None] * inverse[None, :]
    angles = jnp.concatenate([angles, angles], axis=1)
    return (jnp.cos(angles), jnp.sin(angles))


def rotate(values, cosine, sine_table):
    half_dim = HEAD_DIM // 2
    turned = jnp.concatenate([-values[..., half_dim:], values[..., :half_dim]], axis=-1)
    return values * cosine[:, None, :] + turned * sine_table[:, None, :]


def unit_places(unit_owner, capacity, groups):
    owner_marks = (unit_owner[:, None] == jnp.arange(groups, dtype=jnp.int32)[None, :]).astype(
        jnp.int32
    )
    owner_ranks = jnp.cumsum(owner_marks, axis=0) - 1
    slot_index = jnp.sum(owner_ranks * owner_marks, axis=1)
    return unit_owner * capacity + slot_index


def gated_gelu(upper_proj):
    return jax.nn.gelu(upper_proj[:, :FF], approximate=False) * upper_proj[:, FF:]


def adam_update(weight, gradient, first_old, second_old, step_rate, weight_decay):
    first_new = beta_one * first_old + (1.0 - beta_one) * gradient
    second_new = beta_two * second_old + (1.0 - beta_two) * gradient * gradient
    first_fix = 1.0 - beta_one**STEP
    second_fix = 1.0 - beta_two**STEP
    adam_step = first_new / first_fix / (jnp.sqrt(second_new / second_fix) + adam_eps)
    return (weight - step_rate * (adam_step + weight_decay * weight), first_new, second_new)


def split_stack(stacked, model_width):
    return (
        stacked[: 3 * model_width],
        stacked[3 * model_width : 4 * model_width],
        stacked[4 * model_width : 4 * model_width + 2 * FF],
        stacked[4 * model_width + 2 * FF :],
    )


def score_block(query_low, key_block, key_start, lengths):
    slot_count, key_rows = (key_block.shape[0], key_block.shape[1])
    key_heads = key_block.reshape(slot_count, key_rows, HEADS, HEAD_DIM)
    scores = (
        jnp.einsum("sqhd,skhd->shqk", query_low, key_heads, preferred_element_type=jnp.float32)
        * 0.125
    )
    key_pos = key_start + jnp.arange(key_rows, dtype=jnp.int32)
    live_keys = key_pos[None, :] < lengths[:, None]
    return (scores, live_keys[:, None, None, :])


def back_block(
    key_block, value_block, key_start, query_low, grad_heads, row_lse, row_delta, lengths
):
    slot_count, key_rows = (key_block.shape[0], key_block.shape[1])
    scores, live_keys = score_block(query_low, key_block, key_start, lengths)
    weights = jnp.where(live_keys, jnp.exp(scores - row_lse[..., None]), 0.0)
    key_heads = key_block.reshape(slot_count, key_rows, HEADS, HEAD_DIM)
    value_heads = value_block.reshape(slot_count, key_rows, HEADS, HEAD_DIM)
    grad_values = jnp.einsum(
        "shqk,sqhd->skhd",
        weights.astype(jnp.bfloat16),
        grad_heads,
        preferred_element_type=jnp.float32,
    )
    grad_weights = jnp.einsum(
        "sqhd,skhd->shqk", grad_heads, value_heads, preferred_element_type=jnp.float32
    )
    grad_scores = (weights * (grad_weights - row_delta[..., None])).astype(jnp.bfloat16)
    grad_query = (
        jnp.einsum("shqk,skhd->sqhd", grad_scores, key_heads, preferred_element_type=jnp.float32)
        * 0.125
    )
    grad_keys = (
        jnp.einsum("shqk,sqhd->skhd", grad_scores, query_low, preferred_element_type=jnp.float32)
        * 0.125
    )
    return (
        grad_query,
        grad_keys.reshape(slot_count, key_rows, -1),
        grad_values.reshape(slot_count, key_rows, -1),
    )


def shards(
    tokens,
    cotangent,
    lengths,
    unit_owner,
    master,
    first_moment,
    second_moment,
    norm_gains,
    gain_first,
    gain_second,
):
    slot_count, block_len, model_width = tokens.shape
    groups = lax.axis_size("shard")
    devices = lax.axis_size("ctx")
    ctx_index = lax.axis_index("ctx")
    capacity = master.shape[0]
    unit_rows = master.shape[1]
    rows_all = slot_count * block_len
    places = unit_places(unit_owner, capacity, groups)
    master_low = master.astype(jnp.bfloat16)
    gathered = lax.all_gather(master_low, "shard", axis=0, tiled=True)
    stacked = jnp.take(gathered, places, axis=0).reshape(-1, model_width)
    w_qkv, w_out, w_up, w_down = split_stack(stacked, model_width)
    positions = ctx_index * block_len + jnp.arange(block_len, dtype=jnp.int32)
    cosine, sine_table = rope_tables(positions)
    live_rows = (positions[None, :] < lengths[:, None]).astype(jnp.float32)
    inputs = tokens.astype(jnp.float32).reshape(rows_all, model_width)
    norm_one = layer_norm(inputs, norm_gains[0]).astype(jnp.bfloat16)
    qkv_proj = transposed(norm_one, w_qkv).reshape(slot_count, block_len, 3 * model_width)
    head_shape = (slot_count, block_len, HEADS, HEAD_DIM)
    query_low = rotate(qkv_proj[..., :model_width].reshape(head_shape), cosine, sine_table).astype(
        jnp.bfloat16
    )
    key_low = (
        rotate(qkv_proj[..., model_width : 2 * model_width].reshape(head_shape), cosine, sine_table)
        .reshape(slot_count, block_len, model_width)
        .astype(jnp.bfloat16)
    )
    value_low = qkv_proj[..., 2 * model_width :].astype(jnp.bfloat16)
    stat_shape = (slot_count, HEADS, block_len)
    piece_rows = lax.all_gather(key_low, "ctx", axis=1, tiled=True)

    def stats_one_block(block_index, running):
        row_top, row_total = running
        key_block = lax.dynamic_slice_in_dim(piece_rows, block_index * block_len, block_len, 1)
        scores, live_keys = score_block(query_low, key_block, block_index * block_len, lengths)
        scores = jnp.where(live_keys, scores, mask_fill)
        new_top = jnp.maximum(row_top, jnp.max(scores, axis=-1))
        new_total = row_total * jnp.exp(row_top - new_top) + jnp.sum(
            jnp.where(live_keys, jnp.exp(scores - new_top[..., None]), 0.0), axis=-1
        )
        return (new_top, new_total)

    row_top, row_total = lax.fori_loop(
        0,
        piece_rows.shape[1] // block_len,
        stats_one_block,
        (jnp.full(stat_shape, mask_fill, jnp.float32), jnp.zeros(stat_shape, jnp.float32)),
    )
    row_lse = row_top + jnp.log(row_total)
    key_piece = lax.all_gather(key_low, "ctx", axis=1, tiled=True)
    value_piece = lax.all_gather(value_low, "ctx", axis=1, tiled=True)

    def value_one_block(block_index, running):
        key_block = lax.dynamic_slice_in_dim(key_piece, block_index * block_len, block_len, 1)
        value_block = lax.dynamic_slice_in_dim(value_piece, block_index * block_len, block_len, 1)
        scores, live_keys = score_block(query_low, key_block, block_index * block_len, lengths)
        weights = jnp.where(live_keys, jnp.exp(scores - row_lse[..., None]), 0.0).astype(
            jnp.bfloat16
        )
        value_heads = value_block.reshape(slot_count, block_len, HEADS, HEAD_DIM)
        added_part = jnp.einsum(
            "shqk,skhd->sqhd", weights, value_heads, preferred_element_type=jnp.float32
        )
        return running + added_part.reshape(running.shape)

    attended = lax.fori_loop(
        0,
        key_piece.shape[1] // block_len,
        value_one_block,
        jnp.zeros((slot_count, block_len, model_width), jnp.float32),
    )
    mixed_low = attended.astype(jnp.bfloat16).reshape(rows_all, model_width)
    middle = inputs + transposed(mixed_low, w_out)
    norm_two = layer_norm(middle, norm_gains[1]).astype(jnp.bfloat16)
    upper_proj = transposed(norm_two, w_up)
    hidden_low = gated_gelu(upper_proj).astype(jnp.bfloat16)
    result = middle + jnp.dot(hidden_low, w_down, preferred_element_type=jnp.float32)
    output = result.astype(jnp.bfloat16).reshape(slot_count, block_len, model_width)
    regathered = lax.all_gather(master_low, "shard", axis=0, tiled=True)
    back_stack = jnp.take(regathered, places, axis=0).reshape(-1, model_width)
    back_qkv, back_out, back_up, back_down = split_stack(back_stack, model_width)
    grad_result = cotangent.astype(jnp.float32).reshape(rows_all, model_width) * live_rows.reshape(
        rows_all, 1
    )
    grad_down_low = grad_result.astype(jnp.bfloat16)
    grad_w_down = leading(hidden_low, grad_down_low)
    grad_hidden = transposed(grad_down_low, back_down)
    gelu_value, gelu_back = jax.vjp(gated_gelu, upper_proj)
    grad_upper_low = gelu_back(grad_hidden)[0].astype(jnp.bfloat16)
    grad_w_up = leading(grad_upper_low, norm_two)
    grad_norm_two = jnp.dot(grad_upper_low, back_up, preferred_element_type=jnp.float32)
    norm_value, norm_back_two = jax.vjp(layer_norm, middle, norm_gains[1])
    grad_middle_part, grad_gain_two = norm_back_two(grad_norm_two)
    grad_middle = grad_result + grad_middle_part
    grad_attn_low = grad_middle.astype(jnp.bfloat16)
    grad_w_out = leading(grad_attn_low, mixed_low)
    grad_heads = (
        jnp.dot(grad_attn_low, back_out, preferred_element_type=jnp.float32)
        .astype(jnp.bfloat16)
        .reshape(head_shape)
    )
    row_delta = jnp.transpose(
        jnp.sum(grad_heads.astype(jnp.float32) * attended.reshape(head_shape), axis=-1), (0, 2, 1)
    )

    def send_grads(grad_keys, grad_values):
        return (
            passed_along(grad_keys.astype(jnp.bfloat16), "ctx", 1).astype(grad_keys.dtype),
            passed_along(grad_values.astype(jnp.bfloat16), "ctx", 1).astype(grad_values.dtype),
        )

    def key_turn(turn_index, carried):
        key_now, value_now, grad_keys, grad_values, grad_query = carried
        source = (ctx_index - turn_index) % devices
        part_query, part_keys, part_values = back_block(
            key_now,
            value_now,
            source * block_len,
            query_low,
            grad_heads,
            row_lse,
            row_delta,
            lengths,
        )
        grad_keys, grad_values = send_grads(grad_keys + part_keys, grad_values + part_values)
        key_now, value_now = passed_along((key_now, value_now), "ctx", 1)
        return (key_now, value_now, grad_keys, grad_values, grad_query + part_query)

    empty_rows = jnp.zeros((slot_count, block_len, model_width), jnp.float32)
    key_now, value_now, grad_keys, grad_values, grad_query = lax.fori_loop(
        0,
        devices - 1,
        key_turn,
        (key_low, value_low, empty_rows, empty_rows, jnp.zeros(head_shape, jnp.float32)),
    )
    source = (ctx_index + 1) % devices
    part_query, part_keys, part_values = back_block(
        key_now, value_now, source * block_len, query_low, grad_heads, row_lse, row_delta, lengths
    )
    grad_keys, grad_values = send_grads(grad_keys + part_keys, grad_values + part_values)
    grad_query = grad_query + part_query
    query_back = rotate(grad_query, cosine, -sine_table).reshape(rows_all, model_width)
    keys_back = rotate(grad_keys.reshape(head_shape), cosine, -sine_table).reshape(
        rows_all, model_width
    )
    grad_qkv_low = jnp.concatenate(
        [query_back, keys_back, grad_values.reshape(rows_all, model_width)], axis=1
    ).astype(jnp.bfloat16)
    grad_w_qkv = leading(grad_qkv_low, norm_one)
    grad_norm_one = jnp.dot(grad_qkv_low, back_qkv, preferred_element_type=jnp.float32)
    first_value, norm_back_one = jax.vjp(layer_norm, inputs, norm_gains[0])
    grad_input_part, grad_gain_one = norm_back_one(grad_norm_one)
    token_grad = (
        (grad_middle + grad_input_part)
        .astype(jnp.bfloat16)
        .reshape(slot_count, block_len, model_width)
    )
    unit_grads = jnp.concatenate([grad_w_qkv, grad_w_out, grad_w_up, grad_w_down], axis=0).reshape(
        -1, unit_rows, model_width
    )
    gain_terms = jnp.broadcast_to(
        jnp.stack([grad_gain_one, grad_gain_two])[None], (groups, 2, model_width)
    )
    grad_buffer = (
        jnp.zeros((groups * capacity, unit_rows, model_width), jnp.float32)
        .at[places]
        .set(unit_grads)
    )
    owned_part, gain_part = (
        lax.psum_scatter(
            grad_buffer.astype(jnp.bfloat16), "shard", scatter_dimension=0, tiled=True
        ).astype(jnp.float32),
        lax.psum_scatter(
            gain_terms.astype(jnp.bfloat16), "shard", scatter_dimension=0, tiled=True
        ).astype(jnp.float32),
    )
    owned_grads, gain_total = (
        lax.psum(owned_part.astype(jnp.bfloat16), "ctx").astype(jnp.float32),
        lax.psum(gain_part.astype(jnp.bfloat16), "ctx").astype(jnp.float32),
    )
    gain_grad = gain_total[0]
    new_master, new_first, new_second = adam_update(
        master, owned_grads, first_moment, second_moment, rate_matrix, decay_matrix
    )
    new_gains, new_gain_first, new_gain_second = adam_update(
        norm_gains, gain_grad, gain_first, gain_second, rate_gain, 0.0
    )
    return (
        output,
        token_grad,
        new_master,
        new_first,
        new_second,
        new_gains,
        new_gain_first,
        new_gain_second,
    )


def solution(mesh):
    return jax.shard_map(
        shards,
        mesh=mesh,
        in_specs=(
            P("shard", "ctx", None),
            P("shard", "ctx", None),
            P("shard"),
            P(),
            P("shard", None, None),
            P("shard", None, None),
            P("shard", None, None),
            P(),
            P(),
            P(),
        ),
        out_specs=(
            P("shard", "ctx", None),
            P("shard", "ctx", None),
            P("shard", None, None),
            P("shard", None, None),
            P("shard", None, None),
            P(),
            P(),
            P(),
        ),
        check_vma=False,
    )
```

profile of v0, /device:TPU:0, one launch (start us, length us, event | category | flops | bytes accessed | tf_op | source)
XLA Modules:
  0.0 1762.1 jit_solution(17837427015020761361)
XLA Ops:
  7.2 11.2 convert_element_type.176
  25.3 217.4 %all-gather.4.cloned.1.call-done = bf16[280,64,1024]{2,1,0:T(8,128)(2,1)} async-done(((bf16[70,64,1024]{2,1,0:T(8,128)(2,1)}), bf16[280,64,1024]{2,1,0:T(8,128)(2,1)}) %all-gather.4.cloned.1.call-update) | async-done | bytes 36700176 | tf_op jit(solution)/shard_map/all_gather | solution.py:159
  242.7 17.3 gather_fusion
  260.0 21.3 %broadcast_select_fusion = bf16[187,64,1024]{2,1,0:T(8,128)(2,1)} fusion(bf16[187,64,1024]{2,1,0:T(8,128)(2,1)} %gather_fusion, pred[187]{0:T(512)(128)(4,1)S(1)} %get-tuple-element.765), kind=kLoop, calls=%fused_computation.43 | loop fusion | flops 12255232 | bytes 49021116 | tf_op jit(solution)/shard_map/jit(_take)/select_n | solution.py:160
  300.4 10.4 slice.126
  319.8 48.2 %all-gather.8.cloned.1.call-done = bf16[2,1024,1024]{2,1,0:T(8,128)(2,1)} async-done(((bf16[2,128,1024]{2,1,0:T(8,128)(2,1)}), bf16[2,1024,1024]{2,1,0:T(8,128)(2,1)}) %all-gather.8.cloned.1.call-update) | async-done | bytes 4194320 | tf_op jit(solution)/shard_map/all_gather | solution.py:199
  374.2 21.2 %while.54 = (s32[]{:T(128)}, f32[2,16,128]{2,1,0:T(8,128)S(1)}, f32[2,16,128]{2,1,0:T(8,128)S(1)}, s32[2]{0:T(128)S(1)}, bf16[2,1024,1024]{1,2,0:T(8,128)(2,1)},...) while((s32[]{:T(128)}, f32[2,16,128]{2,1,0:T(8,128)S(1)}, ...), condition=%wide.region_8.10_spmd.clone, body=%wide.region_5.9_spmd.clone.sunk | while | flops 71324040 | bytes 6506422 | solution.py:192
  395.5 47.0 %all-gather.6.cloned.1.call-done = bf16[2,1024,1024]{2,1,0:T(8,128)(2,1)} async-done(((bf16[2,128,1024]{2,1,0:T(8,128)(2,1)}), bf16[2,1024,1024]{2,1,0:T(8,128)(2,1)}) %all-gather.6.cloned.1.call-update) | async-done | bytes 4194320 | tf_op jit(solution)/shard_map/all_gather | solution.py:200
  442.5 55.5 %while.55 = (s32[]{:T(128)}, f32[2,128,1024]{1,2,0:T(8,128)}, bf16[2,1024,1024]{2,1,0:T(8,128)(2,1)}, s32[2]{0:T(128)S(1)}, bf16[2,1024,1024]{1,2,0:T(8,128)(2,1...) while((s32[]{:T(128)}, f32[2,128,1024]{1,2,0:T(8,128)}, ...), condition=%wide.region_10.12_spmd.clone, body=%wide.region_9.11_spmd.clone.sunk | while | flops 136839552 | bytes 17319672 | solution.py:215
  502.3 12.9 fusion.66
  515.3 11.3 fusion.37
  542.2 13.4 fusion.45
  555.6 365.6 %while.56 = (s32[]{:T(128)}, bf16[2,128,1024]{1,2,0:T(8,128)(2,1)}, bf16[2,128,1024]{1,2,0:T(8,128)(2,1)}, f32[2,128,1024]{1,2,0:T(8,128)}, f32[2,128,1024]{1,2,...) while((s32[]{:T(128)}, bf16[2,128,1024]{1,2,0:T(8,128)(2,1)}, ...), condition=%wide.region_17.19_spmd.clone, body=%wide.region_16.18_spmd.clone.sunk | while | flops 342360448 | bytes 44599308 | solution.py:279
  570.0 9.7 collective-permute-done.2
  625.1 9.4 collective-permute-done.2
  647.9 9.1 collective-permute-done
  678.1 10.5 collective-permute-done.2
  701.9 9.1 collective-permute-done
  730.2 11.5 collective-permute-done.2
  755.0 9.1 collective-permute-done
  781.4 12.5 collective-permute-done.2
  831.6 13.5 collective-permute-done.2
  882.0 13.5 collective-permute-done.2
  981.4 34.9 %pad_maximum_fusion = f32[11968,1024]{1,0:T(8,128)} fusion(f32[2624,1024]{1,0:T(8,128)} %fusion.77, f32[5248,1024]{1,0:T(8,128)} %fusion.45, f32[1024,1024]{1,0:T(8,128)} %fusion.76, f32[3072,1024]{1,0:T(8,128)} %fusion.38), kind=kLoop, calls=%fused_computation.41 | loop fusion | flops 36765696 | bytes 98041856 | tf_op jit(solution)/shard_map/concatenate | solution.py:307
  1016.3 23.3 %broadcast_in_dim.206 = f32[280,64,1024]{2,1,0:T(8,128)} broadcast(f32[]{:T(128)} %constant.275.clone.1), dimensions={} | broadcast | bytes 73400320 | tf_op jit(solution)/shard_map/broadcast_in_dim | solution.py:314
  1039.5 89.1 %scatter_fusion = f32[280,64,1024]{2,1,0:T(8,128)} fusion(f32[280,64,1024]{2,1,0:T(8,128)} %broadcast_in_dim.206, s32[187]{0:T(256)S(1)} %copy-done.48, f32[187,64,1024]{2,1,0:T(8,128)} %bitcast.231), kind=kCustom, calls=%fused_computation.1 | custom fusion | bytes 147063536 | tf_op jit(solution)/shard_map/scatter | solution.py:316
  1128.7 35.6 %convert_element_type.202 = bf16[280,64,1024]{2,1,0:T(8,128)(2,1)} convert(f32[280,64,1024]{2,1,0:T(8,128)} %scatter_fusion) | non-fusion elementwise | flops 18350080 | bytes 110100480 | tf_op jit(solution)/shard_map/convert_element_type | solution.py:320
  1164.4 252.7 %reduce-scatter.4.cloned.1.call-done = bf16[70,64,1024]{2,1,0:T(8,128)(2,1)} async-done(((bf16[280,64,1024]{2,1,0:T(8,128)(2,1)}), bf16[70,64,1024]{2,1,0:T(8,128)(2,1)}) %reduce-scatter.4.cloned.1.call-update) | async-done | bytes 9175056
  1423.4 10.5 all-reduce.4
  1434.6 22.3 %psum.15 = bf16[2,1024]{1,0:T(2,128)(2,1)S(1)} all-reduce(bf16[2,1024]{1,0:T(2,128)(2,1)S(1)} %dynamic-slice_bitcast_fusion), channel_id=1, replica_groups=mesh['ctx'=8,'shard'=4] {'ctx'}, use_global_device_ids=true, to_apply=%region_26.28 | all-reduce | flops 2048 | bytes 8192 | tf_op jit(solution)/shard_map/psum | solution.py:328
  1457.6 255.9 %all-reduce.7.cloned.1.call-done = bf16[70,64,1024]{2,1,0:T(8,128)(2,1)} async-done(((bf16[70,64,1024]{2,1,0:T(8,128)(2,1)}), bf16[70,64,1024]{2,1,0:T(8,128)(2,1)}) %all-reduce.7.cloned.1.call-update) | async-done | bytes 9175056 | tf_op jit(solution)/shard_map/psum | solution.py:327
  1713.5 41.8 %multiply_subtract_fusion = (f32[70,64,1024]{2,1,0:T(8,128)}, f32[70,64,1024]{2,1,0:T(8,128)}, f32[70,64,1024]{2,1,0:T(8,128)}) fusion(f32[70,64,1024]{2,1,0:T(8,128)} %param.22, bf16[70,64,1024]{2,1,0:T(8,128)(2,1)} %all-reduce.7.cloned.1.call-done, f32[70,64,1024]{2,1,0:T(8,128)} %param.23, f32[70,64,1024]{2,1,0:T(8,128)} %param.24), kind=kLoop, calls=%fused_computation.47 | loop fusion | flops 73400320 | bytes 119275520 | tf_op jit(solution)/shard_map/sub | solution.py:81
  (548 shorter events, 461.1 us)
Async XLA Ops:
  7.2 235.6 %all-gather.4.cloned.1.call-start = ((), (), s32[]{:S(2)}) async-start(), calls=%async_computation.1 | async-start | bytes 45875200 | tf_op jit(solution)/shard_map/all_gather | solution.py:159
  18.5 349.5 %all-gather.8.cloned.1.call-start = ((), (), s32[]{:S(2)}) async-start(), calls=%async_computation.3 | async-start | bytes 4718592 | tf_op jit(solution)/shard_map/all_gather | solution.py:199
  294.5 148.0 %all-gather.6.cloned.1.call-start = ((), (), s32[]{:S(2)}) async-start(), calls=%async_computation.2 | async-start | bytes 4718592 | tf_op jit(solution)/shard_map/all_gather | solution.py:200
  318.9 1098.2 %reduce-scatter.4.cloned.1.call-start = ((), (), s32[]{:S(2)}) async-start(), calls=%async_computation.5 | async-start | bytes 45875200
  561.7 17.9 %collective-permute-start.2 = (bf16[2,128,1024]{1,2,0:T(8,128)(2,1)}, bf16[2,128,1024]{1,2,0:T(8,128)(2,1)}, u32[]{:S(2)}, u32[]{:S(2)}) collective-permute-start(bf16[2,128,1024]{1,2,0:T(8,128)(2,1)} %fusion.156), channel_id=1, source_target_pairs={{28,0},{0,4},{4,8},{8,12},{12,16},{16,20},{20,24},{24,28},{29,1},{... | collective-permute-start | bytes 1572872 | tf_op jit(solution)/shard_map/while/body/eval_jaxpr/ppermute | solution.py:26
  563.6 27.2 %collective-permute-start.3 = (bf16[2,128,1024]{1,2,0:T(8,128)(2,1)}, bf16[2,128,1024]{1,2,0:T(8,128)(2,1)}, u32[]{:S(2)}, u32[]{:S(2)}) collective-permute-start(bf16[2,128,1024]{1,2,0:T(8,128)(2,1)} %fusion.158), channel_id=1, source_target_pairs={{28,0},{0,4},{4,8},{8,12},{12,16},{16,20},{20,24},{24,28},{29,1},{... | collective-permute-start | bytes 1572872 | tf_op jit(solution)/shard_map/while/body/eval_jaxpr/ppermute | solution.py:26
  565.4 36.7 %collective-permute-start = (bf16[2,128,1024]{1,2,0:T(8,128)(2,1)S(1)}, bf16[2,128,1024]{1,2,0:T(8,128)(2,1)}, u32[]{:S(2)}, u32[]{:S(2)}) collective-permute-start(bf16[2,128,1024]{1,2,0:T(8,128)(2,1)S(1)} %copy.141), channel_id=1, source_target_pairs={{28,0},{0,4},{4,8},{8,12},{12,16},{16,20},{20,24},{24,28},{29,1},{... | collective-permute-start | bytes 1572872 | tf_op jit(solution)/shard_map/while/body/eval_jaxpr/ppermute | solution.py:26
  565.9 45.0 %collective-permute-start.1 = (bf16[2,128,1024]{1,2,0:T(8,128)(2,1)S(1)}, bf16[2,128,1024]{1,2,0:T(8,128)(2,1)}, u32[]{:S(2)}, u32[]{:S(2)}) collective-permute-start(bf16[2,128,1024]{1,2,0:T(8,128)(2,1)S(1)} %copy.142), channel_id=1, source_target_pairs={{28,0},{0,4},{4,8},{8,12},{12,16},{16,20},{20,24},{24,28},{29,1},{... | collective-permute-start | bytes 1572872 | tf_op jit(solution)/shard_map/while/body/eval_jaxpr/ppermute | solution.py:26
  616.7 17.9 %collective-permute-start.2 = (bf16[2,128,1024]{1,2,0:T(8,128)(2,1)}, bf16[2,128,1024]{1,2,0:T(8,128)(2,1)}, u32[]{:S(2)}, u32[]{:S(2)}) collective-permute-start(bf16[2,128,1024]{1,2,0:T(8,128)(2,1)} %fusion.156), channel_id=1, source_target_pairs={{28,0},{0,4},{4,8},{8,12},{12,16},{16,20},{20,24},{24,28},{29,1},{... | collective-permute-start | bytes 1572872 | tf_op jit(solution)/shard_map/while/body/eval_jaxpr/ppermute | solution.py:26
  618.0 27.7 %collective-permute-start.3 = (bf16[2,128,1024]{1,2,0:T(8,128)(2,1)}, bf16[2,128,1024]{1,2,0:T(8,128)(2,1)}, u32[]{:S(2)}, u32[]{:S(2)}) collective-permute-start(bf16[2,128,1024]{1,2,0:T(8,128)(2,1)} %fusion.158), channel_id=1, source_target_pairs={{28,0},{0,4},{4,8},{8,12},{12,16},{16,20},{20,24},{24,28},{29,1},{... | collective-permute-start | bytes 1572872 | tf_op jit(solution)/shard_map/while/body/eval_jaxpr/ppermute | solution.py:26
  618.7 38.3 %collective-permute-start = (bf16[2,128,1024]{1,2,0:T(8,128)(2,1)S(1)}, bf16[2,128,1024]{1,2,0:T(8,128)(2,1)}, u32[]{:S(2)}, u32[]{:S(2)}) collective-permute-start(bf16[2,128,1024]{1,2,0:T(8,128)(2,1)S(1)} %copy.141), channel_id=1, source_target_pairs={{28,0},{0,4},{4,8},{8,12},{12,16},{16,20},{20,24},{24,28},{29,1},{... | collective-permute-start | bytes 1572872 | tf_op jit(solution)/shard_map/while/body/eval_jaxpr/ppermute | solution.py:26
  618.7 46.2 %collective-permute-start.1 = (bf16[2,128,1024]{1,2,0:T(8,128)(2,1)S(1)}, bf16[2,128,1024]{1,2,0:T(8,128)(2,1)}, u32[]{:S(2)}, u32[]{:S(2)}) collective-permute-start(bf16[2,128,1024]{1,2,0:T(8,128)(2,1)S(1)} %copy.142), channel_id=1, source_target_pairs={{28,0},{0,4},{4,8},{8,12},{12,16},{16,20},{20,24},{24,28},{29,1},{... | collective-permute-start | bytes 1572872 | tf_op jit(solution)/shard_map/while/body/eval_jaxpr/ppermute | solution.py:26
  670.7 17.9 %collective-permute-start.2 = (bf16[2,128,1024]{1,2,0:T(8,128)(2,1)}, bf16[2,128,1024]{1,2,0:T(8,128)(2,1)}, u32[]{:S(2)}, u32[]{:S(2)}) collective-permute-start(bf16[2,128,1024]{1,2,0:T(8,128)(2,1)} %fusion.156), channel_id=1, source_target_pairs={{28,0},{0,4},{4,8},{8,12},{12,16},{16,20},{20,24},{24,28},{29,1},{... | collective-permute-start | bytes 1572872 | tf_op jit(solution)/shard_map/while/body/eval_jaxpr/ppermute | solution.py:26
  672.1 27.7 %collective-permute-start.3 = (bf16[2,128,1024]{1,2,0:T(8,128)(2,1)}, bf16[2,128,1024]{1,2,0:T(8,128)(2,1)}, u32[]{:S(2)}, u32[]{:S(2)}) collective-permute-start(bf16[2,128,1024]{1,2,0:T(8,128)(2,1)} %fusion.158), channel_id=1, source_target_pairs={{28,0},{0,4},{4,8},{8,12},{12,16},{16,20},{20,24},{24,28},{29,1},{... | collective-permute-start | bytes 1572872 | tf_op jit(solution)/shard_map/while/body/eval_jaxpr/ppermute | solution.py:26
  672.1 39.0 %collective-permute-start = (bf16[2,128,1024]{1,2,0:T(8,128)(2,1)S(1)}, bf16[2,128,1024]{1,2,0:T(8,128)(2,1)}, u32[]{:S(2)}, u32[]{:S(2)}) collective-permute-start(bf16[2,128,1024]{1,2,0:T(8,128)(2,1)S(1)} %copy.141), channel_id=1, source_target_pairs={{28,0},{0,4},{4,8},{8,12},{12,16},{16,20},{20,24},{24,28},{29,1},{... | collective-permute-start | bytes 1572872 | tf_op jit(solution)/shard_map/while/body/eval_jaxpr/ppermute | solution.py:26
  672.1 46.0 %collective-permute-start.1 = (bf16[2,128,1024]{1,2,0:T(8,128)(2,1)S(1)}, bf16[2,128,1024]{1,2,0:T(8,128)(2,1)}, u32[]{:S(2)}, u32[]{:S(2)}) collective-permute-start(bf16[2,128,1024]{1,2,0:T(8,128)(2,1)S(1)} %copy.142), channel_id=1, source_target_pairs={{28,0},{0,4},{4,8},{8,12},{12,16},{16,20},{20,24},{24,28},{29,1},{... | collective-permute-start | bytes 1572872 | tf_op jit(solution)/shard_map/while/body/eval_jaxpr/ppermute | solution.py:26
  723.8 17.9 %collective-permute-start.2 = (bf16[2,128,1024]{1,2,0:T(8,128)(2,1)}, bf16[2,128,1024]{1,2,0:T(8,128)(2,1)}, u32[]{:S(2)}, u32[]{:S(2)}) collective-permute-start(bf16[2,128,1024]{1,2,0:T(8,128)(2,1)} %fusion.156), channel_id=1, source_target_pairs={{28,0},{0,4},{4,8},{8,12},{12,16},{16,20},{20,24},{24,28},{29,1},{... | collective-permute-start | bytes 1572872 | tf_op jit(solution)/shard_map/while/body/eval_jaxpr/ppermute | solution.py:26
  725.2 27.7 %collective-permute-start.3 = (bf16[2,128,1024]{1,2,0:T(8,128)(2,1)}, bf16[2,128,1024]{1,2,0:T(8,128)(2,1)}, u32[]{:S(2)}, u32[]{:S(2)}) collective-permute-start(bf16[2,128,1024]{1,2,0:T(8,128)(2,1)} %fusion.158), channel_id=1, source_target_pairs={{28,0},{0,4},{4,8},{8,12},{12,16},{16,20},{20,24},{24,28},{29,1},{... | collective-permute-start | bytes 1572872 | tf_op jit(solution)/shard_map/while/body/eval_jaxpr/ppermute | solution.py:26
  725.2 39.0 %collective-permute-start = (bf16[2,128,1024]{1,2,0:T(8,128)(2,1)S(1)}, bf16[2,128,1024]{1,2,0:T(8,128)(2,1)}, u32[]{:S(2)}, u32[]{:S(2)}) collective-permute-start(bf16[2,128,1024]{1,2,0:T(8,128)(2,1)S(1)} %copy.141), channel_id=1, source_target_pairs={{28,0},{0,4},{4,8},{8,12},{12,16},{16,20},{20,24},{24,28},{29,1},{... | collective-permute-start | bytes 1572872 | tf_op jit(solution)/shard_map/while/body/eval_jaxpr/ppermute | solution.py:26
  725.2 45.1 %collective-permute-start.1 = (bf16[2,128,1024]{1,2,0:T(8,128)(2,1)S(1)}, bf16[2,128,1024]{1,2,0:T(8,128)(2,1)}, u32[]{:S(2)}, u32[]{:S(2)}) collective-permute-start(bf16[2,128,1024]{1,2,0:T(8,128)(2,1)S(1)} %copy.142), channel_id=1, source_target_pairs={{28,0},{0,4},{4,8},{8,12},{12,16},{16,20},{20,24},{24,28},{29,1},{... | collective-permute-start | bytes 1572872 | tf_op jit(solution)/shard_map/while/body/eval_jaxpr/ppermute | solution.py:26
  776.0 17.9 %collective-permute-start.2 = (bf16[2,128,1024]{1,2,0:T(8,128)(2,1)}, bf16[2,128,1024]{1,2,0:T(8,128)(2,1)}, u32[]{:S(2)}, u32[]{:S(2)}) collective-permute-start(bf16[2,128,1024]{1,2,0:T(8,128)(2,1)} %fusion.156), channel_id=1, source_target_pairs={{28,0},{0,4},{4,8},{8,12},{12,16},{16,20},{20,24},{24,28},{29,1},{... | collective-permute-start | bytes 1572872 | tf_op jit(solution)/shard_map/while/body/eval_jaxpr/ppermute | solution.py:26
  777.3 27.7 %collective-permute-start.3 = (bf16[2,128,1024]{1,2,0:T(8,128)(2,1)}, bf16[2,128,1024]{1,2,0:T(8,128)(2,1)}, u32[]{:S(2)}, u32[]{:S(2)}) collective-permute-start(bf16[2,128,1024]{1,2,0:T(8,128)(2,1)} %fusion.158), channel_id=1, source_target_pairs={{28,0},{0,4},{4,8},{8,12},{12,16},{16,20},{20,24},{24,28},{29,1},{... | collective-permute-start | bytes 1572872 | tf_op jit(solution)/shard_map/while/body/eval_jaxpr/ppermute | solution.py:26
  777.3 38.5 %collective-permute-start = (bf16[2,128,1024]{1,2,0:T(8,128)(2,1)S(1)}, bf16[2,128,1024]{1,2,0:T(8,128)(2,1)}, u32[]{:S(2)}, u32[]{:S(2)}) collective-permute-start(bf16[2,128,1024]{1,2,0:T(8,128)(2,1)S(1)} %copy.141), channel_id=1, source_target_pairs={{28,0},{0,4},{4,8},{8,12},{12,16},{16,20},{20,24},{24,28},{29,1},{... | collective-permute-start | bytes 1572872 | tf_op jit(solution)/shard_map/while/body/eval_jaxpr/ppermute | solution.py:26
  777.3 44.1 %collective-permute-start.1 = (bf16[2,128,1024]{1,2,0:T(8,128)(2,1)S(1)}, bf16[2,128,1024]{1,2,0:T(8,128)(2,1)}, u32[]{:S(2)}, u32[]{:S(2)}) collective-permute-start(bf16[2,128,1024]{1,2,0:T(8,128)(2,1)S(1)} %copy.142), channel_id=1, source_target_pairs={{28,0},{0,4},{4,8},{8,12},{12,16},{16,20},{20,24},{24,28},{29,1},{... | collective-permute-start | bytes 1572872 | tf_op jit(solution)/shard_map/while/body/eval_jaxpr/ppermute | solution.py:26
  827.2 17.9 %collective-permute-start.2 = (bf16[2,128,1024]{1,2,0:T(8,128)(2,1)}, bf16[2,128,1024]{1,2,0:T(8,128)(2,1)}, u32[]{:S(2)}, u32[]{:S(2)}) collective-permute-start(bf16[2,128,1024]{1,2,0:T(8,128)(2,1)} %fusion.156), channel_id=1, source_target_pairs={{28,0},{0,4},{4,8},{8,12},{12,16},{16,20},{20,24},{24,28},{29,1},{... | collective-permute-start | bytes 1572872 | tf_op jit(solution)/shard_map/while/body/eval_jaxpr/ppermute | solution.py:26
  828.6 27.8 %collective-permute-start.3 = (bf16[2,128,1024]{1,2,0:T(8,128)(2,1)}, bf16[2,128,1024]{1,2,0:T(8,128)(2,1)}, u32[]{:S(2)}, u32[]{:S(2)}) collective-permute-start(bf16[2,128,1024]{1,2,0:T(8,128)(2,1)} %fusion.158), channel_id=1, source_target_pairs={{28,0},{0,4},{4,8},{8,12},{12,16},{16,20},{20,24},{24,28},{29,1},{... | collective-permute-start | bytes 1572872 | tf_op jit(solution)/shard_map/while/body/eval_jaxpr/ppermute | solution.py:26
  828.6 37.6 %collective-permute-start = (bf16[2,128,1024]{1,2,0:T(8,128)(2,1)S(1)}, bf16[2,128,1024]{1,2,0:T(8,128)(2,1)}, u32[]{:S(2)}, u32[]{:S(2)}) collective-permute-start(bf16[2,128,1024]{1,2,0:T(8,128)(2,1)S(1)} %copy.141), channel_id=1, source_target_pairs={{28,0},{0,4},{4,8},{8,12},{12,16},{16,20},{20,24},{24,28},{29,1},{... | collective-permute-start | bytes 1572872 | tf_op jit(solution)/shard_map/while/body/eval_jaxpr/ppermute | solution.py:26
  828.6 43.2 %collective-permute-start.1 = (bf16[2,128,1024]{1,2,0:T(8,128)(2,1)S(1)}, bf16[2,128,1024]{1,2,0:T(8,128)(2,1)}, u32[]{:S(2)}, u32[]{:S(2)}) collective-permute-start(bf16[2,128,1024]{1,2,0:T(8,128)(2,1)S(1)} %copy.142), channel_id=1, source_target_pairs={{28,0},{0,4},{4,8},{8,12},{12,16},{16,20},{20,24},{24,28},{29,1},{... | collective-permute-start | bytes 1572872 | tf_op jit(solution)/shard_map/while/body/eval_jaxpr/ppermute | solution.py:26
  878.9 27.7 %collective-permute-start.3 = (bf16[2,128,1024]{1,2,0:T(8,128)(2,1)}, bf16[2,128,1024]{1,2,0:T(8,128)(2,1)}, u32[]{:S(2)}, u32[]{:S(2)}) collective-permute-start(bf16[2,128,1024]{1,2,0:T(8,128)(2,1)} %fusion.158), channel_id=1, source_target_pairs={{28,0},{0,4},{4,8},{8,12},{12,16},{16,20},{20,24},{24,28},{29,1},{... | collective-permute-start | bytes 1572872 | tf_op jit(solution)/shard_map/while/body/eval_jaxpr/ppermute | solution.py:26
  878.9 36.7 %collective-permute-start = (bf16[2,128,1024]{1,2,0:T(8,128)(2,1)S(1)}, bf16[2,128,1024]{1,2,0:T(8,128)(2,1)}, u32[]{:S(2)}, u32[]{:S(2)}) collective-permute-start(bf16[2,128,1024]{1,2,0:T(8,128)(2,1)S(1)} %copy.141), channel_id=1, source_target_pairs={{28,0},{0,4},{4,8},{8,12},{12,16},{16,20},{20,24},{24,28},{29,1},{... | collective-permute-start | bytes 1572872 | tf_op jit(solution)/shard_map/while/body/eval_jaxpr/ppermute | solution.py:26
  878.9 42.3 %collective-permute-start.1 = (bf16[2,128,1024]{1,2,0:T(8,128)(2,1)S(1)}, bf16[2,128,1024]{1,2,0:T(8,128)(2,1)}, u32[]{:S(2)}, u32[]{:S(2)}) collective-permute-start(bf16[2,128,1024]{1,2,0:T(8,128)(2,1)S(1)} %copy.142), channel_id=1, source_target_pairs={{28,0},{0,4},{4,8},{8,12},{12,16},{16,20},{20,24},{24,28},{29,1},{... | collective-permute-start | bytes 1572872 | tf_op jit(solution)/shard_map/while/body/eval_jaxpr/ppermute | solution.py:26
  1164.3 549.2 %all-reduce.7.cloned.1.call-start = ((), (), s32[]{:S(2)}) async-start(), calls=%async_computation.4 | async-start | bytes 18350080 | tf_op jit(solution)/shard_map/psum | solution.py:327
  (86 other events, 1024.8 us)
Sparse Core Ops, SparseCore 0:
  18.6 224.1 all-gather.3
  294.6 73.3 all-gather.7
  370.8 71.6 all-gather.5
  1164.4 252.6 reduce-scatter.3
  1421.3 292.1 all-reduce.6
where the time goes:
time: 1770 us; the launch traced here: 1760 us
  waiting for transfers between devices  1080 us (61%)
  local copies, waits for them, and re-layouts  241 us (14%)
  other arithmetic  236 us (13%)
  matrix products  141 us (8%)
  blocking collectives  32.9 us (2%)
    ppermute x30, waiting for transfers between devices, passed_along(): return lax.ppermute(block, axis, route)  258 us
    psum x1, waiting for transfers between devices, shards(): lax.psum(owned_part.astype(jnp.bfloat16), 'ctx').astype(jnp.float32)  256 us
    unnamed x6, waiting for transfers between devices  253 us
    all_gather x1, waiting for transfers between devices, shards(): gathered = lax.all_gather(master_low, 'shard', axis=0, tiled=True)  217 us
    scatter x1, local copies, waits for them, and re-layouts, shards(): grad_buffer = jnp.zeros((groups * capacity, unit_rows, model_width), jnp....  89.1 us
    all_gather x1, waiting for transfers between devices, shards(): key_piece = lax.all_gather(key_low, 'ctx', axis=1, tiled=True)  48.2 us
    all_gather x1, waiting for transfers between devices, shards(): value_piece = lax.all_gather(value_low, 'ctx', axis=1, tiled=True)  47 us
    sub x2, other arithmetic, adam_update(): weight - step_rate * (adam_step + weight_decay * weight)  42.5 us
  transfers between devices with their start and end apart: 35, of which 35 were waited for; matrix products, arithmetic and copies ran while one was open for 8% of the time, Pallas kernels for 0%

commit v1 on v0

v1 whole, which is shorter than its diff:
```python
import functools

import jax
import jax.numpy as jnp
from jax import lax
from jax.experimental import pallas as pl
from jax.experimental.pallas import tpu as pltpu
from jax.sharding import PartitionSpec as P

HEADS = 16
HEAD_DIM = 64
FF = 2624
STEP = 10
MESH = pl.DeviceIdType.MESH
DMA = pltpu.SemaphoreType.DMA

eps_norm = 1e-05
rope_base = 160000.0
mask_fill = -1e30
beta_one = 0.9
beta_two = 0.98
adam_eps = 1e-06
rate_matrix = 0.03
rate_gain = 0.6
decay_matrix = 0.01
BOTH = ("ctx", "shard")
VMEM_BYTES = 60 * 2**20


def transposed(left, right):
    return lax.dot_general(
        left, right, (((1,), (1,)), ((), ())), preferred_element_type=jnp.float32
    )


def leading(left, right):
    return lax.dot_general(
        left, right, (((0,), (0,)), ((), ())), preferred_element_type=jnp.float32
    )


def layer_norm(values, gain):
    row_mean = jnp.mean(values, axis=-1, keepdims=True)
    centred = values - row_mean
    variance = jnp.mean(centred * centred, axis=-1, keepdims=True)
    return centred * lax.rsqrt(variance + eps_norm) * gain


def rope_tables(positions, heads):
    half_dim = HEAD_DIM // 2
    inverse = rope_base ** (-2.0 * jnp.arange(half_dim, dtype=jnp.float32) / HEAD_DIM)
    angles = positions.astype(jnp.float32)[:, None] * inverse[None, :]
    cosine, sine = jnp.cos(angles), jnp.sin(angles)
    cosine = jnp.concatenate([cosine, cosine] * heads, axis=1)
    sine = jnp.concatenate([-sine, sine] * heads, axis=1)
    return (cosine, sine)


def half_turned(values):
    width = values.shape[-1]
    half = HEAD_DIM // 2
    lane = lax.broadcasted_iota(jnp.int32, values.shape, values.ndim - 1)
    if width == HEAD_DIM:
        return jnp.concatenate([values[:, half:], values[:, :half]], axis=1)
    ahead = pltpu.roll(values, width - half, axis=1)
    behind = pltpu.roll(values, half, axis=1)
    return jnp.where(lane % HEAD_DIM < half, ahead, behind)


def unit_places(unit_owner, capacity, groups):
    owner_marks = (unit_owner[:, None] == jnp.arange(groups, dtype=jnp.int32)[None, :]).astype(
        jnp.int32
    )
    owner_ranks = jnp.cumsum(owner_marks, axis=0) - 1
    return jnp.sum(owner_ranks * owner_marks, axis=1)


def gated_gelu(upper_proj):
    return jax.nn.gelu(upper_proj[:, :FF], approximate=False) * upper_proj[:, FF:]


def adam_update(weight, gradient, first_old, second_old, step_rate, weight_decay):
    first_new = beta_one * first_old + (1.0 - beta_one) * gradient
    second_new = beta_two * second_old + (1.0 - beta_two) * gradient * gradient
    first_fix = 1.0 - beta_one**STEP
    second_fix = 1.0 - beta_two**STEP
    adam_step = first_new / first_fix / (jnp.sqrt(second_new / second_fix) + adam_eps)
    return (weight - step_rate * (adam_step + weight_decay * weight), first_new, second_new)


def qkv_kernel(norm_ref, w_ref, cos_ref, sin_ref, out_ref):
    tile = pl.program_id(0)
    turned_tiles = 2 * pl.num_programs(0) // 3
    values = transposed(norm_ref[...], w_ref[...])

    @pl.when(tile < turned_tiles)
    def _():
        out_ref[...] = (values * cos_ref[...] + half_turned(values) * sin_ref[...]).astype(
            out_ref.dtype
        )

    @pl.when(tile >= turned_tiles)
    def _():
        out_ref[...] = values.astype(out_ref.dtype)


def qkv_call(norm_one, w_qkv, cosine, sine):
    rows, width = norm_one.shape
    cols = 256
    return pl.pallas_call(
        qkv_kernel,
        grid=(3 * width // cols,),
        in_specs=[
            pl.BlockSpec((rows, width), lambda i: (0, 0)),
            pl.BlockSpec((cols, width), lambda i: (i, 0)),
            pl.BlockSpec((rows, cols), lambda i: (0, 0)),
            pl.BlockSpec((rows, cols), lambda i: (0, 0)),
        ],
        out_specs=pl.BlockSpec((rows, cols), lambda i: (0, i)),
        out_shape=jax.ShapeDtypeStruct((rows, 3 * width), jnp.bfloat16),
        name="qkv",
    )(norm_one, w_qkv, cosine, sine)


def head_only(values, head):
    width = values.shape[-1]
    if width == HEAD_DIM:
        return values
    lane = lax.broadcasted_iota(jnp.int32, values.shape, 1)
    return jnp.where(lane // HEAD_DIM == head, values, jnp.zeros_like(values))


def attend_slot(q_ref, k_ref, v_ref, bias, out_ref, wide_ref, lse_ref, chunk):
    seq, width = k_ref.shape
    heads = width // HEAD_DIM
    keys = [head_only(k_ref[...], h) for h in range(heads)]
    values = [head_only(v_ref[...], h) for h in range(heads)]

    def step(i, _):
        rows = pl.ds(pl.multiple_of(i * chunk, chunk), chunk)
        query = q_ref[rows, :] * jnp.bfloat16(0.125)
        total = None
        stats = None
        for h in range(heads):
            scores = transposed(query, keys[h]) + bias
            top = jnp.max(scores, axis=-1, keepdims=True)
            weights = jnp.exp(scores - top)
            norm = jnp.sum(weights, axis=-1, keepdims=True)
            low = (weights * (1.0 / norm)).astype(jnp.bfloat16)
            part = jnp.dot(low, values[h], preferred_element_type=jnp.float32)
            lse = jnp.broadcast_to(top + jnp.log(norm), (chunk, width))
            total = part if total is None else total + part
            if stats is None:
                stats = lse
            else:
                lane = lax.broadcasted_iota(jnp.int32, lse.shape, 1)
                stats = jnp.where(lane // HEAD_DIM == h, lse, stats)
        out_ref[rows, :] = total.astype(jnp.bfloat16)
        wide_ref[rows, :] = total
        lse_ref[rows, :] = stats
        return 0

    lax.fori_loop(0, seq // chunk, step, 0)


def attend_back_slot(
    q_ref, k_ref, v_ref, g_ref, wide_ref, lse_ref, bias, cos, sin, dq_ref, dk_ref, dv_ref, acc_k, acc_v, chunk
):
    seq, width = k_ref.shape
    heads = width // HEAD_DIM
    keys = [head_only(k_ref[...], h) for h in range(heads)]
    values = [head_only(v_ref[...], h) for h in range(heads)]
    acc_k[...] = jnp.zeros_like(acc_k)
    acc_v[...] = jnp.zeros_like(acc_v)

    def turned_back(grad, rows):
        return grad * cos[rows, :] - half_turned(grad) * sin[rows, :]

    def step(i, _):
        rows = pl.ds(pl.multiple_of(i * chunk, chunk), chunk)
        query = q_ref[rows, :]
        grad = g_ref[rows, :]
        lse_all = lse_ref[rows, :]
        both = grad.astype(jnp.float32) * wide_ref[rows, :]
        total = None
        for h in range(heads):
            lse = lse_all[:, h * HEAD_DIM : h * HEAD_DIM + 1]
            delta = jnp.sum(head_only(both, h), axis=-1, keepdims=True)
            scores = transposed(query * jnp.bfloat16(0.125), keys[h])
            weights = jnp.exp(scores + (bias - lse))
            back = transposed(grad, values[h])
            low = (weights * (back - delta)).astype(jnp.bfloat16)
            part = jnp.dot(low, keys[h], preferred_element_type=jnp.float32)
            total = part if total is None else total + part
            acc_v[...] += leading(weights.astype(jnp.bfloat16), head_only(grad, h))
            acc_k[...] += leading(low, head_only(query, h))
        dq_ref[rows, :] = turned_back(total * 0.125, rows).astype(jnp.bfloat16)
        return 0

    lax.fori_loop(0, seq // chunk, step, 0)
    every = slice(None)
    dk_ref[...] = turned_back(acc_k[...] * 0.125, every).astype(jnp.bfloat16)
    dv_ref[...] = acc_v[...].astype(jnp.bfloat16)


def attend_kernel(slots, chunk, qkv_ref, bias_ref, out_ref, wide_ref, lse_ref):
    for s in range(slots):
        attend_slot(
            qkv_ref.at[0, s], qkv_ref.at[1, s], qkv_ref.at[2, s], bias_ref[s],
            out_ref.at[s], wide_ref.at[s], lse_ref.at[s], chunk,
        )


def attend_call(qkv, bias):
    _, slots, seq, width = qkv.shape
    chunk = 256
    return pl.pallas_call(
        functools.partial(attend_kernel, slots, chunk),
        out_shape=(
            jax.ShapeDtypeStruct((slots, seq, width), jnp.bfloat16),
            jax.ShapeDtypeStruct((slots, seq, width), jnp.float32),
            jax.ShapeDtypeStruct((slots, seq, width), jnp.float32),
        ),
        compiler_params=pltpu.CompilerParams(vmem_limit_bytes=VMEM_BYTES),
        name="attend",
    )(qkv, bias)


def attend_back_kernel(slots, chunk, qkv_ref, g_ref, wide_ref, lse_ref, bias_ref, cos_ref, sin_ref, out_ref, acc_k, acc_v):
    for s in range(slots):
        attend_back_slot(
            qkv_ref.at[0, s], qkv_ref.at[1, s], qkv_ref.at[2, s], g_ref.at[s],
            wide_ref.at[s], lse_ref.at[s], bias_ref[s], cos_ref, sin_ref,
            out_ref.at[0, s], out_ref.at[1, s], out_ref.at[2, s], acc_k, acc_v, chunk,
        )


def attend_back_call(qkv, grad_heads, wide, lse, bias, cosine, sine):
    _, slots, seq, width = qkv.shape
    chunk = 256
    return pl.pallas_call(
        functools.partial(attend_back_kernel, slots, chunk),
        out_shape=jax.ShapeDtypeStruct(qkv.shape, jnp.bfloat16),
        scratch_shapes=[pltpu.VMEM((seq, width), jnp.float32)] * 2,
        compiler_params=pltpu.CompilerParams(vmem_limit_bytes=VMEM_BYTES),
        name="attend_back",
    )(qkv, grad_heads, wide, lse, bias, cosine, sine)


def adam_kernel(per, unit_ref, used_ref, *refs):
    grads = refs[:per]
    master, first, second, new_master, new_first, new_second = refs[per:]
    for j in range(per):
        slot = pl.program_id(0) * per + j
        keep = used_ref[slot].astype(jnp.float32)
        grad = grads[j][0].astype(jnp.float32) * keep
        weight, one, two = adam_update(
            master[j], grad, first[j], second[j], rate_matrix, decay_matrix
        )
        new_master[j] = weight
        new_first[j] = one
        new_second[j] = two


def adam_call(unit_of_slot, used, grads, master, first, second):
    capacity, rows, width = master.shape
    per = 2 if capacity % 2 == 0 else 1

    def unit_spec(j):
        return pl.BlockSpec((1, rows, width), lambda i, units, used: (units[i * per + j], 0, 0))

    slot_spec = pl.BlockSpec((per, rows, width), lambda i, units, used: (i, 0, 0))
    return pl.pallas_call(
        functools.partial(adam_kernel, per),
        grid_spec=pltpu.PrefetchScalarGridSpec(
            num_scalar_prefetch=2,
            grid=(capacity // per,),
            in_specs=[unit_spec(j) for j in range(per)] + [slot_spec] * 3,
            out_specs=[slot_spec] * 3,
        ),
        out_shape=[jax.ShapeDtypeStruct(master.shape, jnp.float32)] * 3,
        compiler_params=pltpu.CompilerParams(vmem_limit_bytes=VMEM_BYTES),
        name="adamw",
    )(unit_of_slot, used, *([grads] * per), master, first, second)


def place():
    ctx, shard = lax.axis_index("ctx"), lax.axis_index("shard")
    return ctx // 2, ctx % 2, shard // 2, shard % 2


def device_at(z, y, x, core):
    return (z * 2 + y, x * 2 + core)


def block_at(z, y, x, core):
    return (z * 2 + y) * 4 + x * 2 + core


def remote(src, dst, send, recv, device):
    return pltpu.make_async_remote_copy(
        src_ref=src, dst_ref=dst, send_sem=send, recv_sem=recv, device_id=device, device_id_type=MESH
    )


def greet(devices):
    barrier = pltpu.get_barrier_semaphore()
    for device in devices:
        pl.semaphore_signal(barrier, inc=1, device_id=device, device_id_type=MESH)
    pl.semaphore_wait(barrier, len(devices))


def gather_kernel(units, x_ref, out_ref, lsem, zs, zr, as_, ar, bs, br, a2s, a2r, b2s, b2r, ss, sr, sas, sar, sbs, sbr, sa2s, sa2r, sb2s, sb2r):
    nz = 4
    z, y, x, core = place()
    half = units // 2
    me = block_at(z, y, x, core)
    xn = device_at(z, y, 1 - x, core)
    yn = device_at(z, 1 - y, x, core)
    sib = device_at(z, y, x, 1 - core)
    greet([xn, yn, sib] + [device_at((z + d) % nz, y, x, core) for d in (1, 2, 3)])
    own = pltpu.make_async_copy(x_ref, out_ref.at[me], lsem)
    own.start()

    def part(i, p):
        return out_ref.at[i].at[pl.ds(p * half, half)]

    def moved(ref, send, recv, device):
        return remote(ref, ref, send, recv, device)

    def z_copy(d):
        return remote(x_ref, out_ref.at[me], zs.at[d - 1], zr.at[d - 1], device_at((z + d) % nz, y, x, core))

    def z_got(zb, d):
        ref = out_ref.at[block_at(zb, y, x, core)]
        return moved(ref, zs.at[nz - d - 1], zr.at[nz - d - 1], xn)

    def a_copy(zb, xb):
        return moved(part(block_at(zb, y, xb, core), 0), as_.at[zb], ar.at[zb], xn)

    def b_copy(zb, yb):
        return moved(part(block_at(zb, yb, x, core), 1), bs.at[zb], br.at[zb], yn)

    def a2_copy(zb, yb, xb):
        j = zb * 2 + xb
        return moved(part(block_at(zb, yb, xb, core), 0), a2s.at[j], a2r.at[j], yn)

    def b2_copy(zb, yb, xb):
        j = zb * 2 + yb
        return moved(part(block_at(zb, yb, xb, core), 1), b2s.at[j], b2r.at[j], xn)

    def s_copy(zb, c):
        return moved(out_ref.at[block_at(zb, y, x, c)], ss.at[zb], sr.at[zb], sib)

    def sa_copy(zb, c):
        return moved(part(block_at(zb, y, 1 - x, c), 0), sas.at[zb], sar.at[zb], sib)

    def sb_copy(zb, c):
        return moved(part(block_at(zb, 1 - y, x, c), 1), sbs.at[zb], sbr.at[zb], sib)

    def sa2_copy(zb, xb, c):
        j = zb * 2 + xb
        return moved(part(block_at(zb, 1 - y, xb, c), 0), sa2s.at[j], sa2r.at[j], sib)

    def sb2_copy(zb, yb, c):
        j = zb * 2 + yb
        return moved(part(block_at(zb, yb, 1 - x, c), 1), sb2s.at[j], sb2r.at[j], sib)

    def first(zb):
        a_copy(zb, x).start()
        b_copy(zb, y).start()
        a2_copy(zb, y, x).start()
        b2_copy(zb, y, x).start()
        s_copy(zb, core).start()

    def second(zb):
        a_copy(zb, 1 - x).wait_recv()
        a2_copy(zb, y, 1 - x).start()
        sa_copy(zb, core).start()
        b_copy(zb, 1 - y).wait_recv()
        b2_copy(zb, 1 - y, x).start()
        sb_copy(zb, core).start()

    for d in (1, 3, 2):
        z_copy(d).start()
    own.wait()
    order = [z, (z + 1) % nz, (z + 3) % nz, (z + 2) % nz]
    first(z)
    for n, d in enumerate((1, 3, 2)):
        zb = (z + d) % nz
        z_got(zb, d).wait_recv()
        first(zb)
        second(order[n])
    second(order[3])
    for zb in order:
        for xb in (x, 1 - x):
            a2_copy(zb, 1 - y, xb).wait_recv()
            sa2_copy(zb, xb, core).start()
        for yb in (y, 1 - y):
            b2_copy(zb, yb, 1 - x).wait_recv()
            sb2_copy(zb, yb, core).start()
    for d in (1, 2, 3):
        z_copy(d).wait_send()
    for zb in range(nz):
        a_copy(zb, x).wait_send()
        b_copy(zb, y).wait_send()
        s_copy(zb, core).wait_send()
        s_copy(zb, 1 - core).wait_recv()
        sa_copy(zb, core).wait_send()
        sa_copy(zb, 1 - core).wait_recv()
        sb_copy(zb, core).wait_send()
        sb_copy(zb, 1 - core).wait_recv()
        for q in range(2):
            a2_copy(zb, y, q).wait_send()
            b2_copy(zb, q, x).wait_send()
            sa2_copy(zb, q, core).wait_send()
            sa2_copy(zb, q, 1 - core).wait_recv()
            sb2_copy(zb, q, core).wait_send()
            sb2_copy(zb, q, 1 - core).wait_recv()


def gather_call(block, collective_id):
    units = block.shape[0]
    sems = [DMA] + [DMA((3,))] * 2 + [DMA((4,))] * 4 + [DMA((8,))] * 4 + [DMA((4,))] * 6 + [DMA((8,))] * 4
    out = pl.pallas_call(
        functools.partial(gather_kernel, units),
        out_shape=jax.ShapeDtypeStruct((32,) + block.shape, block.dtype),
        in_specs=[pl.BlockSpec(memory_space=pl.ANY)],
        out_specs=pl.BlockSpec(memory_space=pl.ANY),
        scratch_shapes=sems,
        compiler_params=pltpu.CompilerParams(collective_id=collective_id, has_side_effects=True),
        name="gather_units",
    )(block)
    return out.reshape((-1,) + block.shape[1:])


def swap_kernel(parts, n, x_ref, out_ref, lsem, send, recv):
    ctx, shard = lax.axis_index("ctx"), lax.axis_index("shard")
    rows, width = x_ref.shape[2], out_ref.shape[3]
    greet([(lax.rem(ctx + d, n), shard) for d in range(1, n)])

    def src(to):
        return x_ref.at[:, :, :, pl.ds(pl.multiple_of(to * width, width), width)]

    def dst(owner):
        return out_ref.at[:, :, pl.ds(pl.multiple_of(owner * rows, rows), rows), :]

    def copy(d):
        to = lax.rem(ctx + d, n)
        return remote(src(to), dst(ctx), send.at[d], recv.at[d], (to, shard))

    own = pltpu.make_async_copy(src(ctx), dst(ctx), lsem)
    own.start()
    for d in range(1, n):
        copy(d).start()
    own.wait()
    for d in range(1, n):
        copy(d).wait()


def swap_back_kernel(parts, n, x_ref, out_ref, lsem, send, recv):
    ctx, shard = lax.axis_index("ctx"), lax.axis_index("shard")
    rows, width = out_ref.shape[2], x_ref.shape[3]
    greet([(lax.rem(ctx + d, n), shard) for d in range(1, n)])

    def src(to):
        return x_ref.at[:, :, pl.ds(pl.multiple_of(to * rows, rows), rows), :]

    def dst(owner):
        return out_ref.at[:, :, :, pl.ds(pl.multiple_of(owner * width, width), width)]

    def copy(d):
        to = lax.rem(ctx + d, n)
        return remote(src(to), dst(ctx), send.at[d], recv.at[d], (to, shard))

    own = pltpu.make_async_copy(src(ctx), dst(ctx), lsem)
    own.start()
    for d in range(1, n):
        copy(d).start()
    own.wait()
    for d in range(1, n):
        copy(d).wait()


def swap_call(values, n, back, collective_id, name):
    parts, slots, rows, cols = values.shape
    shape = (parts, slots, rows // n, cols * n) if back else (parts, slots, rows * n, cols // n)
    vmem = pl.BlockSpec(memory_space=pltpu.VMEM)
    return pl.pallas_call(
        functools.partial(swap_back_kernel if back else swap_kernel, parts, n),
        out_shape=jax.ShapeDtypeStruct(shape, values.dtype),
        in_specs=[vmem],
        out_specs=vmem,
        scratch_shapes=[DMA, DMA((n,)), DMA((n,))],
        compiler_params=pltpu.CompilerParams(
            collective_id=collective_id, has_side_effects=True, vmem_limit_bytes=VMEM_BYTES
        ),
        name=name,
    )(values)


def to_heads(values, n, fast, collective_id, name):
    if fast:
        return swap_call(values, n, False, collective_id, name)
    return lax.all_to_all(values, "ctx", split_axis=3, concat_axis=2, tiled=True)


def to_rows(values, n, fast, collective_id, name):
    if fast:
        return swap_call(values, n, True, collective_id, name)
    return lax.all_to_all(values, "ctx", split_axis=2, concat_axis=3, tiled=True)


def shards(
    fast,
    tokens,
    cotangent,
    lengths,
    unit_owner,
    master,
    first_moment,
    second_moment,
    norm_gains,
    gain_first,
    gain_second,
):
    slots, block_len, width = tokens.shape
    groups = lax.axis_size("shard")
    n = lax.axis_size("ctx")
    ctx, shard = lax.axis_index("ctx"), lax.axis_index("shard")
    capacity, unit_rows, _ = master.shape
    units = unit_owner.shape[0]
    rows_all = slots * block_len
    seq = block_len * n
    device_count = n * groups
    my_width = width // n

    per = -(-units // device_count)
    padded = per * device_count
    rank = unit_places(unit_owner, capacity, groups)
    piece = ctx * groups * per + jnp.arange(groups * per, dtype=jnp.int32)
    piece_units = jnp.minimum(piece, units - 1)
    owners = unit_owner[piece_units]
    mine = (owners == shard) & (piece < units)
    given = jnp.where(
        mine[:, None, None], jnp.take(master, rank[piece_units], axis=0, mode="clip"), 0.0
    ).astype(jnp.bfloat16)
    own_units = lax.psum_scatter(given, "shard", scatter_dimension=0, tiled=True)
    if fast:
        stack = gather_call(own_units, 0)
    else:
        stack = lax.all_gather(own_units, BOTH, axis=0, tiled=True)
    stacked = stack.reshape(padded * unit_rows, width)
    w_out = stacked[3 * width : 4 * width]
    w_up = stacked[4 * width : 4 * width + 2 * FF]
    w_down = stacked[4 * width + 2 * FF : 4 * width + 3 * FF]

    positions = ctx * block_len + jnp.arange(block_len, dtype=jnp.int32)
    tile_heads = 256 // HEAD_DIM
    cos_rows, sin_rows = rope_tables(jnp.tile(positions, slots), tile_heads)
    cos_seq, sin_seq = rope_tables(jnp.arange(seq, dtype=jnp.int32), my_width // HEAD_DIM)
    live_rows = (positions[None, :] < lengths[:, None]).astype(jnp.float32)
    bias = jnp.where(
        jnp.arange(seq, dtype=jnp.int32)[None, :] < lengths[:, None], 0.0, mask_fill
    ).astype(jnp.float32)[:, None, :]

    inputs = tokens.astype(jnp.float32).reshape(rows_all, width)
    norm_one = layer_norm(inputs, norm_gains[0]).astype(jnp.bfloat16)
    qkv = qkv_call(norm_one, stacked, cos_rows, sin_rows)
    qkv_rows = jnp.transpose(qkv.reshape(slots, block_len, 3, width), (2, 0, 1, 3))
    qkv_heads = to_heads(qkv_rows, n, fast, 1, "swap_qkv")
    mixed_heads, wide, lse = attend_call(qkv_heads, bias)
    mixed_low = to_rows(mixed_heads[None], n, fast, 2, "swap_mixed").reshape(rows_all, width)

    middle = inputs + transposed(mixed_low, w_out)
    norm_two = layer_norm(middle, norm_gains[1]).astype(jnp.bfloat16)
    upper_proj = transposed(norm_two, w_up)
    hidden_low = gated_gelu(upper_proj).astype(jnp.bfloat16)
    result = middle + jnp.dot(hidden_low, w_down, preferred_element_type=jnp.float32)
    output = result.astype(jnp.bfloat16).reshape(slots, block_len, width)

    grad_result = cotangent.astype(jnp.float32).reshape(rows_all, width) * live_rows.reshape(
        rows_all, 1
    )
    grad_down_low = grad_result.astype(jnp.bfloat16)
    grad_w_down = leading(hidden_low, grad_down_low)
    grad_hidden = transposed(grad_down_low, w_down)
    gelu_value, gelu_back = jax.vjp(gated_gelu, upper_proj)
    grad_upper_low = gelu_back(grad_hidden)[0].astype(jnp.bfloat16)
    grad_w_up = leading(grad_upper_low, norm_two)
    grad_norm_two = jnp.dot(grad_upper_low, w_up, preferred_element_type=jnp.float32)
    norm_value, norm_back_two = jax.vjp(layer_norm, middle, norm_gains[1])
    grad_middle_part, grad_gain_two = norm_back_two(grad_norm_two)
    grad_middle = grad_result + grad_middle_part
    grad_attn_low = grad_middle.astype(jnp.bfloat16)
    grad_w_out = leading(grad_attn_low, mixed_low)
    grad_heads_rows = jnp.dot(grad_attn_low, w_out, preferred_element_type=jnp.float32).astype(
        jnp.bfloat16
    )
    grad_heads = to_heads(
        grad_heads_rows.reshape(1, slots, block_len, width), n, fast, 3, "swap_grad"
    )[0]
    grad_qkv_heads = attend_back_call(qkv_heads, grad_heads, wide, lse, bias, cos_seq, sin_seq)
    grad_qkv_rows = to_rows(grad_qkv_heads, n, fast, 4, "swap_grad_qkv")
    grad_qkv_low = jnp.transpose(grad_qkv_rows, (1, 2, 0, 3)).reshape(rows_all, 3 * width)

    grad_w_qkv = leading(grad_qkv_low, norm_one)
    grad_norm_one = jnp.dot(
        grad_qkv_low, stacked[: 3 * width], preferred_element_type=jnp.float32
    )
    first_value, norm_back_one = jax.vjp(layer_norm, inputs, norm_gains[0])
    grad_input_part, grad_gain_one = norm_back_one(grad_norm_one)
    token_grad = (
        (grad_middle + grad_input_part).astype(jnp.bfloat16).reshape(slots, block_len, width)
    )

    unit_grads = jnp.concatenate(
        [
            grad_w_qkv.astype(jnp.bfloat16),
            grad_w_out.astype(jnp.bfloat16),
            grad_w_up.astype(jnp.bfloat16),
            grad_w_down.astype(jnp.bfloat16),
            jnp.zeros(((padded - units) * unit_rows, width), jnp.bfloat16),
        ],
        axis=0,
    ).reshape(padded, unit_rows, width)
    own_grads = lax.psum_scatter(unit_grads, BOTH, scatter_dimension=0, tiled=True)
    if fast:
        all_grads = gather_call(own_grads, 0)
    else:
        all_grads = lax.all_gather(own_grads, BOTH, axis=0, tiled=True)
    gain_grad = lax.psum(jnp.stack([grad_gain_one, grad_gain_two]), BOTH)

    slot_index = jnp.where(unit_owner == shard, rank, capacity)
    unit_of_slot = (
        jnp.zeros((capacity + 1,), jnp.int32)
        .at[slot_index]
        .set(jnp.arange(units, dtype=jnp.int32))[:capacity]
    )
    used = (jnp.arange(capacity) < jnp.sum(unit_owner == shard)).astype(jnp.int32)
    new_master, new_first, new_second = adam_call(
        unit_of_slot, used, all_grads, master, first_moment, second_moment
    )
    new_gains, new_gain_first, new_gain_second = adam_update(
        norm_gains, gain_grad, gain_first, gain_second, rate_gain, 0.0
    )
    return (
        output,
        token_grad,
        new_master,
        new_first,
        new_second,
        new_gains,
        new_gain_first,
        new_gain_second,
    )


def solution(mesh):
    fast = dict(mesh.shape) == {"ctx": 8, "shard": 4}
    return jax.shard_map(
        functools.partial(shards, fast),
        mesh=mesh,
        in_specs=(
            P("shard", "ctx", None),
            P("shard", "ctx", None),
            P("shard"),
            P(),
            P("shard", None, None),
            P("shard", None, None),
            P("shard", None, None),
            P(),
            P(),
            P(),
        ),
        out_specs=(
            P("shard", "ctx", None),
            P("shard", "ctx", None),
            P("shard", None, None),
            P("shard", None, None),
            P("shard", None, None),
            P(),
            P(),
            P(),
        ),
        check_vma=False,
    )
```

time: 1770 us -> 869 us (0.49)
  waiting for transfers between devices: 1080 us -> 214 us
  Pallas kernels: 0 us -> 471 us
  other arithmetic: 236 us -> 24.9 us
  local copies, waits for them, and re-layouts: 241 us -> 31.2 us
  matrix products: 141 us -> 55.7 us
    pallas_call x0 -> x10, Pallas kernels: none -> 471 us  [the longest x2 270 us: gather_call(): pl.pallas_call(functools.partial(gather_kernel, units), out_shape=jax.Sha...]
    all_gather x3 -> x0, waiting for transfers between devices: 313 us -> none  [the longest x1 217 us: shards(): gathered = lax.all_gather(master_low, 'shard', axis=0, tiled=True)]
    ppermute x30 -> x0, waiting for transfers between devices: 258 us -> none  [passed_along(): return lax.ppermute(block, axis, route)]
    psum x1 -> x0, waiting for transfers between devices: 256 us -> none  [shards(): lax.psum(owned_part.astype(jnp.bfloat16), 'ctx').astype(jnp.float32)]
    unnamed x6 -> x2, waiting for transfers between devices: 253 us -> 0.03 us
    reduce_scatter x0 -> x2, waiting for transfers between devices: none -> 214 us  [the longest x1 184 us: shards(): lax.psum_scatter(unit_grads, BOTH, scatter_dimension=0, tiled=True)]
    convert_element_type x34 -> x4, other arithmetic: 94.9 us -> 6.73 us  [the longest x1 2.91 us: shards(): given = jnp.where(mine[:, None, None], jnp.take(master, rank[piece_units]...]
    scatter x1, local copies, waits for them, and re-layouts: 89.1 us -> 1.75 us  [shards(): unit_of_slot = jnp.zeros((capacity + 1,), jnp.int32).at[slot_index].set(j...]
  transfers between devices with their start and end apart: 35 -> 2, of which waited for: 35 -> 2; matrix products, arithmetic and copies ran while one was open for 8% -> 4% of each run, Pallas kernels for 0% -> 0%
where the time goes in v1:
time: 869 us; the launch traced here: 861 us
  Pallas kernels  471 us (54%)
  waiting for transfers between devices  214 us (25%)
  matrix products  55.7 us (6%)
  blocking collectives  49.6 us (6%)
  local copies, waits for them, and re-layouts  31.2 us (4%)
  other arithmetic  24.9 us (3%)
  between operations  14.9 us (2%)
    pallas_call x2, Pallas kernels, gather_call(): pl.pallas_call(functools.partial(gather_kernel, units), out_shape=jax.Sha...  270 us
    reduce_scatter x1, waiting for transfers between devices, shards(): lax.psum_scatter(unit_grads, BOTH, scatter_dimension=0, tiled=True)  184 us
    pallas_call x4, Pallas kernels, swap_call(): pl.pallas_call(functools.partial(swap_back_kernel if back else swap_kerne...  102 us
    pallas_call x1, Pallas kernels, adam_call(): pl.pallas_call(functools.partial(adam_kernel, per), grid_spec=pltpu.Prefe...  55 us
    psum x1, blocking collectives, shards(): gain_grad = lax.psum(jnp.stack([grad_gain_one, grad_gain_two]), BOTH)  49.6 us
    reduce_scatter x1, waiting for transfers between devices, shards(): lax.psum_scatter(given, 'shard', scatter_dimension=0, tiled=True)  30.1 us
    dot_general x4, matrix products, leading(): lax.dot_general(left, right, (((0,), (0,)), ((), ())), preferred_element_...  19.6 us
    pallas_call x1, Pallas kernels, attend_back_call(): pl.pallas_call(functools.partial(attend_back_kernel, slots, chunk), out_s...  19.2 us
  transfers between devices with their start and end apart: 2, of which 2 were waited for; matrix products, arithmetic and copies ran while one was open for 4% of the time, Pallas kernels for 0%

profile of v1, /device:TPU:0, one launch (start us, length us, event | category | flops | bytes accessed | tf_op | source)
XLA Modules:
  0.0 861.3 jit_solution(6682510898450259773)
XLA Ops:
  12.4 7.5 gather_fusion.2
  19.9 2.9 select_convert_fusion
  25.6 1.9 fusion.42
  33.6 30.1 %reduce-scatter.3.cloned.1.call-done.x_ref = bf16[6,64,1024]{2,1,0:T(8,128)(2,1)} async-done(((bf16[24,64,1024]{2,1,0:T(8,128)(2,1)}), bf16[6,64,1024]{2,1,0:T(8,128)(2,1)}) %reduce-scatter.3.cloned.1.call-update) | async-done | bytes 786448 | tf_op jit(solution)/shard_map/reduce_scatter | solution.py:548
  63.7 135.4 %gather_units.2 = bf16[32,6,64,1024]{3,2,1,0:T(8,128)(2,1)} custom-call(bf16[6,64,1024]{2,1,0:T(8,128)(2,1)} %reduce-scatter.3.cloned.1.call-done.x_ref), custom_call_target="tpu_custom_call" | custom-call | tf_op jit(solution)/shard_map/gather_units/pallas_call | solution.py:425
  199.1 11.5 %qkv.1 = bf16[256,3072]{1,0:T(8,128)(2,1)} custom-call(bf16[256,1024]{1,0:T(8,128)(2,1)} %multiply_convert_fusion.3.norm_ref, bf16[12288,1024]{1,0:T(8,128)(2,1)} %bitcast.87, f32[256,256]{1,0:T(8,128)} %concatenate.15.cos_ref, f32[256,256]{1,0:T(8,128)} %concatenate.16.sin_ref), custom_call_target="tpu_custom_call" | custom-call | tf_op jit(solution)/shard_map/qkv/pallas_call | solution.py:110
  210.6 4.6 reshape.303
  216.9 30.1 %swap_qkv.1.qkv_ref = bf16[3,2,1024,128]{3,2,1,0:T(8,128)(2,1)} custom-call(bf16[3,2,128,1024]{3,2,1,0:T(8,128)(2,1)} %bitcast.96), custom_call_target="tpu_custom_call" | custom-call | tf_op jit(solution)/shard_map/swap_qkv/pallas_call | solution.py:489
  247.1 13.8 %attend.1 = (bf16[2,1024,128]{2,1,0:T(8,128)(2,1)}, f32[2,1024,128]{2,1,0:T(8,128)}, f32[2,1024,128]{2,1,0:T(8,128)}) custom-call(bf16[3,2,1024,128]{3,2,1,0:T(8,128)(2,1)} %swap_qkv.1.qkv_ref, f32[2,1,1024]{2,1,0:T(1,128)} %compare_select_fusion.bias_ref), custom_call_target="tpu_custom_call" | custom-call | tf_op jit(solution)/shard_map/attend/pallas_call | solution.py:217
  260.9 23.5 %swap_mixed.1 = bf16[1,2,128,1024]{3,2,1,0:T(8,128)(2,1)} custom-call(bf16[1,2,1024,128]{3,2,1,0:T(8,128)(2,1)} %bitcast.105), custom_call_target="tpu_custom_call" | custom-call | tf_op jit(solution)/shard_map/swap_mixed/pallas_call | solution.py:489
  284.4 2.6 fusion.62
  287.2 6.2 fusion.3
  293.5 9.1 %fusion.40 = (f32[256,2624]{1,0:T(8,128)S(1)}, f32[256,2624]{1,0:T(8,128)S(1)}, f32[256,2624]{1,0:T(8,128)S(1)}) fusion(f32[256,5248]{1,0:T(8,128)S(1)} %fusion.3, bf16[256,1024]{1,0:T(8,128)(2,1)S(1)} %copy-done.10, bf16[12288,1024]{1,0:T(8,128)(2,1)} %bitcast.90), kind=kOutput, calls=%fused_computation.70 | convolution fusion | flops 1419395072 | bytes 16646144 | tf_op jit(solution)/shard_map/dot_general | solution.py:31
  302.6 2.8 multiply_add_fusion
  305.4 7.1 multiply_reduce_fusion
  314.1 3.1 fusion.35
  317.1 15.7 %swap_grad.1 = bf16[1,2,1024,128]{3,2,1,0:T(8,128)(2,1)} custom-call(bf16[1,2,128,1024]{3,2,1,0:T(8,128)(2,1)} %bitcast.106), custom_call_target="tpu_custom_call" | custom-call | tf_op jit(solution)/shard_map/swap_grad/pallas_call | solution.py:489
  332.8 19.2 %attend_back.1.x_ref = bf16[3,2,1024,128]{3,2,1,0:T(8,128)(2,1)} custom-call(bf16[3,2,1024,128]{3,2,1,0:T(8,128)(2,1)} %swap_qkv.1.qkv_ref, bf16[2,1024,128]{2,1,0:T(8,128)(2,1)} %bitcast.98, f32[2,1024,128]{2,1,0:T(8,128)} %get-tuple-element.15.wide_ref, f32[2,1024,128]{2,1,0:T(8,128)} %get-tuple-element.16.lse_ref, ...), custom_call_target="tpu_custom_call" | custom-call | tf_op jit(solution)/shard_map/attend_back/pallas_call | solution.py:241
  352.0 32.8 %swap_grad_qkv.1 = bf16[3,2,128,1024]{3,2,1,0:T(8,128)(2,1)} custom-call(bf16[3,2,1024,128]{3,2,1,0:T(8,128)(2,1)} %attend_back.1.x_ref), custom_call_target="tpu_custom_call" | custom-call | tf_op jit(solution)/shard_map/swap_grad_qkv/pallas_call | solution.py:489
  384.9 5.1 copy.37
  390.1 6.2 convert_dynamic-update-slice_fusion
  396.3 2.1 convert_dynamic-update-slice_fusion.1
  398.4 7.4 fusion
  405.8 4.0 fusion.5
  414.9 3.6 slice.53
  418.6 2.8 multiply_reduce_fusion.2
  423.2 49.6 %psum.7 = f32[2,1024]{1,0:T(2,128)S(1)} all-reduce(f32[2,1024]{1,0:T(2,128)S(1)} %pad_maximum_fusion.2), channel_id=1, replica_groups=mesh['ctx'=8,'shard'=4] {'ctx','shard'}, use_global_device_ids=true, to_apply=%region_17.18 | all-reduce | flops 2048 | bytes 16384 | tf_op jit(solution)/shard_map/psum | solution.py:632
  473.4 2.6 add_convert_fusion.1
  476.0 5.1 fusion.32
  481.1 183.5 %reduce-scatter.5.cloned.1.call-done.x_ref = bf16[6,64,1024]{2,1,0:T(8,128)(2,1)} async-done(((bf16[192,64,1024]{2,1,0:T(8,128)(2,1)}), bf16[6,64,1024]{2,1,0:T(8,128)(2,1)}) %reduce-scatter.5.cloned.1.call-update) | async-done | bytes 786448 | tf_op jit(solution)/shard_map/reduce_scatter | solution.py:627
  664.7 134.2 %gather_units.3 = bf16[32,6,64,1024]{3,2,1,0:T(8,128)(2,1)} custom-call(bf16[6,64,1024]{2,1,0:T(8,128)(2,1)} %reduce-scatter.5.cloned.1.call-done.x_ref), custom_call_target="tpu_custom_call" | custom-call | tf_op jit(solution)/shard_map/gather_units/pallas_call | solution.py:425
  798.9 55.0 %adamw.1 = (f32[70,64,1024]{2,1,0:T(8,128)}, f32[70,64,1024]{2,1,0:T(8,128)}, f32[70,64,1024]{2,1,0:T(8,128)}) custom-call(s32[70]{0:T(128)} %bitcast.120, s32[70]{0:T(128)} %compare_convert_fusion.used_ref, bf16[192,64,1024]{2,1,0:T(8,128)(2,1)} %bitcast.85, bf16[192,64,1024]{2,1,0:T(8,128)(2,1)} %bitcast.86, f32[70,64,1024]{2,1,0:T(8,128)} %refs_2_.1, ...), custom_call_target="tpu_custom_call" | custom-call | tf_op jit(solution)/shard_map/adamw/pallas_call | solution.py:273
  (97 shorter events, 25.2 us)
Async XLA Ops:
  7.2 56.5 %reduce-scatter.3.cloned.1.call-start = ((), (), s32[]{:S(2)}) async-start(), calls=%async_computation.2 | async-start | bytes 3932160 | tf_op jit(solution)/shard_map/reduce_scatter | solution.py:548
  22.8 2.6 copy-start.1
  22.9 641.8 %reduce-scatter.5.cloned.1.call-start = ((), (), s32[]{:S(2)}) async-start(), calls=%async_computation.3 | async-start | bytes 25952256 | tf_op jit(solution)/shard_map/reduce_scatter | solution.py:627
  25.4 4.3 copy-start.16
  25.4 5.0 copy-start.13
  25.4 5.0 copy-start.2
  287.2 6.3 copy-start.10
  302.6 2.8 copy-start.17
  305.4 7.2 copy-start.3
  313.2 0.8 copy-start.8
  390.0 6.2 copy-start.9
  390.1 6.2 copy-start.12
  390.1 8.3 copy-start.18
  396.3 2.1 copy-start.4
  398.4 7.4 copy-start.6
  398.4 7.4 copy-start.11
  410.7 0.7 copy-start
  414.9 3.6 copy-start.5
  418.6 54.2 %copy-start.14 = (f32[2,1024]{1,0:T(2,128)S(1)}, f32[2,1024]{1,0:T(2,128)}, u32[]{:S(2)}) copy-start(f32[2,1024]{1,0:T(2,128)} %param.18) | copy-start | bytes 24580
  418.6 54.2 %copy-start.15 = (f32[2,1024]{1,0:T(2,128)S(1)}, f32[2,1024]{1,0:T(2,128)}, u32[]{:S(2)}) copy-start(f32[2,1024]{1,0:T(2,128)} %param.19) | copy-start | bytes 24580
  472.8 3.2 copy-start.7
Sparse Core Ops, SparseCore 0:
  23.0 40.6 reduce-scatter.2
  410.8 253.8 reduce-scatter.4

commit v2 on v1

--- a/solution.py
+++ b/solution.py
@@ -95,18 +95,19 @@
 
     @pl.when(tile < turned_tiles)
     def _():
-        out_ref[...] = (values * cos_ref[...] + half_turned(values) * sin_ref[...]).astype(
+        out_ref[0] = (values * cos_ref[...] + half_turned(values) * sin_ref[...]).astype(
             out_ref.dtype
         )
 
     @pl.when(tile >= turned_tiles)
     def _():
-        out_ref[...] = values.astype(out_ref.dtype)
+        out_ref[0] = values.astype(out_ref.dtype)
 
 
 def qkv_call(norm_one, w_qkv, cosine, sine):
     rows, width = norm_one.shape
     cols = 256
+    tiles = width // cols
     return pl.pallas_call(
         qkv_kernel,
         grid=(3 * width // cols,),
@@ -116,8 +117,8 @@
             pl.BlockSpec((rows, cols), lambda i: (0, 0)),
             pl.BlockSpec((rows, cols), lambda i: (0, 0)),
         ],
-        out_specs=pl.BlockSpec((rows, cols), lambda i: (0, i)),
-        out_shape=jax.ShapeDtypeStruct((rows, 3 * width), jnp.bfloat16),
+        out_specs=pl.BlockSpec((1, rows, cols), lambda i: (i // tiles, 0, i % tiles)),
+        out_shape=jax.ShapeDtypeStruct((3, rows, width), jnp.bfloat16),
         name="qkv",
     )(norm_one, w_qkv, cosine, sine)
 
@@ -247,13 +248,14 @@
     )(qkv, grad_heads, wide, lse, bias, cosine, sine)
 
 
-def adam_kernel(per, unit_ref, used_ref, *refs):
-    grads = refs[:per]
-    master, first, second, new_master, new_first, new_second = refs[per:]
+def adam_kernel(per, unit_ref, a_ref, b_ref, *refs):
+    grads = (refs[:per], refs[per : 2 * per])
+    master, first, second, new_master, new_first, new_second = refs[2 * per :]
     for j in range(per):
         slot = pl.program_id(0) * per + j
-        keep = used_ref[slot].astype(jnp.float32)
-        grad = grads[j][0].astype(jnp.float32) * keep
+        unit = unit_ref[slot]
+        grad = jnp.where(unit == 0, grads[0][j][0], grads[1][j][0]).astype(jnp.float32)
+        grad = jnp.where(unit >= 0, grad, 0.0)
         weight, one, two = adam_update(
             master[j], grad, first[j], second[j], rate_matrix, decay_matrix
         )
@@ -262,26 +264,28 @@
         new_second[j] = two
 
 
-def adam_call(unit_of_slot, used, grads, master, first, second):
+def adam_call(kind, at_a, at_b, grads_a, grads_b, master, first, second):
     capacity, rows, width = master.shape
-    per = 2 if capacity % 2 == 0 else 1
-
-    def unit_spec(j):
-        return pl.BlockSpec((1, rows, width), lambda i, units, used: (units[i * per + j], 0, 0))
-
-    slot_spec = pl.BlockSpec((per, rows, width), lambda i, units, used: (i, 0, 0))
+    per = max(p for p in range(1, 8) if capacity % p == 0)
+
+    def unit_spec(j, chunk):
+        return pl.BlockSpec(
+            (1, rows, width), lambda i, kind, *at: (at[chunk][i * per + j], 0, 0)
+        )
+
+    slot_spec = pl.BlockSpec((per, rows, width), lambda i, kind, *at: (i, 0, 0))
     return pl.pallas_call(
         functools.partial(adam_kernel, per),
         grid_spec=pltpu.PrefetchScalarGridSpec(
-            num_scalar_prefetch=2,
+            num_scalar_prefetch=3,
             grid=(capacity // per,),
-            in_specs=[unit_spec(j) for j in range(per)] + [slot_spec] * 3,
+            in_specs=[unit_spec(j, c) for c in range(2) for j in range(per)] + [slot_spec] * 3,
             out_specs=[slot_spec] * 3,
         ),
         out_shape=[jax.ShapeDtypeStruct(master.shape, jnp.float32)] * 3,
         compiler_params=pltpu.CompilerParams(vmem_limit_bytes=VMEM_BYTES),
         name="adamw",
-    )(unit_of_slot, used, *([grads] * per), master, first, second)
+    )(kind, at_a, at_b, *([grads_a] * per), *([grads_b] * per), master, first, second)
 
 
 def place():
@@ -293,8 +297,8 @@
     return (z * 2 + y, x * 2 + core)
 
 
-def block_at(z, y, x, core):
-    return (z * 2 + y) * 4 + x * 2 + core
+def piece_at(zb, c, h, a, b):
+    return (((zb * 2 + c) * 2 + h) * 2 + a) * 2 + b
 
 
 def remote(src, dst, send, recv, device):
@@ -310,128 +314,446 @@
     pl.semaphore_wait(barrier, len(devices))
 
 
-def gather_kernel(units, x_ref, out_ref, lsem, zs, zr, as_, ar, bs, br, a2s, a2r, b2s, b2r, ss, sr, sas, sar, sbs, sbr, sa2s, sa2r, sb2s, sb2r):
-    nz = 4
+GATHER_SEMS = [DMA((2,)), DMA((2, 4, 2)), DMA((2, 4, 2)), DMA((2, 4)), DMA((2, 4)), DMA((2, 4, 2)), DMA((2, 4, 2)), DMA((4,)), DMA((4,))]
+
+class Gather:
+    def __init__(self, own, buf, sems):
+        self.own, self.buf = own, buf
+        self.lsem, self.zs, self.zr, self.fs, self.fr, self.ts, self.tr, self.ss, self.sr = sems
+        self.z, self.y, self.x, self.core = place()
+        z, y, x, core = self.z, self.y, self.x, self.core
+        self.xn = device_at(z, y, 1 - x, core)
+        self.yn = device_at(z, 1 - y, x, core)
+        self.sib = device_at(z, y, x, 1 - core)
+    def side(self, h):
+        return (self.y, self.x) if h == 0 else (self.x, self.y)
+    def near(self, h):
+        return (self.xn, self.yn) if h == 0 else (self.yn, self.xn)
+    def keep(self, h):
+        a, b = self.side(h)
+        return pltpu.make_async_copy(self.own.at[h], self.buf.at[piece_at(self.z, self.core, h, a, b)], self.lsem.at[h])
+    def up(self, d, h, step, src=None):
+        a, b = self.side(h)
+        ref = self.buf.at[piece_at(self.z + d, self.core, h, a, b)]
+        k = 0 if step > 0 else 1
+        hop = -d if step > 0 else d
+        return remote(ref if src is None else src, ref, self.zs.at[k, hop, h], self.zr.at[k, hop, h],
+                      device_at(self.z + step, self.y, self.x, self.core))
+    def got(self, d, h):
+        a, b = self.side(h)
+        ref = self.buf.at[piece_at(self.z + d, self.core, h, a, b)]
+        k = 0 if d < 0 else 1
+        hop = abs(d) - 1
+        remote(ref, ref, self.zs.at[k, hop, h], self.zr.at[k, hop, h], self.xn).wait_recv()
+    def first(self, zb, h, mine, src=None):
+        a, b = self.side(h)
+        b = b if mine else 1 - b
+        ref = self.buf.at[piece_at(zb, self.core, h, a, b)]
+        return remote(ref if src is None else src, ref, self.fs.at[h, zb], self.fr.at[h, zb], self.near(h)[0])
+    def second(self, zb, h, j, mine, src=None):
+        a, b = self.side(h)
+        a = a if mine else 1 - a
+        b = b if j == 0 else 1 - b
+        if True:
+            ref = self.buf.at[piece_at(zb, self.core, h, a, b)]
+        return remote(ref if src is None else src, ref, self.ts.at[h, zb, j], self.tr.at[h, zb, j], self.near(h)[1])
+    def whole(self, zb, c):
+        ref = self.buf.at[pl.ds((zb * 2 + c) * 8, 8)]
+        return remote(ref, ref, self.ss.at[zb], self.sr.at[zb], self.sib)
+    def start(self):
+        for h in range(2):
+            self.keep(h).start()
+        for h in range(2):
+            @pl.when(self.z < 3)
+            def _():
+                self.up(0, h, 1, self.own.at[h]).start()
+            @pl.when(self.z > 0)
+            def _():
+                self.up(0, h, -1, self.own.at[h]).start()
+            self.first(self.z, h, True, self.own.at[h]).start()
+        for h in range(2):
+            self.second(self.z, h, 0, True, self.own.at[h]).start()
+        for h in range(2):
+            self.keep(h).wait()
+    def line(self, d, z_ok=None):
+        def work():
+            zb = self.z + d
+            for h in range(2):
+                self.got(d, h)
+                if d < 0:
+                    @pl.when(self.z < 3)
+                    def _():
+                        self.up(d, h, 1).start()
+                else:
+                    @pl.when(self.z > 0)
+                    def _():
+                        self.up(d, h, -1).start()
+                self.first(zb, h, True).start()
+            for h in range(2):
+                self.second(zb, h, 0, True).start()
+        self.there(d, work)
+    def there(self, d, work):
+        if d == 0:
+            work()
+        else:
+            pl.when((self.z + d >= 0) & (self.z + d < 4))(work)
+    def cross(self, d):
+        def work():
+            zb = self.z + d
+            for h in range(2):
+                self.first(zb, h, False).wait_recv()
+                self.second(zb, h, 1, True).start()
+        self.there(d, work)
+    def close(self, d):
+        def work():
+            zb = self.z + d
+            for h in range(2):
+                for j in range(2):
+                    self.second(zb, h, j, False).wait_recv()
+            self.whole(zb, self.core).start()
+        self.there(d, work)
+    def finish(self):
+        for h in range(2):
+            for d in range(4):
+                @pl.when((self.z - d >= 0) & (self.z < 3))
+                def _():
+                    self.up(-d, h, 1).wait_send()
+                @pl.when((self.z + d < 4) & (self.z > 0))
+                def _():
+                    self.up(d, h, -1).wait_send()
+        for zb in range(4):
+            for h in range(2):
+                self.first(zb, h, True).wait_send()
+                for j in range(2):
+                    self.second(zb, h, j, True).wait_send()
+            self.whole(zb, self.core).wait_send()
+            self.whole(zb, 1 - self.core).wait_recv()
+
+
+def reduce_scratch(rows, width):
+    buf = lambda n: pltpu.VMEM((n, rows, width), jnp.bfloat16)
+    return [buf(32), buf(32), buf(16), buf(8), buf(6),
+            DMA((4,)), DMA((4,)), DMA((4,)), DMA((4, 2)), DMA((4, 2)), DMA((4, 2)), DMA((4, 2)), DMA((4, 2)), DMA((4, 2))]
+
+class Reduce:
+    def __init__(self, partial, refs):
+        self.partial = partial
+        (self.acc, self.got0, self.got1, self.got2, self.got3,
+         self.lsem, self.s0, self.r0, self.s1, self.r1, self.s2, self.r2, self.s3, self.r3) = refs
+        self.z, self.y, self.x, self.core = z, y, x, core = place()
+        self.xn = device_at(z, y, 1 - x, core)
+        self.yn = device_at(z, 1 - y, x, core)
+        self.sib = device_at(z, y, x, 1 - core)
+        self.rows = partial.shape[1]
+    def zb(self, t):
+        return (self.z + (2, 1, 3, 0)[t]) % 4
+    def side(self, h):
+        return (self.y, self.x) if h == 0 else (self.x, self.y)
+    def near(self, h):
+        return (self.yn, self.xn) if h == 0 else (self.xn, self.yn)
+    def send0(self, t):
+        zb = self.zb(t)
+        return remote(self.partial.at[pl.ds((zb * 2 + 1 - self.core) * 8, 8)], self.got0.at[pl.ds(zb * 8, 8)], self.s0.at[zb], self.r0.at[zb], self.sib)
+    def keep(self, t):
+        zb = self.zb(t)
+        return pltpu.make_async_copy(self.partial.at[pl.ds((zb * 2 + self.core) * 8, 8)], self.acc.at[pl.ds(zb * 8, 8)], self.lsem.at[zb])
+    def send1(self, t, h):
+        zb = self.zb(t)
+        a, b = self.side(h)
+        return remote(self.acc.at[pl.ds(zb * 8 + h * 4 + (1 - a) * 2, 2)], self.got1.at[pl.ds(zb * 4 + h * 2, 2)], self.s1.at[zb, h], self.r1.at[zb, h], self.near(h)[0])
+    def send2(self, t, h):
+        zb = self.zb(t)
+        a, b = self.side(h)
+        return remote(self.acc.at[zb * 8 + h * 4 + a * 2 + 1 - b], self.got2.at[zb * 2 + h], self.s2.at[zb, h], self.r2.at[zb, h], self.near(h)[1])
+    def send3(self, t, h):
+        zb = self.zb(t)
+        a, b = self.side(h)
+        d = (2, 1, 3)[t]
+        return remote(self.acc.at[zb * 8 + h * 4 + a * 2 + b], self.got3.at[(d - 1) * 2 + h], self.s3.at[d - 1, h], self.r3.at[d - 1, h], device_at(zb, self.y, self.x, self.core))
+    def add(self, dst, src, count):
+        ref, at = src
+        step = 32
+        tiles = self.rows // step
+        def body(i, _):
+            p, r = i // tiles, (i % tiles) * step
+            rows = pl.ds(pl.multiple_of(r, step), step)
+            self.acc[dst + p, rows, :] = self.acc[dst + p, rows, :] + ref[at + p, rows, :]
+            return 0
+        lax.fori_loop(0, count * tiles, body, 0)
+    def start(self):
+        for t in range(4):
+            self.send0(t).start()
+            self.keep(t).start()
+    def add0(self, t):
+        zb = self.zb(t)
+        self.keep(t).wait()
+        self.send0(t).wait_recv()
+        for h in range(2):
+            a, b = self.side(h)
+            lo = h * 4 + (1 - a) * 2
+            self.add(zb * 8 + lo, (self.got0, zb * 8 + lo), 2)
+            self.send1(t, h).start()
+        for h in range(2):
+            a, b = self.side(h)
+            lo = h * 4 + a * 2
+            self.add(zb * 8 + lo, (self.got0, zb * 8 + lo), 2)
+    def add1(self, t):
+        zb = self.zb(t)
+        for h in range(2):
+            a, b = self.side(h)
+            self.send1(t, h).wait_recv()
+            lo = h * 4 + a * 2
+            self.add(zb * 8 + lo + 1 - b, (self.got1, zb * 4 + h * 2 + 1 - b), 1)
+            self.send2(t, h).start()
+            self.add(zb * 8 + lo + b, (self.got1, zb * 4 + h * 2 + b), 1)
+    def add2(self, t):
+        zb = self.zb(t)
+        for h in range(2):
+            a, b = self.side(h)
+            self.send2(t, h).wait_recv()
+            self.add(zb * 8 + h * 4 + a * 2 + b, (self.got2, zb * 2 + h), 1)
+            if t < 3:
+                self.send3(t, h).start()
+    def add3(self):
+        for t in range(3):
+            for h in range(2):
+                self.send3(t, h).wait_recv()
+        step = 32
+        for h in range(2):
+            a, b = self.side(h)
+            at = self.z * 8 + h * 4 + a * 2 + b
+            def body(i, _):
+                rows = pl.ds(pl.multiple_of(i * step, step), step)
+                total = self.acc[at, rows, :].astype(jnp.float32)
+                for q in range(3):
+                    total = total + self.got3[q * 2 + h, rows, :].astype(jnp.float32)
+                self.acc[at, rows, :] = total.astype(jnp.bfloat16)
+                return 0
+            lax.fori_loop(0, self.rows // step, body, 0)
+    def own(self, h):
+        a, b = self.side(h)
+        return self.acc.at[self.z * 8 + h * 4 + a * 2 + b]
+    def finish(self):
+        for t in range(4):
+            self.send0(t).wait_send()
+            for h in range(2):
+                self.send1(t, h).wait_send()
+                self.send2(t, h).wait_send()
+                if t < 3:
+                    self.send3(t, h).wait_send()
+
+class Own:
+    def __init__(self, get): self.at = self; self.get = get
+    def __getitem__(self, h): return self.get(h)
+
+
+def line_neighbours():
     z, y, x, core = place()
-    half = units // 2
-    me = block_at(z, y, x, core)
-    xn = device_at(z, y, 1 - x, core)
-    yn = device_at(z, 1 - y, x, core)
-    sib = device_at(z, y, x, 1 - core)
-    greet([xn, yn, sib] + [device_at((z + d) % nz, y, x, core) for d in (1, 2, 3)])
-    own = pltpu.make_async_copy(x_ref, out_ref.at[me], lsem)
-    own.start()
-
-    def part(i, p):
-        return out_ref.at[i].at[pl.ds(p * half, half)]
-
-    def moved(ref, send, recv, device):
-        return remote(ref, ref, send, recv, device)
-
-    def z_copy(d):
-        return remote(x_ref, out_ref.at[me], zs.at[d - 1], zr.at[d - 1], device_at((z + d) % nz, y, x, core))
-
-    def z_got(zb, d):
-        ref = out_ref.at[block_at(zb, y, x, core)]
-        return moved(ref, zs.at[nz - d - 1], zr.at[nz - d - 1], xn)
-
-    def a_copy(zb, xb):
-        return moved(part(block_at(zb, y, xb, core), 0), as_.at[zb], ar.at[zb], xn)
-
-    def b_copy(zb, yb):
-        return moved(part(block_at(zb, yb, x, core), 1), bs.at[zb], br.at[zb], yn)
-
-    def a2_copy(zb, yb, xb):
-        j = zb * 2 + xb
-        return moved(part(block_at(zb, yb, xb, core), 0), a2s.at[j], a2r.at[j], yn)
-
-    def b2_copy(zb, yb, xb):
-        j = zb * 2 + yb
-        return moved(part(block_at(zb, yb, xb, core), 1), b2s.at[j], b2r.at[j], xn)
-
-    def s_copy(zb, c):
-        return moved(out_ref.at[block_at(zb, y, x, c)], ss.at[zb], sr.at[zb], sib)
-
-    def sa_copy(zb, c):
-        return moved(part(block_at(zb, y, 1 - x, c), 0), sas.at[zb], sar.at[zb], sib)
-
-    def sb_copy(zb, c):
-        return moved(part(block_at(zb, 1 - y, x, c), 1), sbs.at[zb], sbr.at[zb], sib)
-
-    def sa2_copy(zb, xb, c):
-        j = zb * 2 + xb
-        return moved(part(block_at(zb, 1 - y, xb, c), 0), sa2s.at[j], sa2r.at[j], sib)
-
-    def sb2_copy(zb, yb, c):
-        j = zb * 2 + yb
-        return moved(part(block_at(zb, yb, 1 - x, c), 1), sb2s.at[j], sb2r.at[j], sib)
-
-    def first(zb):
-        a_copy(zb, x).start()
-        b_copy(zb, y).start()
-        a2_copy(zb, y, x).start()
-        b2_copy(zb, y, x).start()
-        s_copy(zb, core).start()
-
-    def second(zb):
-        a_copy(zb, 1 - x).wait_recv()
-        a2_copy(zb, y, 1 - x).start()
-        sa_copy(zb, core).start()
-        b_copy(zb, 1 - y).wait_recv()
-        b2_copy(zb, 1 - y, x).start()
-        sb_copy(zb, core).start()
-
-    for d in (1, 3, 2):
-        z_copy(d).start()
-    own.wait()
-    order = [z, (z + 1) % nz, (z + 3) % nz, (z + 2) % nz]
-    first(z)
-    for n, d in enumerate((1, 3, 2)):
-        zb = (z + d) % nz
-        z_got(zb, d).wait_recv()
-        first(zb)
-        second(order[n])
-    second(order[3])
-    for zb in order:
-        for xb in (x, 1 - x):
-            a2_copy(zb, 1 - y, xb).wait_recv()
-            sa2_copy(zb, xb, core).start()
-        for yb in (y, 1 - y):
-            b2_copy(zb, yb, 1 - x).wait_recv()
-            sb2_copy(zb, yb, core).start()
-    for d in (1, 2, 3):
-        z_copy(d).wait_send()
-    for zb in range(nz):
-        a_copy(zb, x).wait_send()
-        b_copy(zb, y).wait_send()
-        s_copy(zb, core).wait_send()
-        s_copy(zb, 1 - core).wait_recv()
-        sa_copy(zb, core).wait_send()
-        sa_copy(zb, 1 - core).wait_recv()
-        sb_copy(zb, core).wait_send()
-        sb_copy(zb, 1 - core).wait_recv()
-        for q in range(2):
-            a2_copy(zb, y, q).wait_send()
-            b2_copy(zb, q, x).wait_send()
-            sa2_copy(zb, q, core).wait_send()
-            sa2_copy(zb, q, 1 - core).wait_recv()
-            sb2_copy(zb, q, core).wait_send()
-            sb2_copy(zb, q, 1 - core).wait_recv()
-
-
-def gather_call(block, collective_id):
-    units = block.shape[0]
-    sems = [DMA] + [DMA((3,))] * 2 + [DMA((4,))] * 4 + [DMA((8,))] * 4 + [DMA((4,))] * 6 + [DMA((8,))] * 4
-    out = pl.pallas_call(
-        functools.partial(gather_kernel, units),
-        out_shape=jax.ShapeDtypeStruct((32,) + block.shape, block.dtype),
-        in_specs=[pl.BlockSpec(memory_space=pl.ANY)],
-        out_specs=pl.BlockSpec(memory_space=pl.ANY),
-        scratch_shapes=sems,
-        compiler_params=pltpu.CompilerParams(collective_id=collective_id, has_side_effects=True),
-        name="gather_units",
-    )(block)
-    return out.reshape((-1,) + block.shape[1:])
+    return [device_at(z, y, 1 - x, core), device_at(z, 1 - y, x, core), device_at(z, y, x, 1 - core)] + [
+        device_at((z + d) % 4, y, x, core) for d in (1, 2, 3)
+    ]
+
+
+def run_gathers(first, second):
+    pair = (first, second)
+    for g in pair:
+        g.start()
+    for g in pair:
+        g.line(-1), g.line(1), g.cross(0)
+    for g in pair:
+        g.line(-2), g.line(2), g.cross(-1), g.cross(1), g.close(0)
+    for g in pair:
+        g.line(-3), g.line(3), g.cross(-2), g.cross(2), g.close(-1), g.close(1)
+    for g in pair:
+        g.cross(-3), g.cross(3), g.close(-2), g.close(2)
+    for g in pair:
+        g.close(-3), g.close(3)
+    for g in pair:
+        g.finish()
+
+
+def spread_kernel(a_ref, b_ref, oa_ref, ob_ref, got_a, got_b, new_a, new_b, own_a, own_b, send, recv, *sems):
+    z, y, x, core = place()
+    m = len(GATHER_SEMS)
+    ga = Gather(own_a, oa_ref, sems[:m])
+    gb = Gather(own_b, ob_ref, sems[m:])
+    greet(line_neighbours())
+    jobs = ((a_ref, got_a, new_a, own_a), (b_ref, got_b, new_b, own_b))
+
+    def to_core(i):
+        given, got, new, own = jobs[i]
+        return remote(given.at[1 - core], got, send.at[i], recv.at[i], ga.sib)
+
+    def to_x(i):
+        given, got, new, own = jobs[i]
+        return remote(got.at[1 - x], new, send.at[2 + i], recv.at[2 + i], ga.xn)
+
+    for i in range(2):
+        to_core(i).start()
+    for i in range(2):
+        given, got, new, own = jobs[i]
+        to_core(i).wait_recv()
+        got[1 - x] = got[1 - x] + given[core, 1 - x]
+        to_x(i).start()
+        own[...] = got[x] + given[core, x]
+    for i in range(2):
+        given, got, new, own = jobs[i]
+        to_x(i).wait_recv()
+        own[...] = own[...] + new[...]
+    run_gathers(ga, gb)
+    for i in range(2):
+        to_core(i).wait_send()
+        to_x(i).wait_send()
+
+
+def spread_call(given_a, given_b, collective_id):
+    scratch = []
+    for lead in (1, 0, 0):
+        for g in (given_a, given_b):
+            scratch.append(pltpu.VMEM(g.shape[1:] if lead else g.shape[2:], g.dtype))
+    vmem = pl.BlockSpec(memory_space=pltpu.VMEM)
+    any_ = pl.BlockSpec(memory_space=pl.ANY)
+    return pl.pallas_call(
+        spread_kernel,
+        out_shape=tuple(
+            jax.ShapeDtypeStruct((64,) + g.shape[3:], g.dtype) for g in (given_a, given_b)
+        ),
+        in_specs=[vmem] * 2,
+        out_specs=(any_,) * 2,
+        scratch_shapes=scratch + [DMA((4,)), DMA((4,))] + GATHER_SEMS * 2,
+        compiler_params=pltpu.CompilerParams(
+            collective_id=collective_id, has_side_effects=True, vmem_limit_bytes=VMEM_BYTES
+        ),
+        name="spread_units",
+    )(given_a, given_b)
+
+
+GAIN_SEMS = [DMA((6,)), DMA((6,))]
+
+
+class GainSum:
+    def __init__(self, ref, got, line, sems):
+        self.ref, self.got, self.all = ref, got, line
+        self.send, self.recv = sems
+        self.z, self.y, self.x, self.core = place()
+
+    def step(self, i):
+        z, y, x, core = self.z, self.y, self.x, self.core
+        to = (device_at(z, y, x, 1 - core), device_at(z, y, 1 - x, core), device_at(z, 1 - y, x, core))[i]
+        return remote(self.ref, self.got.at[i], self.send.at[i], self.recv.at[i], to)
+
+    def far(self, d):
+        to = device_at((self.z + d) % 4, self.y, self.x, self.core)
+        return remote(self.ref, self.all.at[self.z], self.send.at[2 + d], self.recv.at[2 + d], to)
+
+    def begin(self, i):
+        self.step(i).start()
+
+    def end(self, i):
+        self.step(i).wait()
+        self.ref[...] = self.ref[...] + self.got[i]
+
+    def begin_far(self):
+        for d in (1, 2, 3):
+            self.far(d).start()
+        self.all[self.z] = self.ref[...]
+
+    def end_far(self, out):
+        for d in (1, 2, 3):
+            self.far(d).wait()
+        total = self.all[0]
+        for i in range(1, 4):
+            total = total + self.all[i]
+        out[...] = total
+
+
+def sum_kernel(a_ref, b_ref, gain_ref, oa_ref, ob_ref, og_ref, gain, gain_got, gain_all, *refs):
+    n = len(reduce_scratch(1, 1))
+    m = len(GATHER_SEMS)
+    ra, rb = Reduce(a_ref, refs[:n]), Reduce(b_ref, refs[n : 2 * n])
+    refs = refs[2 * n :]
+    ga, gb = Gather(Own(ra.own), oa_ref, refs[:m]), Gather(Own(rb.own), ob_ref, refs[m : 2 * m])
+    gs = GainSum(gain, gain_got, gain_all, refs[2 * m :])
+    greet(line_neighbours())
+    gain[...] = gain_ref[...]
+    gs.begin(0)
+    rb.start()
+    ra.start()
+    for t in range(4):
+        rb.add0(t)
+    gs.end(0), gs.begin(1)
+    rb.add1(0)
+    rb.add1(1), rb.add2(0)
+    gs.end(1), gs.begin(2)
+    rb.add1(2), rb.add2(1)
+    ra.add0(0), ra.add0(1)
+    gs.end(2), gs.begin_far()
+    rb.add1(3), rb.add2(2)
+    ra.add0(2), ra.add0(3)
+    rb.add2(3)
+    ra.add1(0)
+    rb.add3()
+    gb.start()
+    ra.add1(1), ra.add2(0)
+    ra.add1(2), ra.add2(1)
+    gb.line(-1), gb.line(1)
+    ra.add1(3), ra.add2(2)
+    gb.cross(0)
+    ra.add2(3)
+    gb.line(-2), gb.line(2)
+    ra.add3()
+    gb.cross(-1), gb.cross(1)
+    ga.start()
+    gb.close(0)
+    gb.line(-3), gb.line(3)
+    ga.line(-1), ga.line(1)
+    gb.cross(-2), gb.cross(2)
+    ga.cross(0)
+    gb.close(-1), gb.close(1)
+    ga.line(-2), ga.line(2)
+    gb.cross(-3), gb.cross(3)
+    ga.cross(-1), ga.cross(1)
+    gb.close(-2), gb.close(2)
+    ga.close(0)
+    ga.line(-3), ga.line(3)
+    gb.close(-3), gb.close(3)
+    ga.cross(-2), ga.cross(2)
+    ga.close(-1), ga.close(1)
+    ga.cross(-3), ga.cross(3)
+    ga.close(-2), ga.close(2)
+    ga.close(-3), ga.close(3)
+    gs.end_far(og_ref)
+    ra.finish(), rb.finish(), ga.finish(), gb.finish()
+
+
+def sum_call(grads_a, grads_b, gain_part, collective_id):
+    any_ = pl.BlockSpec(memory_space=pl.ANY)
+    vmem = pl.BlockSpec(memory_space=pltpu.VMEM)
+    width = grads_a.shape[2]
+    gain = gain_part.shape
+    return pl.pallas_call(
+        sum_kernel,
+        out_shape=(
+            jax.ShapeDtypeStruct(grads_a.shape, grads_a.dtype),
+            jax.ShapeDtypeStruct(grads_b.shape, grads_b.dtype),
+            jax.ShapeDtypeStruct(gain, jnp.float32),
+        ),
+        in_specs=[any_, any_, vmem],
+        out_specs=(any_, any_, vmem),
+        scratch_shapes=[
+            pltpu.VMEM(gain, jnp.float32),
+            pltpu.VMEM((3,) + gain, jnp.float32),
+            pltpu.VMEM((4,) + gain, jnp.float32),
+        ]
+        + reduce_scratch(grads_a.shape[1], width)
+        + reduce_scratch(grads_b.shape[1], width)
+        + GATHER_SEMS * 2
+        + GAIN_SEMS,
+        compiler_params=pltpu.CompilerParams(
+            collective_id=collective_id, has_side_effects=True, vmem_limit_bytes=VMEM_BYTES
+        ),
+        name="sum_units",
+    )(grads_a, grads_b, gain_part)
 
 
 def swap_kernel(parts, n, x_ref, out_ref, lsem, send, recv):
@@ -535,25 +857,42 @@
     device_count = n * groups
     my_width = width // n
 
-    per = -(-units // device_count)
-    padded = per * device_count
+    split = 4 * width // unit_rows
     rank = unit_places(unit_owner, capacity, groups)
-    piece = ctx * groups * per + jnp.arange(groups * per, dtype=jnp.int32)
-    piece_units = jnp.minimum(piece, units - 1)
-    owners = unit_owner[piece_units]
-    mine = (owners == shard) & (piece < units)
-    given = jnp.where(
-        mine[:, None, None], jnp.take(master, rank[piece_units], axis=0, mode="clip"), 0.0
-    ).astype(jnp.bfloat16)
-    own_units = lax.psum_scatter(given, "shard", scatter_dimension=0, tiled=True)
+
+    def share_of(first, count, per, wanted):
+        at = wanted[..., None] * per + jnp.arange(per, dtype=jnp.int32)
+        unit = first + jnp.minimum(at, count - 1)
+        mine = (unit_owner[unit] == shard) & (at < count)
+        shape = at.shape[:-1] + (per * unit_rows, width)
+        taken = jnp.take(master, rank[unit].reshape(-1), axis=0, mode="clip")
+        kept = jnp.where(mine.reshape(-1, 1, 1), taken, 0.0).astype(jnp.bfloat16)
+        return kept.reshape(shape)
+
+    chunks = ((0, split), (split, units - split))
     if fast:
-        stack = gather_call(own_units, 0)
+        z, y, x, core = place()
+        wanted = jnp.stack(
+            [
+                jnp.stack([jnp.stack([piece_at(z, c, 0, y, q), piece_at(z, c, 1, q, y)]) for q in range(2)])
+                for c in range(2)
+            ]
+        )
+        given = [share_of(first, count, -(-count // 64), wanted) for first, count in chunks]
+        stack_a, stack_b = spread_call(given[0], given[1], 0)
     else:
-        stack = lax.all_gather(own_units, BOTH, axis=0, tiled=True)
-    stacked = stack.reshape(padded * unit_rows, width)
-    w_out = stacked[3 * width : 4 * width]
-    w_up = stacked[4 * width : 4 * width + 2 * FF]
-    w_down = stacked[4 * width + 2 * FF : 4 * width + 3 * FF]
+        wanted = ctx * groups + jnp.arange(groups, dtype=jnp.int32)
+        stacks = []
+        for first, count in chunks:
+            given = share_of(first, count, -(-count // device_count), wanted)
+            own = lax.psum_scatter(given, "shard", scatter_dimension=0, tiled=True)
+            stacks.append(lax.all_gather(own, BOTH, axis=0, tiled=True))
+        stack_a, stack_b = stacks
+    stack_a = stack_a.reshape(-1, width)
+    stack_b = stack_b.reshape(-1, width)
+    w_out = stack_a[3 * width : 4 * width]
+    w_up = stack_b[: 2 * FF]
+    w_down = stack_b[2 * FF : 3 * FF]
 
     positions = ctx * block_len + jnp.arange(block_len, dtype=jnp.int32)
     tile_heads = 256 // HEAD_DIM
@@ -566,8 +905,8 @@
 
     inputs = tokens.astype(jnp.float32).reshape(rows_all, width)
     norm_one = layer_norm(inputs, norm_gains[0]).astype(jnp.bfloat16)
-    qkv = qkv_call(norm_one, stacked, cos_rows, sin_rows)
-    qkv_rows = jnp.transpose(qkv.reshape(slots, block_len, 3, width), (2, 0, 1, 3))
+    qkv = qkv_call(norm_one, stack_a, cos_rows, sin_rows)
+    qkv_rows = qkv.reshape(3, slots, block_len, width)
     qkv_heads = to_heads(qkv_rows, n, fast, 1, "swap_qkv")
     mixed_heads, wide, lse = attend_call(qkv_heads, bias)
     mixed_low = to_rows(mixed_heads[None], n, fast, 2, "swap_mixed").reshape(rows_all, width)
@@ -585,11 +924,11 @@
     grad_down_low = grad_result.astype(jnp.bfloat16)
     grad_w_down = leading(hidden_low, grad_down_low)
     grad_hidden = transposed(grad_down_low, w_down)
-    gelu_value, gelu_back = jax.vjp(gated_gelu, upper_proj)
+    _, gelu_back = jax.vjp(gated_gelu, upper_proj)
     grad_upper_low = gelu_back(grad_hidden)[0].astype(jnp.bfloat16)
     grad_w_up = leading(grad_upper_low, norm_two)
     grad_norm_two = jnp.dot(grad_upper_low, w_up, preferred_element_type=jnp.float32)
-    norm_value, norm_back_two = jax.vjp(layer_norm, middle, norm_gains[1])
+    _, norm_back_two = jax.vjp(layer_norm, middle, norm_gains[1])
     grad_middle_part, grad_gain_two = norm_back_two(grad_norm_two)
     grad_middle = grad_result + grad_middle_part
     grad_attn_low = grad_middle.astype(jnp.bfloat16)
@@ -602,44 +941,66 @@
     )[0]
     grad_qkv_heads = attend_back_call(qkv_heads, grad_heads, wide, lse, bias, cos_seq, sin_seq)
     grad_qkv_rows = to_rows(grad_qkv_heads, n, fast, 4, "swap_grad_qkv")
-    grad_qkv_low = jnp.transpose(grad_qkv_rows, (1, 2, 0, 3)).reshape(rows_all, 3 * width)
-
-    grad_w_qkv = leading(grad_qkv_low, norm_one)
-    grad_norm_one = jnp.dot(
-        grad_qkv_low, stacked[: 3 * width], preferred_element_type=jnp.float32
-    )
-    first_value, norm_back_one = jax.vjp(layer_norm, inputs, norm_gains[0])
+    grad_qkv_low = grad_qkv_rows.reshape(3, rows_all, width)
+    grad_norm_one = sum(
+        jnp.dot(
+            grad_qkv_low[i],
+            stack_a[i * width : (i + 1) * width],
+            preferred_element_type=jnp.float32,
+        )
+        for i in range(3)
+    )
+    _, norm_back_one = jax.vjp(layer_norm, inputs, norm_gains[0])
     grad_input_part, grad_gain_one = norm_back_one(grad_norm_one)
     token_grad = (
         (grad_middle + grad_input_part).astype(jnp.bfloat16).reshape(slots, block_len, width)
     )
 
-    unit_grads = jnp.concatenate(
+    low = jnp.bfloat16
+    grads_a = jnp.concatenate(
+        [leading(grad_qkv_low[i], norm_one).astype(low) for i in range(3)]
+        + [grad_w_out.astype(low)]
+        + [jnp.zeros((stack_a.shape[0] - split * unit_rows, width), low)],
+        axis=0,
+    )
+    grads_b = jnp.concatenate(
         [
-            grad_w_qkv.astype(jnp.bfloat16),
-            grad_w_out.astype(jnp.bfloat16),
-            grad_w_up.astype(jnp.bfloat16),
-            grad_w_down.astype(jnp.bfloat16),
-            jnp.zeros(((padded - units) * unit_rows, width), jnp.bfloat16),
+            grad_w_up.astype(low),
+            grad_w_down.astype(low),
+            jnp.zeros((stack_b.shape[0] - (units - split) * unit_rows, width), low),
         ],
         axis=0,
-    ).reshape(padded, unit_rows, width)
-    own_grads = lax.psum_scatter(unit_grads, BOTH, scatter_dimension=0, tiled=True)
+    )
+    gain_part = jnp.zeros((8, width), jnp.float32).at[:2].set(
+        jnp.stack([grad_gain_one, grad_gain_two])
+    )
     if fast:
-        all_grads = gather_call(own_grads, 0)
+        all_a, all_b, gain_grad = sum_call(
+            grads_a.reshape(64, -1, width), grads_b.reshape(64, -1, width), gain_part, 5
+        )
     else:
-        all_grads = lax.all_gather(own_grads, BOTH, axis=0, tiled=True)
-    gain_grad = lax.psum(jnp.stack([grad_gain_one, grad_gain_two]), BOTH)
+        all_a, all_b = (
+            lax.all_gather(
+                lax.psum_scatter(g, BOTH, scatter_dimension=0, tiled=True), BOTH, axis=0, tiled=True
+            )
+            for g in (grads_a, grads_b)
+        )
+        gain_grad = lax.psum(gain_part, BOTH)
+    gain_grad = gain_grad[:2]
+    all_a = all_a.reshape(-1, unit_rows, width)
+    all_b = all_b.reshape(-1, unit_rows, width)
 
     slot_index = jnp.where(unit_owner == shard, rank, capacity)
     unit_of_slot = (
-        jnp.zeros((capacity + 1,), jnp.int32)
+        jnp.full((capacity + 1,), -1, jnp.int32)
         .at[slot_index]
         .set(jnp.arange(units, dtype=jnp.int32))[:capacity]
     )
-    used = (jnp.arange(capacity) < jnp.sum(unit_owner == shard)).astype(jnp.int32)
+    kind = jnp.where(unit_of_slot < 0, -1, (unit_of_slot >= split).astype(jnp.int32))
+    at_a = jnp.maximum(lax.cummax(jnp.where(kind == 0, unit_of_slot, -1)), 0)
+    at_b = jnp.maximum(lax.cummax(jnp.where(kind == 1, unit_of_slot, -1)) - split, 0)
     new_master, new_first, new_second = adam_call(
-        unit_of_slot, used, all_grads, master, first_moment, second_moment
+        kind, at_a, at_b, all_a, all_b, master, first_moment, second_moment
     )
     new_gains, new_gain_first, new_gain_second = adam_update(
         norm_gains, gain_grad, gain_first, gain_second, rate_gain, 0.0

time: 869 us -> 706 us (0.81)
  waiting for transfers between devices: 214 us -> 0 us
  Pallas kernels: 471 us -> 567 us
  blocking collectives: 49.6 us -> 0 us
  other arithmetic: 24.9 us -> 43 us
  between operations: 14.9 us -> 1.73 us
    reduce_scatter x2 -> x0, waiting for transfers between devices: 214 us -> none  [the longest x1 184 us: shards(): lax.psum_scatter(unit_grads, BOTH, scatter_dimension=0, tiled=True)]
    pallas_call x2, Pallas kernels: 270 us -> 375 us  [the longest x1 238 us: sum_call(): pl.pallas_call(sum_kernel, out_shape=(jax.ShapeDtypeStruct(grads_a.shape,...]
    psum x1 -> x0, blocking collectives: 49.6 us -> none  [shards(): gain_grad = lax.psum(jnp.stack([grad_gain_one, grad_gain_two]), BOTH)]
    concatenate x0 -> x2, other arithmetic: none -> 14.6 us  [the longest x1 10.6 us: shards(): jnp.concatenate([grad_w_up.astype(low), grad_w_down.astype(low), jnp.zero...]
    pallas_call x1, Pallas kernels: 55 us -> 45.4 us  [adam_call(): pl.pallas_call(functools.partial(adam_kernel, per), grid_spec=pltpu.Prefe...]
    slice x3, local copies, waits for them, and re-layouts: 3.79 us -> 13.4 us  [the longest x1 5.98 us: shards(): w_up = stack_b[:2 * FF]]
    dot_general x4 -> x6, matrix products: 19.6 us -> 12.2 us  [leading(): lax.dot_general(left, right, (((0,), (0,)), ((), ())), preferred_element_...]
  transfers between devices with their start and end apart: 2 -> 0, of which waited for: 2 -> 0; matrix products, arithmetic and copies ran while one was open for 4% -> 0% of each run, Pallas kernels for 0% -> 0%
where the time goes in v2:
time: 706 us; the launch traced here: 695 us
  Pallas kernels  567 us (80%)
  matrix products  47.1 us (7%)
  other arithmetic  43 us (6%)
  local copies, waits for them, and re-layouts  36.7 us (5%)
    pallas_call x1, Pallas kernels, sum_call(): pl.pallas_call(sum_kernel, out_shape=(jax.ShapeDtypeStruct(grads_a.shape,...  238 us
    pallas_call x1, Pallas kernels, spread_call(): pl.pallas_call(spread_kernel, out_shape=tuple((jax.ShapeDtypeStruct((64,)...  137 us
    pallas_call x4, Pallas kernels, swap_call(): pl.pallas_call(functools.partial(swap_back_kernel if back else swap_kerne...  102 us
    pallas_call x1, Pallas kernels, adam_call(): pl.pallas_call(functools.partial(adam_kernel, per), grid_spec=pltpu.Prefe...  45.4 us
    dot_general x3, matrix products, transposed(): lax.dot_general(left, right, (((1,), (1,)), ((), ())), preferred_element_...  21.2 us
    pallas_call x1, Pallas kernels, attend_back_call(): pl.pallas_call(functools.partial(attend_back_kernel, slots, chunk), out_s...  19.2 us
    gather x4, local copies, waits for them, and re-layouts, share_of(): taken = jnp.take(master, rank[unit].reshape(-1), axis=0, mode='clip')  15.1 us

profile of v2, /device:TPU:0, one launch (start us, length us, event | category | flops | bytes accessed | tf_op | source)
XLA Modules:
  0.0 695.4 jit_solution(2258502451558896729)
XLA Ops:
  3.5 1.3 multiply_reduce_fusion.5
  6.2 1.3 gather_fusion
  18.6 6.9 gather_fusion.2
  26.8 1.9 fusion.22
  28.7 1.9 pad_maximum_fusion.1
  30.5 7.0 %gather_fusion.5 = bf16[16,64,1024]{2,1,0:T(8,128)(2,1)S(1)} fusion(f32[70,64,1024]{2,1,0:T(8,128)} %refs_14_.1, s32[1024]{0:T(1024)S(1)} %pad_clamp_fusion), kind=kCustom, calls=%fused_computation.5 | custom fusion | bytes 4194368 | tf_op jit(solution)/shard_map/jit(_take)/gather | solution.py:868
  37.5 1.8 select_convert_fusion.b_ref
  39.2 137.1 %spread_units.1 = (bf16[64,64,1024]{2,1,0:T(8,128)(2,1)}, bf16[64,128,1024]{2,1,0:T(8,128)(2,1)}) custom-call(bf16[2,2,2,64,1024]{4,3,2,1,0:T(8,128)(2,1)} %select_convert_fusion.1.a_ref, bf16[2,2,2,128,1024]{4,3,2,1,0:T(8,128)(2,1)} %select_convert_fusion.b_ref), custom_call_target="tpu_custom_call" | custom-call | tf_op jit(solution)/shard_map/spread_units/pallas_call | solution.py:616
  176.4 11.8 %qkv.1 = bf16[3,256,1024]{2,1,0:T(8,128)(2,1)} custom-call(bf16[256,1024]{1,0:T(8,128)(2,1)} %multiply_convert_fusion.3.norm_ref, bf16[4096,1024]{1,0:T(8,128)(2,1)} %bitcast.146, f32[256,256]{1,0:T(8,128)} %concatenate.33.cos_ref, f32[256,256]{1,0:T(8,128)} %concatenate.34.sin_ref), custom_call_target="tpu_custom_call" | custom-call | tf_op jit(solution)/shard_map/qkv/pallas_call | solution.py:111
  188.2 30.1 %swap_qkv.1.qkv_ref = bf16[3,2,1024,128]{3,2,1,0:T(8,128)(2,1)} custom-call(bf16[3,2,128,1024]{3,2,1,0:T(8,128)(2,1)} %bitcast.160), custom_call_target="tpu_custom_call" | custom-call | tf_op jit(solution)/shard_map/swap_qkv/pallas_call | solution.py:811
  218.4 13.8 %attend.1 = (bf16[2,1024,128]{2,1,0:T(8,128)(2,1)}, f32[2,1024,128]{2,1,0:T(8,128)}, f32[2,1024,128]{2,1,0:T(8,128)}) custom-call(bf16[3,2,1024,128]{3,2,1,0:T(8,128)(2,1)} %swap_qkv.1.qkv_ref, f32[2,1,1024]{2,1,0:T(1,128)} %compare_select_fusion.bias_ref), custom_call_target="tpu_custom_call" | custom-call | tf_op jit(solution)/shard_map/attend/pallas_call | solution.py:218
  232.1 23.5 %swap_mixed.1 = bf16[1,2,128,1024]{3,2,1,0:T(8,128)(2,1)} custom-call(bf16[1,2,1024,128]{3,2,1,0:T(8,128)(2,1)} %bitcast.172), custom_call_target="tpu_custom_call" | custom-call | tf_op jit(solution)/shard_map/swap_mixed/pallas_call | solution.py:811
  255.7 5.8 fusion.49
  262.6 6.0 slice.102
  268.6 8.8 %fusion.45 = f32[256,5248]{1,0:T(8,128)} fusion(bf16[5248,1024]{1,0:T(8,128)(2,1)S(1)} %bitcast.147, f32[256,1024]{1,0:T(8,128)S(1)} %get-tuple-element.81, f32[1024]{0:T(1024)S(1)} %bitcast.179, f32[256]{0:T(256)S(1)} %fusion.28, f32[256]{0:T(256)S(1)} %broadcast_multiply_fusion), kind=kOutput, calls=%fused_computation.149 | convolution fusion | flops 2752512000 | bytes 17176576 | tf_op jit(solution)/shard_map/dot_general | solution.py:31
  277.4 11.5 %fusion.19 = (f32[256,2624]{1,0:T(8,128)S(1)}, f32[256,2624]{1,0:T(8,128)}, f32[256,2624]{1,0:T(8,128)}) fusion(f32[256,5248]{1,0:T(8,128)} %fusion.45, bf16[256,1024]{1,0:T(8,128)(2,1)S(1)} %copy-done.12, bf16[8192,1024]{1,0:T(8,128)(2,1)} %bitcast.158), kind=kOutput, calls=%fused_computation.64 | convolution fusion | flops 1419395072 | bytes 16711680 | tf_op jit(solution)/shard_map/dot_general | solution.py:31
  288.9 6.8 multiply_add_fusion
  295.7 6.5 fusion.14
  302.2 3.5 multiply_reduce_fusion
  307.0 1.5 convolution_convert_fusion.6
  308.5 15.6 %swap_grad.1 = bf16[1,2,1024,128]{3,2,1,0:T(8,128)(2,1)} custom-call(bf16[1,2,128,1024]{3,2,1,0:T(8,128)(2,1)} %bitcast.173), custom_call_target="tpu_custom_call" | custom-call | tf_op jit(solution)/shard_map/swap_grad/pallas_call | solution.py:811
  324.1 19.2 %attend_back.1.x_ref = bf16[3,2,1024,128]{3,2,1,0:T(8,128)(2,1)} custom-call(bf16[3,2,1024,128]{3,2,1,0:T(8,128)(2,1)} %swap_qkv.1.qkv_ref, bf16[2,1024,128]{2,1,0:T(8,128)(2,1)} %bitcast.170, f32[2,1024,128]{2,1,0:T(8,128)} %get-tuple-element.34.wide_ref, f32[2,1024,128]{2,1,0:T(8,128)} %get-tuple-element.35.lse_ref, ...), custom_call_target="tpu_custom_call" | custom-call | tf_op jit(solution)/shard_map/attend_back/pallas_call | solution.py:242
  343.4 32.6 %swap_grad_qkv.1 = bf16[3,2,128,1024]{3,2,1,0:T(8,128)(2,1)} custom-call(bf16[3,2,1024,128]{3,2,1,0:T(8,128)(2,1)} %attend_back.1.x_ref), custom_call_target="tpu_custom_call" | custom-call | tf_op jit(solution)/shard_map/swap_grad_qkv/pallas_call | solution.py:811
  376.0 1.6 fusion.50
  381.8 1.3 add_convert_fusion.1
  386.8 3.9 pad_maximum_fusion
  390.7 6.2 convolution_convert_fusion
  397.0 2.9 convolution_convert_fusion.1
  399.9 10.6 %maximum_maximum_fusion = bf16[8192,1024]{1,0:T(8,128)(2,1)} fusion(bf16[2624,1024]{1,0:T(8,128)(2,1)S(1)} %convolution_convert_fusion.1, bf16[5248,1024]{1,0:T(8,128)(2,1)S(1)} %convolution_convert_fusion, bf16[8192]{0:T(1024)(128)(2,1)S(1)} %pad.20.clone), kind=kLoop, calls=%fused_computation.7 | loop fusion | flops 50331648 | bytes 32915456 | tf_op jit(solution)/shard_map/concatenate | solution.py:966
  410.6 237.5 %sum_units.1 = (bf16[64,64,1024]{2,1,0:T(8,128)(2,1)}, bf16[64,128,1024]{2,1,0:T(8,128)(2,1)}, f32[8,1024]{1,0:T(8,128)}) custom-call(bf16[64,64,1024]{2,1,0:T(8,128)(2,1)} %bitcast.145, bf16[64,128,1024]{2,1,0:T(8,128)(2,1)} %bitcast.143, f32[8,1024]{1,0:T(8,128)} %select_maximum_fusion.gain_ref), custom_call_target="tpu_custom_call" | custom-call | tf_op jit(solution)/shard_map/sum_units/pallas_call | solution.py:734
  648.1 1.4 multiply_subtract_fusion
  649.5 45.4 %adamw.1 = (f32[70,64,1024]{2,1,0:T(8,128)}, f32[70,64,1024]{2,1,0:T(8,128)}, f32[70,64,1024]{2,1,0:T(8,128)}) custom-call(s32[70]{0:T(128)} %copy-done.20, s32[70]{0:T(128)} %get-tuple-element.95.a_ref, s32[70]{0:T(128)} %get-tuple-element.94.b_ref, bf16[64,64,1024]{2,1,0:T(8,128)(2,1)} %get-tuple-element.36.refs_0_.refs_1_.refs_2_.refs_3_.refs_4_.refs_5_.refs_6_, ...), custom_call_target="tpu_custom_call" | custom-call | tf_op jit(solution)/shard_map/adamw/pallas_call | solution.py:277
  (127 shorter events, 26.4 us)
Async XLA Ops:
  0.6 7.4 %copy-start = (s32[187]{0:T(256)S(1)}, s32[187]{0:T(256)}, u32[]{:S(2)}) copy-start(s32[187]{0:T(256)} %param.15) | copy-start | bytes 2248
  9.9 1.6 copy-start.20
  10.8 1.1 copy-start.19
  10.8 1.8 copy-start.16
  11.5 4.7 copy-start.1
  11.5 5.0 copy-start.8
  255.7 5.8 copy-start.10
  262.3 43.4 %copy-start.2 = (f32[256,1024]{1,0:T(8,128)}, f32[256,1024]{1,0:T(8,128)S(1)}, u32[]{:S(2)}) copy-start(f32[256,1024]{1,0:T(8,128)S(1)} %get-tuple-element.81) | copy-start | bytes 3145732
  268.6 8.8 %copy-start.12 = (bf16[256,1024]{1,0:T(8,128)(2,1)S(1)}, bf16[256,1024]{1,0:T(8,128)(2,1)}, u32[]{:S(2)}) copy-start(bf16[256,1024]{1,0:T(8,128)(2,1)} %fusion.18) | copy-start | bytes 1572868
  288.9 13.3 %copy-start.11 = (f32[256,2624]{1,0:T(8,128)}, f32[256,2624]{1,0:T(8,128)S(1)}, u32[]{:S(2)}) copy-start(f32[256,2624]{1,0:T(8,128)S(1)} %get-tuple-element.53) | copy-start | bytes 8060932
  295.7 6.5 copy-start.7
  295.7 6.5 copy-start.3
  305.7 1.0 copy-start.9
  307.0 1.5 copy-start.14
  376.0 2.1 copy-start.5
  376.0 2.8 copy-start.6
  378.8 1.6 copy-start.4
  381.2 2.5 copy-start.15
  390.7 6.3 copy-start.13
  410.6 237.6 %copy-start.17 = (f32[2,1024]{1,0:T(2,128)S(1)}, f32[2,1024]{1,0:T(2,128)}, u32[]{:S(2)}) copy-start(f32[2,1024]{1,0:T(2,128)} %param.20) | copy-start | bytes 24580
  410.6 237.6 %copy-start.18 = (f32[2,1024]{1,0:T(2,128)S(1)}, f32[2,1024]{1,0:T(2,128)}, u32[]{:S(2)}) copy-start(f32[2,1024]{1,0:T(2,128)} %param.21) | copy-start | bytes 24580

commit v3 on v2

v3 whole, which is shorter than its diff:
```python
import functools

import jax
import jax.numpy as jnp
from jax import lax
from jax.experimental import pallas as pl
from jax.experimental.pallas import tpu as pltpu
from jax.sharding import PartitionSpec as P

HEADS = 16
HEAD_DIM = 64
FF = 2624
FF_WIDE = -(-FF // 128) * 128
STEP = 10
MESH = pl.DeviceIdType.MESH
DMA = pltpu.SemaphoreType.DMA

eps_norm = 1e-05
rope_base = 160000.0
mask_fill = -1e30
beta_one = 0.9
beta_two = 0.98
adam_eps = 1e-06
rate_matrix = 0.03
rate_gain = 0.6
decay_matrix = 0.01
BOTH = ("ctx", "shard")
VMEM_BYTES = 60 * 2**20


def transposed(left, right):
    return lax.dot_general(
        left, right, (((1,), (1,)), ((), ())), preferred_element_type=jnp.float32
    )


def leading(left, right):
    return lax.dot_general(
        left, right, (((0,), (0,)), ((), ())), preferred_element_type=jnp.float32
    )


def layer_norm(values, gain):
    row_mean = jnp.mean(values, axis=-1, keepdims=True)
    centred = values - row_mean
    variance = jnp.mean(centred * centred, axis=-1, keepdims=True)
    return centred * lax.rsqrt(variance + eps_norm) * gain


def rope_tables(positions, heads):
    half_dim = HEAD_DIM // 2
    inverse = rope_base ** (-2.0 * jnp.arange(half_dim, dtype=jnp.float32) / HEAD_DIM)
    angles = positions.astype(jnp.float32)[:, None] * inverse[None, :]
    cosine, sine = jnp.cos(angles), jnp.sin(angles)
    cosine = jnp.concatenate([cosine, cosine] * heads, axis=1)
    sine = jnp.concatenate([-sine, sine] * heads, axis=1)
    return (cosine, sine)


def half_turned(values):
    width = values.shape[-1]
    half = HEAD_DIM // 2
    lane = lax.broadcasted_iota(jnp.int32, values.shape, values.ndim - 1)
    if width == HEAD_DIM:
        return jnp.concatenate([values[:, half:], values[:, :half]], axis=1)
    ahead = pltpu.roll(values, width - half, axis=1)
    behind = pltpu.roll(values, half, axis=1)
    return jnp.where(lane % HEAD_DIM < half, ahead, behind)


def unit_places(unit_owner, chosen):
    every = jnp.arange(unit_owner.shape[0], dtype=jnp.int32)
    owner = jnp.sum(jnp.where(every == chosen[:, None], unit_owner, 0), axis=1)
    below = (every < chosen[:, None]) & (unit_owner == owner[:, None])
    return owner, jnp.sum(below.astype(jnp.int32), axis=1)


def gated_gelu(upper_proj):
    return jax.nn.gelu(upper_proj[:, :FF_WIDE], approximate=False) * upper_proj[:, FF_WIDE:]


def adam_update(weight, gradient, first_old, second_old, step_rate, weight_decay):
    first_new = beta_one * first_old + (1.0 - beta_one) * gradient
    second_new = beta_two * second_old + (1.0 - beta_two) * gradient * gradient
    first_fix = 1.0 - beta_one**STEP
    second_fix = 1.0 - beta_two**STEP
    adam_step = first_new / first_fix / (jnp.sqrt(second_new / second_fix) + adam_eps)
    return (weight - step_rate * (adam_step + weight_decay * weight), first_new, second_new)


def qkv_kernel(norm_ref, w_ref, cos_ref, sin_ref, out_ref):
    tile = pl.program_id(0)
    turned_tiles = 2 * pl.num_programs(0) // 3
    values = transposed(norm_ref[...], w_ref[...])

    @pl.when(tile < turned_tiles)
    def _():
        out_ref[0] = (values * cos_ref[...] + half_turned(values) * sin_ref[...]).astype(
            out_ref.dtype
        )

    @pl.when(tile >= turned_tiles)
    def _():
        out_ref[0] = values.astype(out_ref.dtype)


def qkv_call(norm_one, w_qkv, cosine, sine):
    rows, width = norm_one.shape
    cols = 256
    tiles = width // cols
    return pl.pallas_call(
        qkv_kernel,
        grid=(3 * width // cols,),
        in_specs=[
            pl.BlockSpec((rows, width), lambda i: (0, 0)),
            pl.BlockSpec((cols, width), lambda i: (i, 0)),
            pl.BlockSpec((rows, cols), lambda i: (0, 0)),
            pl.BlockSpec((rows, cols), lambda i: (0, 0)),
        ],
        out_specs=pl.BlockSpec((1, rows, cols), lambda i: (i // tiles, 0, i % tiles)),
        out_shape=jax.ShapeDtypeStruct((3, rows, width), jnp.bfloat16),
        name="qkv",
    )(norm_one, w_qkv, cosine, sine)


def head_only(values, head):
    width = values.shape[-1]
    if width == HEAD_DIM:
        return values
    lane = lax.broadcasted_iota(jnp.int32, values.shape, 1)
    return jnp.where(lane // HEAD_DIM == head, values, jnp.zeros_like(values))


def attend_step(i, q_ref, k_ref, v_ref, bias, out_ref, wide_ref, lse_ref, chunk):
    width = k_ref.shape[1]
    heads = width // HEAD_DIM
    rows = pl.ds(pl.multiple_of(i * chunk, chunk), chunk)
    query = q_ref[rows, :] * jnp.bfloat16(0.125)
    total = None
    stats = None
    for h in range(heads):
        scores = transposed(query, head_only(k_ref[...], h)) + bias
        top = jnp.max(scores, axis=-1, keepdims=True)
        weights = jnp.exp(scores - top)
        norm = jnp.sum(weights, axis=-1, keepdims=True)
        low = (weights * (1.0 / norm)).astype(jnp.bfloat16)
        part = jnp.dot(low, head_only(v_ref[...], h), preferred_element_type=jnp.float32)
        lse = jnp.broadcast_to(top + jnp.log(norm), (chunk, width))
        total = part if total is None else total + part
        if stats is None:
            stats = lse
        else:
            lane = lax.broadcasted_iota(jnp.int32, lse.shape, 1)
            stats = jnp.where(lane // HEAD_DIM == h, lse, stats)
    out_ref[rows, :] = total.astype(jnp.bfloat16)
    wide_ref[rows, :] = total
    lse_ref[rows, :] = stats


def attend_slot(*args):
    def step(i, _):
        attend_step(i, *args)
        return 0

    lax.fori_loop(0, args[1].shape[0] // args[-1], step, 0)


def turned_back(grad, cos, sin):
    return grad * cos - half_turned(grad) * sin


def attend_back_step(
    i, q_ref, k_ref, v_ref, g_ref, wide_ref, lse_ref, bias, cos, sin, dq_ref, dk_ref, dv_ref, acc_k, acc_v, chunk
):
    seq, width = k_ref.shape
    heads = width // HEAD_DIM
    rows = pl.ds(pl.multiple_of(i * chunk, chunk), chunk)
    query = q_ref[rows, :]
    grad = g_ref[rows, :]
    lse_all = lse_ref[rows, :]
    both = grad.astype(jnp.float32) * wide_ref[rows, :]
    total = None
    for h in range(heads):
        key = head_only(k_ref[...], h)
        lse = lse_all[:, h * HEAD_DIM : h * HEAD_DIM + 1]
        delta = jnp.sum(head_only(both, h), axis=-1, keepdims=True)
        scores = transposed(query * jnp.bfloat16(0.125), key)
        weights = jnp.exp(scores + (bias - lse))
        back = transposed(grad, head_only(v_ref[...], h))
        low = (weights * (back - delta)).astype(jnp.bfloat16)
        part = jnp.dot(low, key, preferred_element_type=jnp.float32)
        total = part if total is None else total + part
        acc_v[...] += leading(weights.astype(jnp.bfloat16), head_only(grad, h))
        acc_k[...] += leading(low, head_only(query, h))
    dq_ref[rows, :] = turned_back(total * 0.125, cos[rows, :], sin[rows, :]).astype(jnp.bfloat16)


def attend_back_end(
    q_ref, k_ref, v_ref, g_ref, wide_ref, lse_ref, bias, cos, sin, dq_ref, dk_ref, dv_ref, acc_k, acc_v, chunk
):
    dk_ref[...] = turned_back(acc_k[...] * 0.125, cos[...], sin[...]).astype(jnp.bfloat16)
    dv_ref[...] = acc_v[...].astype(jnp.bfloat16)


def attend_back_slot(*args):
    acc_k, acc_v, chunk = args[-3:]
    acc_k[...] = jnp.zeros_like(acc_k)
    acc_v[...] = jnp.zeros_like(acc_v)

    def step(i, _):
        attend_back_step(i, *args)
        return 0

    lax.fori_loop(0, args[1].shape[0] // chunk, step, 0)
    attend_back_end(*args)


def attend_kernel(slots, chunk, qkv_ref, bias_ref, out_ref, wide_ref, lse_ref):
    for s in range(slots):
        attend_slot(
            qkv_ref.at[0, s], qkv_ref.at[1, s], qkv_ref.at[2, s], bias_ref[s],
            out_ref.at[s], wide_ref.at[s], lse_ref.at[s], chunk,
        )


def attend_call(qkv, bias):
    _, slots, seq, width = qkv.shape
    chunk = 256
    return pl.pallas_call(
        functools.partial(attend_kernel, slots, chunk),
        out_shape=(
            jax.ShapeDtypeStruct((slots, seq, width), jnp.bfloat16),
            jax.ShapeDtypeStruct((slots, seq, width), jnp.float32),
            jax.ShapeDtypeStruct((slots, seq, width), jnp.float32),
        ),
        compiler_params=pltpu.CompilerParams(vmem_limit_bytes=VMEM_BYTES),
        name="attend",
    )(qkv, bias)


def attend_back_kernel(slots, chunk, qkv_ref, g_ref, wide_ref, lse_ref, bias_ref, cos_ref, sin_ref, out_ref, acc_k, acc_v):
    for s in range(slots):
        attend_back_slot(
            qkv_ref.at[0, s], qkv_ref.at[1, s], qkv_ref.at[2, s], g_ref.at[s],
            wide_ref.at[s], lse_ref.at[s], bias_ref[s], cos_ref, sin_ref,
            out_ref.at[0, s], out_ref.at[1, s], out_ref.at[2, s], acc_k, acc_v, chunk,
        )


def attend_back_call(qkv, grad_heads, wide, lse, bias, cosine, sine):
    _, slots, seq, width = qkv.shape
    chunk = 256
    return pl.pallas_call(
        functools.partial(attend_back_kernel, slots, chunk),
        out_shape=jax.ShapeDtypeStruct(qkv.shape, jnp.bfloat16),
        scratch_shapes=[pltpu.VMEM((seq, width), jnp.float32)] * 2,
        compiler_params=pltpu.CompilerParams(vmem_limit_bytes=VMEM_BYTES),
        name="attend_back",
    )(qkv, grad_heads, wide, lse, bias, cosine, sine)


def adam_kernel(per, unit_ref, a_ref, b_ref, *refs):
    grads = (refs[:per], refs[per : 2 * per])
    master, first, second, new_master, new_first, new_second = refs[2 * per :]
    for j in range(per):
        slot = pl.program_id(0) * per + j
        unit = unit_ref[slot]
        grad = jnp.where(unit == 0, grads[0][j][0], grads[1][j][0]).astype(jnp.float32)
        grad = jnp.where(unit >= 0, grad, 0.0)
        weight, one, two = adam_update(
            master[j], grad, first[j], second[j], rate_matrix, decay_matrix
        )
        new_master[j] = weight
        new_first[j] = one
        new_second[j] = two


def adam_call(kind, at_a, at_b, grads_a, grads_b, master, first, second):
    capacity, rows, width = master.shape
    per = max(p for p in range(1, 8) if capacity % p == 0)

    def unit_spec(j, chunk):
        return pl.BlockSpec(
            (1, rows, width), lambda i, kind, *at: (at[chunk][i * per + j], 0, 0)
        )

    slot_spec = pl.BlockSpec((per, rows, width), lambda i, kind, *at: (i, 0, 0))
    return pl.pallas_call(
        functools.partial(adam_kernel, per),
        grid_spec=pltpu.PrefetchScalarGridSpec(
            num_scalar_prefetch=3,
            grid=(capacity // per,),
            in_specs=[unit_spec(j, c) for c in range(2) for j in range(per)] + [slot_spec] * 3,
            out_specs=[slot_spec] * 3,
        ),
        out_shape=[jax.ShapeDtypeStruct(master.shape, jnp.float32)] * 3,
        compiler_params=pltpu.CompilerParams(vmem_limit_bytes=VMEM_BYTES),
        name="adamw",
    )(kind, at_a, at_b, *([grads_a] * per), *([grads_b] * per), master, first, second)


def pick_kernel(part_ref, master_ref, out_ref, got, sems):
    count, rows = got.shape[:2]

    def at(p):
        return pl.ds(pl.multiple_of(p * rows, rows), rows)

    def copy(p):
        return pltpu.make_async_copy(master_ref.at[part_ref[p]], got.at[p], sems.at[p])

    def start(p, _):
        @pl.when(part_ref[p] >= 0)
        def _():
            copy(p).start()

        return 0

    def end(p, _):
        @pl.when(part_ref[p] >= 0)
        def _():
            copy(p).wait()
            out_ref[at(p), :] = got[p].astype(out_ref.dtype)

        @pl.when(part_ref[p] < 0)
        def _():
            out_ref[at(p), :] = jnp.zeros((rows, out_ref.shape[1]), out_ref.dtype)

        return 0

    lax.fori_loop(0, count, start, 0)
    lax.fori_loop(0, count, end, 0)


def pick_call(part, parts):
    shape = (part.shape[0],) + parts.shape[1:]
    flat = (shape[0] * shape[1], shape[2])
    return pl.pallas_call(
        pick_kernel,
        grid_spec=pltpu.PrefetchScalarGridSpec(
            num_scalar_prefetch=1,
            grid=(1,),
            in_specs=[pl.BlockSpec(memory_space=pl.ANY)],
            out_specs=pl.BlockSpec(flat, lambda i, part: (0, 0)),
            scratch_shapes=[pltpu.VMEM(shape, parts.dtype), DMA((part.shape[0],))],
        ),
        out_shape=jax.ShapeDtypeStruct(flat, jnp.bfloat16),
        compiler_params=pltpu.CompilerParams(vmem_limit_bytes=VMEM_BYTES),
        name="pick",
    )(part, parts)


def place():
    ctx, shard = lax.axis_index("ctx"), lax.axis_index("shard")
    return ctx // 2, ctx % 2, shard // 2, shard % 2


def device_at(z, y, x, core):
    return (z * 2 + y, x * 2 + core)


def piece_at(zb, c, h, a, b):
    return (((zb * 2 + c) * 2 + h) * 2 + a) * 2 + b


def remote(src, dst, send, recv, device):
    return pltpu.make_async_remote_copy(
        src_ref=src, dst_ref=dst, send_sem=send, recv_sem=recv, device_id=device, device_id_type=MESH
    )


def greet(devices):
    barrier = pltpu.get_barrier_semaphore()
    for device in devices:
        pl.semaphore_signal(barrier, inc=1, device_id=device, device_id_type=MESH)
    pl.semaphore_wait(barrier, len(devices))


def line_neighbours():
    z, y, x, core = place()
    return [device_at(z, y, 1 - x, core), device_at(z, 1 - y, x, core), device_at(z, y, x, 1 - core)] + [
        device_at((z + d) % 4, y, x, core) for d in (1, 2, 3)
    ]


def rows_at(ref, piece, count, rows):
    return ref.at[pl.ds(pl.multiple_of(piece * rows, 16), count * rows)]


GATHER_SEMS = [DMA((2,))] + [DMA((2, 4, 2))] * 2 + [DMA((2, 4))] * 2 + [DMA((2, 4, 2))] * 2 + [DMA((4,))] * 2


class Gather:
    def __init__(self, own, buf, rows, sems):
        self.own, self.buf, self.rows = own, buf, rows
        self.lsem, self.zs, self.zr, self.fs, self.fr, self.ts, self.tr, self.ss, self.sr = sems
        self.z, self.y, self.x, self.core = z, y, x, core = place()
        self.xn = device_at(z, y, 1 - x, core)
        self.yn = device_at(z, 1 - y, x, core)
        self.sib = device_at(z, y, x, 1 - core)

    def side(self, h):
        return (self.y, self.x) if h == 0 else (self.x, self.y)

    def near(self, h):
        return (self.xn, self.yn) if h == 0 else (self.yn, self.xn)

    def piece(self, zb, h, a, b):
        return rows_at(self.buf, piece_at(zb, self.core, h, a, b), 1, self.rows)

    def keep(self, h):
        return pltpu.make_async_copy(self.own(h), self.piece(self.z, h, *self.side(h)), self.lsem.at[h])

    def up(self, d, h, step, src=None):
        ref = self.piece(self.z + d, h, *self.side(h))
        k, hop = (0, -d) if step > 0 else (1, d)
        return remote(
            ref if src is None else src,
            ref,
            self.zs.at[k, hop, h],
            self.zr.at[k, hop, h],
            device_at(self.z + step, self.y, self.x, self.core),
        )

    def got(self, d, h):
        ref = self.piece(self.z + d, h, *self.side(h))
        k, hop = (0 if d < 0 else 1), abs(d) - 1
        remote(ref, ref, self.zs.at[k, hop, h], self.zr.at[k, hop, h], self.xn).wait_recv()

    def first(self, zb, h, mine, src=None):
        a, b = self.side(h)
        ref = self.piece(zb, h, a, b if mine else 1 - b)
        return remote(
            ref if src is None else src, ref, self.fs.at[h, zb], self.fr.at[h, zb], self.near(h)[0]
        )

    def second(self, zb, h, j, mine, src=None):
        a, b = self.side(h)
        ref = self.piece(zb, h, a if mine else 1 - a, b if j == 0 else 1 - b)
        return remote(
            ref if src is None else src, ref, self.ts.at[h, zb, j], self.tr.at[h, zb, j], self.near(h)[1]
        )

    def whole(self, zb, c):
        ref = rows_at(self.buf, (zb * 2 + c) * 8, 8, self.rows)
        return remote(ref, ref, self.ss.at[zb], self.sr.at[zb], self.sib)

    def start(self):
        for h in range(2):
            self.keep(h).start()
        for h in range(2):

            @pl.when(self.z < 3)
            def _():
                self.up(0, h, 1, self.own(h)).start()

            @pl.when(self.z > 0)
            def _():
                self.up(0, h, -1, self.own(h)).start()

            self.first(self.z, h, True, self.own(h)).start()
        for h in range(2):
            self.second(self.z, h, 0, True, self.own(h)).start()
        for h in range(2):
            self.keep(h).wait()

    def there(self, d, work):
        if d == 0:
            work()
        else:
            pl.when((self.z + d >= 0) & (self.z + d < 4))(work)

    def line(self, d):
        def work():
            zb = self.z + d
            for h in range(2):
                self.got(d, h)
                if d < 0:

                    @pl.when(self.z < 3)
                    def _():
                        self.up(d, h, 1).start()
                else:

                    @pl.when(self.z > 0)
                    def _():
                        self.up(d, h, -1).start()

                self.first(zb, h, True).start()
            for h in range(2):
                self.second(zb, h, 0, True).start()

        self.there(d, work)

    def cross(self, d):
        def work():
            zb = self.z + d
            for h in range(2):
                self.first(zb, h, False).wait_recv()
                self.second(zb, h, 1, True).start()

        self.there(d, work)

    def close(self, d):
        def work():
            zb = self.z + d
            for h in range(2):
                for j in range(2):
                    self.second(zb, h, j, False).wait_recv()
            self.whole(zb, self.core).start()

        self.there(d, work)

    def finish(self, take=True):
        for h in range(2):
            for d in range(4):

                @pl.when((self.z - d >= 0) & (self.z < 3))
                def _():
                    self.up(-d, h, 1).wait_send()

                @pl.when((self.z + d < 4) & (self.z > 0))
                def _():
                    self.up(d, h, -1).wait_send()

        for zb in range(4):
            for h in range(2):
                self.first(zb, h, True).wait_send()
                for j in range(2):
                    self.second(zb, h, j, True).wait_send()
            self.whole(zb, self.core).wait_send()
            if take:
                self.whole(zb, 1 - self.core).wait_recv()


REDUCE_REFS = 10


def reduce_scratch(rows, width):
    def buf(n):
        return pltpu.VMEM((n * rows, width), jnp.bfloat16)

    return (
        [buf(32), buf(16), buf(8), buf(10)]
        + [DMA((4, 2, 2))] * 2
        + [DMA((4, 2))] * 3
        + [DMA((5, 2))]
    )


class Reduce:
    def __init__(self, rows, refs):
        self.acc, self.got1, self.got2, self.got3 = refs[:4]
        self.s1, self.r1, self.s2, self.r2, self.s3, self.r3 = refs[4:]
        self.rows = rows
        self.z, self.y, self.x, self.core = z, y, x, core = place()
        self.xn = device_at(z, y, 1 - x, core)
        self.yn = device_at(z, 1 - y, x, core)
        self.sib = device_at(z, y, x, 1 - core)

    def zb(self, t):
        s = self.z // 2
        return (3 - 3 * s, 2 - s, 1 - self.z + 4 * s, self.z)[t]

    def base(self, zb):
        return zb * 8

    def side(self, h):
        return (self.y, self.x) if h == 0 else (self.x, self.y)

    def near(self, h):
        return (self.yn, self.xn) if h == 0 else (self.xn, self.yn)

    def send1(self, t, h, q):
        zb = self.zb(t)
        a, b = self.side(h)
        b = 1 - b if q == 0 else b
        return remote(
            rows_at(self.acc, self.base(zb) + h * 4 + (1 - a) * 2 + b, 1, self.rows),
            rows_at(self.got1, zb * 4 + h * 2 + b, 1, self.rows),
            self.s1.at[zb, h, q],
            self.r1.at[zb, h, q],
            self.near(h)[0],
        )

    def send2(self, t, h):
        zb = self.zb(t)
        a, b = self.side(h)
        return remote(
            rows_at(self.acc, self.base(zb) + h * 4 + a * 2 + 1 - b, 1, self.rows),
            rows_at(self.got2, zb * 2 + h, 1, self.rows),
            self.s2.at[zb, h],
            self.r2.at[zb, h],
            self.near(h)[1],
        )

    def send3(self, t, h, up):
        zb = self.zb(t)
        a, b = self.side(h)
        slot = zb if up else zb + (4 - zb) * (1 - (self.z - 1 - zb + 2) // 3)
        return remote(
            rows_at(self.acc, self.base(zb) + h * 4 + a * 2 + b, 1, self.rows),
            rows_at(self.got3, slot * 2 + h, 1, self.rows),
            self.s3.at[t, h],
            self.r3.at[slot, h],
            device_at(self.z + (1 if up else -1), self.y, self.x, self.core),
        )

    def come3(self, slot, h):
        ref = rows_at(self.got3, slot * 2 + h, 1, self.rows)
        remote(ref, ref, self.s3.at[0, h], self.r3.at[slot, h], self.xn).wait_recv()
        a, b = self.side(h)
        zb = self.z if isinstance(slot, int) else slot
        self.add(self.base(zb) + h * 4 + a * 2 + b, self.got3, slot * 2 + h, 1)

    def add(self, at, ref, start, count):
        step = 48

        def body(i, _):
            to = pl.ds(pl.multiple_of(at * self.rows + i * step, 16), step)
            given = pl.ds(pl.multiple_of(start * self.rows + i * step, 16), step)
            self.acc[to, :] = self.acc[to, :] + ref[given, :]
            return 0

        lax.fori_loop(0, count * self.rows // step, body, 0)

    def go1(self, t, q):
        for h in range(2):
            self.send1(t, h, q).start()

    def one(self, t, q):
        zb = self.zb(t)
        for h in range(2):
            a, b = self.side(h)
            b = 1 - b if q == 0 else b
            self.send1(t, h, q).wait_recv()
            self.add(self.base(zb) + h * 4 + a * 2 + b, self.got1, zb * 4 + h * 2 + b, 1)
            if q == 0:
                self.send2(t, h).start()

    def two(self, t):
        zb = self.zb(t)
        for h in range(2):
            a, b = self.side(h)
            self.send2(t, h).wait_recv()
            self.add(self.base(zb) + h * 4 + a * 2 + b, self.got2, zb * 2 + h, 1)

    def tri(self, t):
        zb = self.zb(t)
        z = self.z
        for h in range(2):

            @pl.when(((zb > z) & (z > 0)) | ((zb < z) & (z < 3)))
            def _():
                self.come3(zb, h)

            @pl.when(zb > z)
            def _():
                self.send3(t, h, True).start()

            @pl.when(zb < z)
            def _():
                self.send3(t, h, False).start()

    def three(self):
        for h in range(2):

            @pl.when(self.z > 0)
            def _():
                self.come3(self.z, h)

            @pl.when(self.z < 3)
            def _():
                self.come3(4, h)

    def own(self, h):
        a, b = self.side(h)
        return rows_at(self.acc, self.base(self.z) + h * 4 + a * 2 + b, 1, self.rows)

    def finish(self):
        for t in range(4):
            for h in range(2):
                for q in range(2):
                    self.send1(t, h, q).wait_send()
                self.send2(t, h).wait_send()
                if t < 3:
                    ref = rows_at(self.got3, h, 1, self.rows)
                    remote(ref, ref, self.s3.at[t, h], self.r3.at[0, h], self.xn).wait_send()


def front_kernel(
    given_ref, norm_ref, cos_ref, sin_ref, bias_ref,
    oa_ref, ob_ref, heads, wide_ref, lse_ref, mixed_ref,
    stack, rows, seen, low, mixed, got_a, got_b, new_a, new_b, own_a, own_b, send, recv, csem, ql, qsend, qrecv, ml, msend, mrecv, *sems
):
    n = 8
    z, y, x, core = place()
    ctx, shard = lax.axis_index("ctx"), lax.axis_index("shard")
    m = len(GATHER_SEMS)
    rows_a, rows_b = own_a.shape[0] // 2, own_b.shape[0] // 2
    ga = Gather(lambda h: rows_at(own_a, h, 1, rows_a), stack, rows_a, sems[:m])
    gb = Gather(lambda h: rows_at(own_b, h, 1, rows_b), ob_ref, rows_b, sems[m:])
    _, slots, block_len, width = rows.shape
    seq, my_width = seen.shape[2:]
    greet([ga.xn, ga.sib] + [(lax.rem(ctx + d, n), shard) for d in range(1, n)])
    jobs = ((0, got_a, new_a, own_a), (8 * rows_a, got_b, new_b, own_b))

    def share(i, c, xb):
        start, got, new, own = jobs[i]
        size = own.shape[0]
        at = start + c * 2 * size
        if xb is None:
            return given_ref.at[pl.ds(pl.multiple_of(at, 16), 2 * size)]
        return given_ref[pl.ds(pl.multiple_of(at + xb * size, 16), size), :]

    def held(i, xb):
        size = jobs[i][3].shape[0]
        return pl.ds(pl.multiple_of(xb * size, 16), size)

    def to_core(i):
        return remote(share(i, 1 - core, None), jobs[i][1], send.at[i], recv.at[i], ga.sib)

    def to_x(i):
        start, got, new, own = jobs[i]
        return remote(got.at[held(i, 1 - x)], new, send.at[2 + i], recv.at[2 + i], ga.xn)

    def spread(i):
        start, got, new, own = jobs[i]
        to_core(i).wait_recv()
        got[held(i, 1 - x), :] = got[held(i, 1 - x), :] + share(i, core, 1 - x)
        to_x(i).start()
        own[...] = got[held(i, x), :] + share(i, core, x)

    def cross(i):
        start, got, new, own = jobs[i]
        to_x(i).wait_recv()
        own[...] = own[...] + new[...]

    def peer(d):
        return lax.rem(ctx + d, n)

    def lanes(owner):
        return pl.ds(pl.multiple_of(owner * my_width, my_width), my_width)

    def block(owner):
        return pl.ds(pl.multiple_of(owner * block_len, block_len), block_len)

    def head_copy(j, owner):
        return remote(
            rows.at[j, :, :, lanes(owner)], seen.at[j, :, block(ctx), :], qsend.at[j, owner], qrecv.at[j, ctx], (owner, shard)
        )

    def head_own(j):
        return pltpu.make_async_copy(rows.at[j, :, :, lanes(ctx)], seen.at[j, :, block(ctx), :], ql.at[j])

    def mixed_copy(s, d):
        return remote(
            low.at[s, block(peer(d)), :], mixed.at[s, :, lanes(ctx)], msend.at[s, d], mrecv.at[s, d], (peer(d), shard)
        )

    def mixed_own(s):
        return pltpu.make_async_copy(low.at[s, block(ctx), :], mixed.at[s, :, lanes(ctx)], ml.at[s])

    cols = 256
    tiles = width // cols
    per_z = 16 * rows_a // cols

    def region(i):
        s = z // 2
        t = z % 2
        return (
            z,
            (1 - t) * (1 - s) + s * (1 + t),
            2 * (1 - s) + s * (3 - 2 * t),
            3 * (1 - s),
        )[i]

    def qkv(i):
        zb = region(i)
        ga.whole(zb, 1 - core).wait_recv()

        def tile_step(k, _):
            tile = zb * per_z + k
            j, t = tile // tiles, tile % tiles
            at = pl.ds(pl.multiple_of(t * cols, cols), cols)
            weight = stack[pl.ds(pl.multiple_of(tile * cols, cols), cols), :]
            values = transposed(norm_ref[...], weight)
            turn = (j < 2).astype(jnp.float32)
            cos = cos_ref[...] * turn + (1.0 - turn)
            values = values * cos + half_turned(values) * (sin_ref[...] * turn)
            rows[j, :, :, at] = values.astype(jnp.bfloat16).reshape(slots, block_len, cols)
            for q in range(cols // my_width):
                owner = t * (cols // my_width) + q

                @pl.when(owner == ctx)
                def _():
                    head_own(j).start()

                @pl.when(owner != ctx)
                def _():
                    head_copy(j, owner).start()

            return 0

        lax.fori_loop(0, per_z, tile_step, 0)

    def heads_wait():
        for j in range(3):
            head_own(j).wait()
            for d in range(1, n):
                ref = seen.at[j, :, block(peer(d)), :]
                remote(ref, ref, qsend.at[j, peer(d)], qrecv.at[j, peer(d)], (peer(d), shard)).wait_recv()

    def mixed_wait():
        for s in range(slots):
            mixed_own(s).wait()
            for d in range(1, n):
                mixed_copy(s, d).wait_recv()

    for i in range(2):
        to_core(i).start()
    spread(0)
    spread(1)
    cross(0)
    ga.start()
    ga.line(-1), ga.line(1)
    ga.cross(0)
    ga.line(-2), ga.line(2)
    ga.cross(-1), ga.cross(1)
    ga.close(0)
    cross(1)
    ga.line(-3), ga.line(3)
    ga.cross(-2), ga.cross(2)
    qkv(0)
    ga.close(-1), ga.close(1)
    gb.start()
    ga.cross(-3), ga.cross(3)
    qkv(1)
    ga.close(-2), ga.close(2)
    gb.line(-1), gb.line(1)
    qkv(2)
    ga.close(-3), ga.close(3)
    gb.cross(0)
    qkv(3)
    gb.line(-2), gb.line(2)
    heads_wait()
    keep_a = pltpu.make_async_copy(stack, oa_ref, csem.at[0])
    keep_heads = pltpu.make_async_copy(seen, heads, csem.at[1])
    keep_a.start()
    keep_heads.start()
    chunk = 256
    per_slot = seq // chunk

    def attend_at(i, _):
        s, c = i // per_slot, i % per_slot
        attend_step(
            c, seen.at[0, s], seen.at[1, s], seen.at[2, s], bias_ref[s], low.at[s], wide_ref.at[s], lse_ref.at[s], chunk
        )

        @pl.when(c == per_slot - 1)
        def _():
            mixed_own(s).start()
            for d in range(1, n):
                mixed_copy(s, d).start()

        @pl.when(i == 0)
        def _():
            gb.cross(-1), gb.cross(1)

        @pl.when(i == 3)
        def _():
            gb.close(0)

        @pl.when(i == 5)
        def _():
            gb.line(-3), gb.line(3)

        return 0

    lax.fori_loop(0, slots * per_slot, attend_at, 0)
    gb.cross(-2), gb.cross(2)
    gb.close(-1), gb.close(1)
    gb.cross(-3), gb.cross(3)
    gb.close(-2), gb.close(2)
    gb.close(-3), gb.close(3)
    mixed_wait()
    mixed_ref[...] = mixed[...]
    keep_a.wait()
    keep_heads.wait()
    for i in range(2):
        to_core(i).wait_send()
        to_x(i).wait_send()
    for d in range(1, n):
        for j in range(3):
            head_copy(j, peer(d)).wait_send()
        for s in range(slots):
            mixed_copy(s, d).wait_send()
    ga.finish(False)
    gb.finish()


def front_call(given, rows_a, rows_b, norm_one, cosine, sine, bias, slots, block_len, collective_id):
    vmem = pl.BlockSpec(memory_space=pltpu.VMEM)
    any_ = pl.BlockSpec(memory_space=pl.ANY)
    low = jnp.bfloat16
    width = norm_one.shape[1]
    seq = block_len * 8
    my_width = width // 8
    stack_a, stack_b = (jax.ShapeDtypeStruct((64 * r, width), low) for r in (rows_a, rows_b))
    scratch = [
        pltpu.VMEM(stack_a.shape, low),
        pltpu.VMEM((3, slots, block_len, width), low),
        pltpu.VMEM((3, slots, seq, my_width), low),
        pltpu.VMEM((slots, seq, my_width), low),
        pltpu.VMEM((slots, block_len, width), low),
    ]
    for pieces in (4, 2, 2):
        for r in (rows_a, rows_b):
            scratch.append(pltpu.VMEM((pieces * r, width), low))
    return pl.pallas_call(
        front_kernel,
        out_shape=(
            stack_a,
            stack_b,
            jax.ShapeDtypeStruct((3, slots, seq, my_width), low),
            jax.ShapeDtypeStruct((slots, seq, my_width), jnp.float32),
            jax.ShapeDtypeStruct((slots, seq, my_width), jnp.float32),
            jax.ShapeDtypeStruct((slots, block_len, width), low),
        ),
        in_specs=[vmem] * 5,
        out_specs=(any_, any_, any_, vmem, vmem, vmem),
        scratch_shapes=scratch
        + [DMA((4,)), DMA((4,)), DMA((2,)), DMA((3,)), DMA((3, 8)), DMA((3, 8)), DMA((slots,)), DMA((slots, 8)), DMA((slots, 8))]
        + GATHER_SEMS * 2,
        compiler_params=pltpu.CompilerParams(
            collective_id=collective_id, has_side_effects=True, vmem_limit_bytes=VMEM_BYTES
        ),
        name="spread_and_attend",
    )(given, norm_one, cosine, sine, bias)


GAIN_SEMS = [DMA((6,)), DMA((6,))]


class GainSum:
    def __init__(self, ref, got, line, sems):
        self.ref, self.got, self.all = ref, got, line
        self.send, self.recv = sems
        self.z, self.y, self.x, self.core = place()

    def step(self, i):
        z, y, x, core = self.z, self.y, self.x, self.core
        to = (device_at(z, y, x, 1 - core), device_at(z, y, 1 - x, core), device_at(z, 1 - y, x, core))[i]
        return remote(self.ref, self.got.at[i], self.send.at[i], self.recv.at[i], to)

    def far(self, d):
        to = device_at((self.z + d) % 4, self.y, self.x, self.core)
        return remote(self.ref, self.all.at[self.z], self.send.at[2 + d], self.recv.at[2 + d], to)

    def begin(self, i):
        self.step(i).start()

    def end(self, i):
        self.step(i).wait()
        self.ref[...] = self.ref[...] + self.got[i]

    def begin_far(self):
        for d in (1, 2, 3):
            self.far(d).start()
        self.all[self.z] = self.ref[...]

    def end_far(self, out):
        for d in (1, 2, 3):
            self.far(d).wait()
        total = self.all[0]
        for i in range(1, 4):
            total = total + self.all[i]
        out[...] = total


def back_kernel(
    g_ref, qkv_ref, wide_ref, lse_ref, bias_ref, cos_ref, sin_ref, norm_ref, tokens_ref, gains_ref, middle_ref, gain_ref,
    left_ref, right_ref, w_ref,
    oa_ref, ob_ref, og_ref, tok_ref,
    left_got, right_got, norm_got, rows_got, weight_ref, xsend, xrecv, heads, grad, rows, acc_k, acc_v, dnorm, gain, gain_got, gain_all, wsem, gl, gsend, grecv, dl, dsend, drecv, *refs
):
    n = 8
    slots, block_len, width = g_ref.shape
    seq, my_width = qkv_ref.shape[2:]
    chunk = 256
    per_slot = seq // chunk
    m = len(GATHER_SEMS)
    rows_a, rows_b = oa_ref.shape[0] // 64, ob_ref.shape[0] // 64
    ra = Reduce(rows_a, refs[:REDUCE_REFS])
    rb = Reduce(rows_b, refs[REDUCE_REFS : 2 * REDUCE_REFS])
    refs = refs[2 * REDUCE_REFS :]
    ga = Gather(ra.own, oa_ref, rows_a, refs[:m])
    gb = Gather(rb.own, ob_ref, rows_b, refs[m : 2 * m])
    gs = GainSum(gain, gain_got, gain_all, refs[2 * m :])
    z, y, x, core = place()
    ctx, shard = lax.axis_index("ctx"), lax.axis_index("shard")
    greet([ra.xn, ra.sib] + [(lax.rem(ctx + d, n), shard) for d in range(1, n)])

    def peer(d):
        return lax.rem(ctx + d, n)

    def lanes(owner):
        return pl.ds(pl.multiple_of(owner * my_width, my_width), my_width)

    def block(owner):
        return pl.ds(pl.multiple_of(owner * block_len, block_len), block_len)

    def go_copy(d):
        return remote(
            g_ref.at[:, :, lanes(peer(d))], grad.at[:, block(ctx), :], gsend.at[d], grecv.at[d], (peer(d), shard)
        )

    def back_copy(s, d):
        return remote(
            heads.at[:, s, block(peer(d)), :], rows.at[:, s, :, lanes(ctx)], dsend.at[s, d], drecv.at[s, d], (peer(d), shard)
        )

    def back_own(s):
        return pltpu.make_async_copy(heads.at[:, s, block(ctx), :], rows.at[:, s, :, lanes(ctx)], dl.at[s])

    go_own = pltpu.make_async_copy(g_ref.at[:, :, lanes(ctx)], grad.at[:, block(ctx), :], gl)
    w_copy = pltpu.make_async_copy(w_ref, weight_ref, wsem)
    cut = 128
    rows_all = slots * block_len

    def to_sib(src, dst, i):
        return remote(src, dst, xsend.at[i], xrecv.at[i], ra.sib)

    def left_copy(t, c):
        lane = pl.ds(pl.multiple_of((rb.zb(t) * 2 + c) * 8 * rows_b, cut), 8 * rows_b)
        return to_sib(left_ref.at[:, lane], left_got.at[rb.zb(t)], t)

    right_copy = to_sib(right_ref, right_got, 4)
    norm_copy = to_sib(norm_ref, norm_got, 5)
    rows_copy = to_sib(rows, rows_got, 6)

    def given():
        left_copy(0, 1 - core).start()
        right_copy.start()
        for t in range(1, 4):
            left_copy(t, 1 - core).start()
        norm_copy.start()
        right_copy.wait_recv()

    def fill(t):
        zb = rb.zb(t)
        left_copy(t, core).wait_recv()
        count = 8 * rows_b // cut

        def step(i, _):
            g = (zb * 2 + core) * count + i
            kind = (g >= width // cut).astype(jnp.int32) + (g >= (width + 2 * FF_WIDE) // cut).astype(jnp.int32)
            mine = left_ref[:, pl.ds(pl.multiple_of(g * cut, cut), cut)]
            other = left_got[zb, :, pl.ds(pl.multiple_of(i * cut, cut), cut)]
            total = leading(mine, right_ref[kind]) + leading(other, right_got[kind])
            at = pl.ds(pl.multiple_of(zb * 8 * rows_b + i * cut, cut), cut)
            rb.acc[at, :] = total.astype(jnp.bfloat16)
            return 0

        lax.fori_loop(0, count, step, 0)
    cols = 256
    tiles = width // cols

    def rows_wait():
        for s in range(slots):
            back_own(s).wait()
            for d in range(1, n):
                back_copy(s, d).wait_recv()
        rows_copy.start()
        norm_copy.wait_recv()
        rows_copy.wait_recv()

    def weight(t):
        zb = ra.zb(t)
        count = 8 * rows_a // cut

        def step(i, _):
            g = (zb * 2 + core) * count + i
            j = g * cut // width
            lane = pl.ds(pl.multiple_of(g * cut - j * width, cut), cut)
            total = leading(rows[j, :, :, lane].reshape(rows_all, cut), norm_ref[...])
            total += leading(rows_got[j, :, :, lane].reshape(rows_all, cut), norm_got[...])
            at = pl.ds(pl.multiple_of(zb * 8 * rows_a + i * cut, cut), cut)
            ra.acc[at, :] = total.astype(jnp.bfloat16)
            return 0

        lax.fori_loop(0, count, step, 0)

    def norm_step(t, _):
        at = pl.ds(pl.multiple_of(t * cols, cols), cols)
        total = None
        for j in range(3):
            left = rows[j].reshape(slots * block_len, width)
            right = weight_ref[pl.ds(j * width, width), at]
            part = jnp.dot(left, right, preferred_element_type=jnp.float32)
            total = part if total is None else total + part
        dnorm[:, at] = total
        return 0

    some = 64
    def token_step(i, _):
        at = pl.ds(pl.multiple_of(i * some, some), some)
        values = tokens_ref[at, :].astype(jnp.float32)
        mean = jnp.mean(values, axis=-1, keepdims=True)
        centred = values - mean
        scale = lax.rsqrt(jnp.mean(centred * centred, axis=-1, keepdims=True) + eps_norm)
        unit = centred * scale
        given = dnorm[at, :]
        inner = given * gains_ref[0:1, :]
        inner_mean = jnp.mean(inner, axis=-1, keepdims=True)
        along = jnp.mean(inner * unit, axis=-1, keepdims=True)
        grads = middle_ref[at, :] + scale * (inner - inner_mean - unit * along)
        tok_ref[at, :] = grads.astype(jnp.bfloat16)
        gain[0:1, :] += jnp.sum(given * unit, axis=0, keepdims=True)
        return 0

    def token():
        w_copy.wait()
        lax.fori_loop(0, tiles, norm_step, 0)
        gain[...] = gain_ref[...]
        lax.fori_loop(0, slots * block_len // some, token_step, 0)
        gs.begin(0)

    for d in range(1, n):
        go_copy(d).start()
    go_own.start()
    given()
    fill(0)
    rb.go1(0, 0)
    rb.go1(0, 1)
    fill(1)
    fill(2)
    fill(3)
    w_copy.start()
    go_own.wait()
    for d in range(1, n):
        go_copy(d).wait_recv()

    def attend_step(i, _):
        s, c = i // per_slot, i % per_slot
        slot = (
            qkv_ref.at[0, s], qkv_ref.at[1, s], qkv_ref.at[2, s], grad.at[s], wide_ref.at[s], lse_ref.at[s], bias_ref[s],
            cos_ref, sin_ref, heads.at[0, s], heads.at[1, s], heads.at[2, s], acc_k, acc_v, chunk,
        )

        @pl.when(c == 0)
        def _():
            acc_k[...] = jnp.zeros_like(acc_k)
            acc_v[...] = jnp.zeros_like(acc_v)

        attend_back_step(c, *slot)

        @pl.when(c == per_slot - 1)
        def _():
            attend_back_end(*slot)
            back_own(s).start()
            for d in range(1, n):
                back_copy(s, d).start()

        @pl.when(i == 1)
        def _():
            rb.one(0, 0)
            rb.go1(1, 0)
            rb.one(0, 1)
            rb.go1(1, 1)

        return 0

    lax.fori_loop(0, slots * per_slot, attend_step, 0)
    rb.two(0)
    rb.one(1, 0)
    rb.go1(2, 0)
    rb.one(1, 1)
    rb.go1(2, 1)
    rb.tri(0)
    rb.two(1)
    rb.one(2, 0)
    rb.go1(3, 0)
    rb.one(2, 1)
    rb.go1(3, 1)
    rb.tri(1)
    rb.two(2)
    rb.one(3, 0)
    rb.one(3, 1)
    rb.tri(2)
    rows_wait()
    weight(0)
    ra.go1(0, 0)
    ra.go1(0, 1)
    weight(1)
    ra.go1(1, 0)
    ra.go1(1, 1)
    rb.two(3)
    weight(2)
    ra.go1(2, 0)
    ra.go1(2, 1)
    weight(3)
    ra.go1(3, 0)
    ra.go1(3, 1)
    ra.one(0, 0)
    ra.one(0, 1)
    rb.three()
    gb.start()
    token()
    ra.one(1, 0)
    ra.one(1, 1)
    ra.two(0)
    ra.one(2, 0)
    ra.one(2, 1)
    ra.tri(0)
    ra.two(1)
    gb.line(-1), gb.line(1)
    ra.one(3, 0)
    ra.one(3, 1)
    ra.tri(1)
    ra.two(2)
    gb.cross(0)
    gs.end(0)
    gs.begin(1)
    ra.tri(2)
    ra.two(3)
    gb.line(-2), gb.line(2)
    ra.three()
    ga.start()
    gb.cross(-1), gb.cross(1)
    gs.end(1)
    gs.begin(2)
    gb.close(0)
    gb.line(-3), gb.line(3)
    ga.line(-1), ga.line(1)
    gb.cross(-2), gb.cross(2)
    gs.end(2)
    gs.begin_far()
    ga.cross(0)
    gb.close(-1), gb.close(1)
    ga.line(-2), ga.line(2)
    gb.cross(-3), gb.cross(3)
    ga.cross(-1), ga.cross(1)
    ga.close(0)
    gb.close(-2), gb.close(2)
    ga.line(-3), ga.line(3)
    ga.cross(-2), ga.cross(2)
    ga.close(-1), ga.close(1)
    gb.close(-3), gb.close(3)
    ga.cross(-3), ga.cross(3)
    ga.close(-2), ga.close(2)
    ga.close(-3), ga.close(3)
    gs.end_far(og_ref)
    for d in range(1, n):
        go_copy(d).wait_send()
        for s in range(slots):
            back_copy(s, d).wait_send()
    for t in range(4):
        left_copy(t, 1 - core).wait_send()
    for copy in (right_copy, norm_copy, rows_copy):
        copy.wait_send()
    ra.finish(), rb.finish(), ga.finish(), gb.finish()


def back_call(
    grad_rows, qkv_heads, wide, lse, bias, cosine, sine, norm_one, tokens, gains, grad_middle, gain_part, left, right, w_qkv, collective_id
):
    any_ = pl.BlockSpec(memory_space=pl.ANY)
    vmem = pl.BlockSpec(memory_space=pltpu.VMEM)
    low = jnp.bfloat16
    slots, block_len, width = grad_rows.shape
    seq, my_width = qkv_heads.shape[2:]
    rows_all = slots * block_len
    gain = gain_part.shape
    rows_a, rows_b = w_qkv.shape[0] // 64, left.shape[1] // 64
    return pl.pallas_call(
        back_kernel,
        out_shape=(
            jax.ShapeDtypeStruct(w_qkv.shape, low),
            jax.ShapeDtypeStruct((64 * rows_b, width), low),
            jax.ShapeDtypeStruct(gain, jnp.float32),
            jax.ShapeDtypeStruct((rows_all, width), low),
        ),
        in_specs=[vmem] * 14 + [any_],
        out_specs=(any_, any_, vmem, vmem),
        scratch_shapes=[
            pltpu.VMEM((4, rows_all, 8 * rows_b), low),
            pltpu.VMEM(right.shape, low),
            pltpu.VMEM((rows_all, width), low),
            pltpu.VMEM((3, slots, block_len, width), low),
            pltpu.VMEM(w_qkv.shape, low),
            DMA((7,)),
            DMA((7,)),
            pltpu.VMEM(qkv_heads.shape, low),
            pltpu.VMEM((slots, seq, my_width), low),
            pltpu.VMEM((3, slots, block_len, width), low),
            pltpu.VMEM((seq, my_width), jnp.float32),
            pltpu.VMEM((seq, my_width), jnp.float32),
            pltpu.VMEM((rows_all, width), jnp.float32),
            pltpu.VMEM(gain, jnp.float32),
            pltpu.VMEM((3,) + gain, jnp.float32),
            pltpu.VMEM((4,) + gain, jnp.float32),
            DMA,
            DMA,
            DMA((8,)),
            DMA((8,)),
            DMA((slots,)),
            DMA((slots, 8)),
            DMA((slots, 8)),
        ]
        + reduce_scratch(rows_a, width)
        + reduce_scratch(rows_b, width)
        + GATHER_SEMS * 2
        + GAIN_SEMS,
        compiler_params=pltpu.CompilerParams(
            collective_id=collective_id, has_side_effects=True, vmem_limit_bytes=VMEM_BYTES
        ),
        name="back_and_sum",
    )(grad_rows, qkv_heads, wide, lse, bias, cosine, sine, norm_one, tokens, gains, grad_middle, gain_part, left, right, w_qkv)


def to_heads(values):
    return lax.all_to_all(values, "ctx", split_axis=3, concat_axis=2, tiled=True)


def to_rows(values):
    return lax.all_to_all(values, "ctx", split_axis=2, concat_axis=3, tiled=True)


def shards(
    fast,
    tokens,
    cotangent,
    lengths,
    unit_owner,
    master,
    first_moment,
    second_moment,
    norm_gains,
    gain_first,
    gain_second,
):
    slots, block_len, width = tokens.shape
    groups = lax.axis_size("shard")
    n = lax.axis_size("ctx")
    ctx, shard = lax.axis_index("ctx"), lax.axis_index("shard")
    capacity, unit_rows, _ = master.shape
    units = unit_owner.shape[0]
    rows_all = slots * block_len
    seq = block_len * n
    device_count = n * groups
    my_width = width // n

    low = jnp.bfloat16
    rows_a = 3 * width
    rows_b = width + 3 * FF_WIDE
    split = rows_a // unit_rows
    lead, ff_units, wide_units = (r // unit_rows for r in (width, FF, FF_WIDE))

    def unit_of(block, chunk):
        if chunk == 0:
            return jnp.where(block < split, block, -1)
        inner = block - lead
        third = inner // wide_units
        at = inner - third * wide_units
        there = (block < lead) | ((at < ff_units) & (third < 3))
        return jnp.where(there, split + jnp.where(block < lead, block, lead + third * ff_units + at), -1)

    def block_of(unit):
        inner = unit - split - lead
        third = jnp.maximum(inner, 0) // ff_units
        return unit - split + third * (wide_units - ff_units)

    part_rows = 16
    per_unit = unit_rows // part_rows
    parts = master.reshape(capacity * per_unit, part_rows, width)

    def units_at(chunk, per, wanted):
        at = wanted[..., None] * (per // part_rows) + jnp.arange(per // part_rows, dtype=jnp.int32)
        at = at.reshape(-1)
        return unit_of(at // per_unit, chunk), at % per_unit

    def pick(unit, inner):
        owner, rank = unit_places(unit_owner, unit)
        mine = (owner == shard) & (unit >= 0)
        return pick_call(jnp.where(mine, rank * per_unit + inner, -1), parts)

    def piece_rows(count, pieces):
        return -(-count // (pieces * part_rows)) * part_rows

    positions = ctx * block_len + jnp.arange(block_len, dtype=jnp.int32)
    tile_heads = 256 // HEAD_DIM
    cos_rows, sin_rows = rope_tables(jnp.tile(positions, slots), tile_heads)
    cos_seq, sin_seq = rope_tables(jnp.arange(seq, dtype=jnp.int32), my_width // HEAD_DIM)
    live_rows = (positions[None, :] < lengths[:, None]).astype(jnp.float32)
    bias = jnp.where(
        jnp.arange(seq, dtype=jnp.int32)[None, :] < lengths[:, None], 0.0, mask_fill
    ).astype(jnp.float32)[:, None, :]

    inputs = tokens.astype(jnp.float32).reshape(rows_all, width)
    norm_one = layer_norm(inputs, norm_gains[0]).astype(jnp.bfloat16)
    if fast:
        z, y, x, core = place()
        wanted = jnp.stack(
            [
                jnp.stack([jnp.stack([piece_at(z, c, 0, y, q), piece_at(z, c, 1, q, y)]) for q in range(2)])
                for c in range(2)
            ]
        )
        per_a, per_b = piece_rows(rows_a, 64), piece_rows(rows_b, 64)
        at_pieces = [units_at(0, per_a, wanted), units_at(1, per_b, wanted)]
        given = pick(*(jnp.concatenate(both) for both in zip(*at_pieces)))
        stack_a, stack_b, qkv_heads, wide, lse, mixed_low = front_call(
            given, per_a, per_b, norm_one, cos_rows, sin_rows, bias, slots, block_len, 0
        )
    else:
        wanted = ctx * groups + jnp.arange(groups, dtype=jnp.int32)
        stacks = []
        for chunk, count in enumerate((rows_a, rows_b)):
            share = pick(*units_at(chunk, piece_rows(count, device_count), wanted))
            own = lax.psum_scatter(share, "shard", scatter_dimension=0, tiled=True)
            stacks.append(lax.all_gather(own, BOTH, axis=0, tiled=True))
        stack_a, stack_b = stacks
        qkv = qkv_call(norm_one, stack_a, cos_rows, sin_rows)
        qkv_heads = to_heads(qkv.reshape(3, slots, block_len, width))
        mixed_heads, wide, lse = attend_call(qkv_heads, bias)
        mixed_low = to_rows(mixed_heads[None])
    mixed_low = mixed_low.reshape(rows_all, width)
    w_out = stack_b[:width]
    w_up = stack_b[width : width + 2 * FF_WIDE]
    w_down = stack_b[width + 2 * FF_WIDE : rows_b]

    middle = inputs + transposed(mixed_low, w_out)
    norm_two = layer_norm(middle, norm_gains[1]).astype(jnp.bfloat16)
    upper_proj = transposed(norm_two, w_up)
    hidden_low = gated_gelu(upper_proj).astype(jnp.bfloat16)
    result = middle + jnp.dot(hidden_low, w_down, preferred_element_type=jnp.float32)
    output = result.astype(jnp.bfloat16).reshape(slots, block_len, width)

    grad_result = cotangent.astype(jnp.float32).reshape(rows_all, width) * live_rows.reshape(
        rows_all, 1
    )
    grad_down_low = grad_result.astype(jnp.bfloat16)
    grad_hidden = transposed(grad_down_low, w_down)
    _, gelu_back = jax.vjp(gated_gelu, upper_proj)
    grad_upper_low = gelu_back(grad_hidden)[0].astype(jnp.bfloat16)
    grad_norm_two = jnp.dot(grad_upper_low, w_up, preferred_element_type=jnp.float32)
    _, norm_back_two = jax.vjp(layer_norm, middle, norm_gains[1])
    grad_middle_part, grad_gain_two = norm_back_two(grad_norm_two)
    grad_middle = grad_result + grad_middle_part
    grad_attn_low = grad_middle.astype(jnp.bfloat16)
    grad_heads_rows = jnp.dot(grad_attn_low, w_out, preferred_element_type=jnp.float32).astype(
        jnp.bfloat16
    )
    grad_heads_rows = grad_heads_rows.reshape(slots, block_len, width)

    gain_part = jnp.zeros((8, width), jnp.float32).at[1].set(grad_gain_two)
    if fast:
        left = jnp.concatenate(
            [
                grad_attn_low,
                grad_upper_low,
                hidden_low,
                jnp.zeros((rows_all, stack_b.shape[0] - rows_b), low),
            ],
            axis=1,
        )
        right = jnp.stack([mixed_low, norm_two, grad_down_low])
        all_a, all_b, gain_grad, token_grad = back_call(
            grad_heads_rows, qkv_heads, wide, lse, bias, cos_seq, sin_seq, norm_one, tokens.reshape(rows_all, width),
            norm_gains, grad_middle, gain_part, left, right, stack_a, 1,
        )
    else:
        grads_b = jnp.concatenate(
            [
                leading(grad_attn_low, mixed_low).astype(low),
                leading(grad_upper_low, norm_two).astype(low),
                leading(hidden_low, grad_down_low).astype(low),
                jnp.zeros((stack_b.shape[0] - rows_b, width), low),
            ],
            axis=0,
        )
        grad_heads = to_heads(grad_heads_rows[None])[0]
        grad_qkv_heads = attend_back_call(qkv_heads, grad_heads, wide, lse, bias, cos_seq, sin_seq)
        grad_qkv_low = to_rows(grad_qkv_heads).reshape(3, rows_all, width)
        grad_norm_one = sum(
            jnp.dot(
                grad_qkv_low[i],
                stack_a[i * width : (i + 1) * width],
                preferred_element_type=jnp.float32,
            )
            for i in range(3)
        )
        _, norm_back_one = jax.vjp(layer_norm, inputs, norm_gains[0])
        grad_input_part, grad_gain_one = norm_back_one(grad_norm_one)
        token_grad = (grad_middle + grad_input_part).astype(low)
        grads_a = jnp.concatenate(
            [leading(grad_qkv_low[i], norm_one).astype(low) for i in range(3)]
            + [jnp.zeros((stack_a.shape[0] - rows_a, width), low)],
            axis=0,
        )
        all_a, all_b = (
            lax.all_gather(
                lax.psum_scatter(g, BOTH, scatter_dimension=0, tiled=True), BOTH, axis=0, tiled=True
            )
            for g in (grads_a, grads_b)
        )
        gain_grad = lax.psum(gain_part.at[0].set(grad_gain_one), BOTH)
    token_grad = token_grad.reshape(slots, block_len, width)
    gain_grad = gain_grad[:2]
    all_a = all_a.reshape(-1, unit_rows, width)
    all_b = all_b.reshape(-1, unit_rows, width)

    every = jnp.arange(units, dtype=jnp.int32)
    rank = unit_places(unit_owner, every)[1]
    here = (unit_owner == shard) & (rank == jnp.arange(capacity, dtype=jnp.int32)[:, None])
    unit_of_slot = jnp.sum(jnp.where(here, every + 1, 0), axis=1) - 1
    kind = jnp.where(unit_of_slot < 0, -1, (unit_of_slot >= split).astype(jnp.int32))
    at_a = jnp.maximum(lax.cummax(jnp.where(kind == 0, unit_of_slot, -1)), 0)
    at_b = jnp.maximum(block_of(lax.cummax(jnp.where(kind == 1, unit_of_slot, -1))), 0)
    new_master, new_first, new_second = adam_call(
        kind, at_a, at_b, all_a, all_b, master, first_moment, second_moment
    )
    new_gains, new_gain_first, new_gain_second = adam_update(
        norm_gains, gain_grad, gain_first, gain_second, rate_gain, 0.0
    )
    return (
        output,
        token_grad,
        new_master,
        new_first,
        new_second,
        new_gains,
        new_gain_first,
        new_gain_second,
    )


def solution(mesh):
    fast = dict(mesh.shape) == {"ctx": 8, "shard": 4}
    return jax.shard_map(
        functools.partial(shards, fast),
        mesh=mesh,
        in_specs=(
            P("shard", "ctx", None),
            P("shard", "ctx", None),
            P("shard"),
            P(),
            P("shard", None, None),
            P("shard", None, None),
            P("shard", None, None),
            P(),
            P(),
            P(),
        ),
        out_specs=(
            P("shard", "ctx", None),
            P("shard", "ctx", None),
            P("shard", None, None),
            P("shard", None, None),
            P("shard", None, None),
            P(),
            P(),
            P(),
        ),
        check_vma=False,
    )
```

time: 706 us -> 521 us (0.74); the launches traced: 695 us -> 521 us
  Pallas kernels: 567 us -> 456 us
  local copies, waits for them, and re-layouts: 36.7 us -> 4.46 us
  other arithmetic: 43 us -> 26.8 us
  matrix products: 47.1 us -> 32.1 us
    pallas_call x9 -> x3, Pallas kernels: 521 us -> 411 us  [the longest x1 247 us: back_call(): pl.pallas_call(back_kernel, out_shape=(jax.ShapeDtypeStruct(w_qkv.shape,...]
    gather x6 -> x0, local copies, waits for them, and re-layouts: 17.1 us -> none  [the longest x4 15.1 us: share_of(): taken = jnp.take(master, rank[unit].reshape(-1), axis=0, mode='clip')]
    dot_general x9 -> x0, matrix products: 14.5 us -> none  [the longest x6 12.2 us: leading(): lax.dot_general(left, right, (((0,), (0,)), ((), ())), preferred_element_...]
    slice x3 -> x0, local copies, waits for them, and re-layouts: 13.4 us -> none  [the longest x1 5.98 us: shards(): w_up = stack_b[:2 * FF]]
    concatenate x2, other arithmetic: 14.6 us -> 2.71 us  [the longest x1 2.63 us: shards(): jnp.concatenate([grad_attn_low, grad_upper_low, hidden_low, jnp.zeros((ro...]
where the time goes in v3:
time: 521 us
  Pallas kernels  456 us (88%)
  matrix products  32.1 us (6%)
  other arithmetic  26.8 us (5%)
    pallas_call x1, Pallas kernels, back_call(): pl.pallas_call(back_kernel, out_shape=(jax.ShapeDtypeStruct(w_qkv.shape,...  247 us
    pallas_call x1, Pallas kernels, front_call(): pl.pallas_call(front_kernel, out_shape=(stack_a, stack_b, jax.ShapeDtypeS...  157 us
    pallas_call x1, Pallas kernels, adam_call(): pl.pallas_call(functools.partial(adam_kernel, per), grid_spec=pltpu.Prefe...  45.7 us
    dot_general x3, matrix products, transposed(): lax.dot_general(left, right, (((1,), (1,)), ((), ())), preferred_element_...  18 us

profile of v3, /device:TPU:0, one launch (start us, length us, event | category | flops | bytes accessed | tf_op | source)
XLA Modules:
  0.0 520.7 jit_solution(6084976604125817330)
XLA Ops:
  0.9 0.7 broadcast_compare_fusion.2
  1.6 0.7 fusion.50
  2.3 1.2 convert_reduce_fusion
  3.5 0.8 select_reduce_fusion
  4.3 0.9 convert_reduce_fusion.1
  5.9 1.3 multiply_reduce_fusion.3
  7.7 0.9 select_reduce_fusion.1
  8.5 0.9 convert_reduce_fusion.2
  10.0 1.3 compare_select_fusion.bias_ref
  11.3 0.8 fusion.62
  12.5 0.7 maximum_reduce_fusion.a_ref
  14.5 1.0 concatenate.34.sin_ref
  15.5 1.0 concatenate.33.cos_ref
  16.4 1.1 fusion.34.norm_ref
  17.9 1.9 fusion.38
  19.9 1.9 pad_maximum_fusion.1
  21.7 6.7 %pick.1.given_ref = bf16[1536,1024]{1,0:T(8,128)(2,1)} custom-call(s32[96]{0:T(128)} %and_select_fusion.2.part_ref, f32[280,16,1024]{2,1,0:T(8,128)} %bitcast.84), custom_call_target="tpu_custom_call" | custom-call | tf_op jit(solution)/shard_map/pick/pallas_call | solution.py:337
  28.4 157.0 %spread_and_attend.1 = (bf16[3072,1024]{1,0:T(8,128)(2,1)}, bf16[9216,1024]{1,0:T(8,128)(2,1)}, bf16[3,2,1024,128]{3,2,1,0:T(8,128)(2,1)}, f32[2,1024,128]{2,1,0...) custom-call(bf16[1536,1024]{1,0:T(8,128)(2,1)} %pick.1.given_ref, bf16[256,1024]{1,0:T(8,128)(2,1)} %fusion.34.norm_ref, ...), custom_call_target="tpu_custom_call" | custom-call | tf_op jit(solution)/shard_map/spread_and_attend/pallas_call | solution.py:919
  185.4 2.6 fusion.63
  188.3 6.1 %fusion.2 = f32[256,5376]{1,0:T(8,128)S(1)} fusion(bf16[9216,1024]{1,0:T(8,128)(2,1)} %get-tuple-element.34, f32[256,1024]{1,0:T(8,128)S(1)} %get-tuple-element.83, f32[1024]{0:T(1024)S(1)} %bitcast.92, f32[256]{0:T(256)S(1)} %fusion.51, f32[256]{0:T(256)S(1)} %broadcast_multiply_fusion.2), kind=kOutput, calls=%fused_computation.2 | convolution fusion | flops 2819620864 | bytes 17569792 | tf_op jit(solution)/shard_map/dot_general | solution.py:32
  194.4 9.3 %fusion.36 = (f32[256,2688]{1,0:T(8,128)S(1)}, f32[256,2688]{1,0:T(8,128)S(1)}, f32[256,2688]{1,0:T(8,128)S(1)}) fusion(f32[256,5376]{1,0:T(8,128)S(1)} %fusion.2, bf16[256,1024]{1,0:T(8,128)(2,1)S(1)} %fusion.35, bf16[9216,1024]{1,0:T(8,128)(2,1)} %get-tuple-element.34), kind=kOutput, calls=%fused_computation.53 | convolution fusion | flops 1454014464 | bytes 17039360 | tf_op jit(solution)/shard_map/dot_general | solution.py:32
  203.7 1.4 multiply_add_fusion
  205.4 5.0 fusion.25
  210.4 6.0 %multiply_reduce_fusion = (f32[1024]{0:T(1024)S(1)}, f32[256]{0:T(256)S(1)}, f32[256,1024]{1,0:T(8,128)S(1)}) fusion(f32[256,1024]{1,0:T(8,128)S(1)} %get-tuple-element.83, f32[256]{0:T(256)S(1)} %fusion.51, f32[256]{0:T(256)S(1)} %broadcast_multiply_fusion.2, f32[1024]{0:T(1024)S(1)} %bitcast.93, bf16[256,5376]{1,0:T(8,128)(2,1)S(1)} %add_convert_fusion, ...), kind=kOutput, calls=%fused_computation.46 | convolution fusion | flops 2820406016 | bytes 15870976 | tf_op jit(solution)/shard_map/dot_general | solution.py:1446
  217.6 1.2 fusion.59
  218.7 3.1 fusion.28
  221.9 1.3 pad_maximum_fusion.right_ref
  223.2 2.6 maximum_maximum_fusion.left_ref
  225.9 246.9 %back_and_sum.1 = (bf16[3072,1024]{1,0:T(8,128)(2,1)}, bf16[9216,1024]{1,0:T(8,128)(2,1)}, f32[8,1024]{1,0:T(8,128)}, bf16[256,1024]{1,0:T(8,128)(2,1)}) custom-call(bf16[2,128,1024]{2,1,0:T(8,128)(2,1)} %bitcast.88, bf16[3,2,1024,128]{3,2,1,0:T(8,128)(2,1)} %get-tuple-element.35.qkv_ref, f32[2,1024,128]{2,1,0:T(8,128)} %get-tuple-element.36.wide_ref, ...), custom_call_target="tpu_custom_call" | custom-call | tf_op jit(solution)/shard_map/back_and_sum/pallas_call | solution.py:1275
  472.7 1.4 multiply_subtract_fusion
  474.1 45.7 %adamw.1 = (f32[70,64,1024]{2,1,0:T(8,128)}, f32[70,64,1024]{2,1,0:T(8,128)}, f32[70,64,1024]{2,1,0:T(8,128)}) custom-call(s32[70]{0:T(128)} %get-tuple-element.77.unit_ref, s32[70]{0:T(128)} %maximum_reduce_fusion.a_ref, s32[70]{0:T(128)} %fusion.54.b_ref, bf16[48,64,1024]{2,1,0:T(8,128)(2,1)} %bitcast.77, bf16[48,64,1024]{2,1,0:T(8,128)(2,1)} %bitcast.78, ...), custom_call_target="tpu_custom_call" | custom-call | tf_op jit(solution)/shard_map/adamw/pallas_call | solution.py:288
  519.9 0.8 copy.37
  (57 shorter events, 5.6 us)
Async XLA Ops:
  0.6 15.8 %copy-start = (bf16[2,128,1024]{2,1,0:T(8,128)(2,1)S(1)}, bf16[2,128,1024]{2,1,0:T(8,128)(2,1)}, u32[]{:S(2)}) copy-start(bf16[2,128,1024]{2,1,0:T(8,128)(2,1)} %param.12) | copy-start | bytes 1572868
  2.3 15.2 %copy-start.1 = (bf16[2,128,1024]{2,1,0:T(8,128)(2,1)S(1)}, bf16[2,128,1024]{2,1,0:T(8,128)(2,1)}, u32[]{:S(2)}) copy-start(bf16[2,128,1024]{2,1,0:T(8,128)(2,1)} %param.13) | copy-start | bytes 1572868
  218.7 3.2 copy-start.3
  225.8 246.9 %copy-start.4 = (f32[2,1024]{1,0:T(2,128)S(1)}, f32[2,1024]{1,0:T(2,128)}, u32[]{:S(2)}) copy-start(f32[2,1024]{1,0:T(2,128)} %gains_ref.1) | copy-start | bytes 24580
  225.8 246.9 %copy-start.5 = (f32[2,1024]{1,0:T(2,128)S(1)}, f32[2,1024]{1,0:T(2,128)}, u32[]{:S(2)}) copy-start(f32[2,1024]{1,0:T(2,128)} %param.20) | copy-start | bytes 24580
  225.8 246.9 %copy-start.6 = (f32[2,1024]{1,0:T(2,128)S(1)}, f32[2,1024]{1,0:T(2,128)}, u32[]{:S(2)}) copy-start(f32[2,1024]{1,0:T(2,128)} %param.21) | copy-start | bytes 24580
  474.1 45.7 %copy-start.2 = (bf16[256,1024]{1,0:T(8,128)(2,1)S(1)}, bf16[256,1024]{1,0:T(8,128)(2,1)}, u32[]{:S(2)}) copy-start(bf16[256,1024]{1,0:T(8,128)(2,1)} %get-tuple-element.39) | copy-start | bytes 1572868

commit v4 on v3

--- a/solution.py
+++ b/solution.py
@@ -1,7 +1,9 @@
 import functools
+import math
 
 import jax
 import jax.numpy as jnp
+import numpy as np
 from jax import lax
 from jax.experimental import pallas as pl
 from jax.experimental.pallas import tpu as pltpu
@@ -47,14 +49,15 @@
     return centred * lax.rsqrt(variance + eps_norm) * gain
 
 
-def rope_tables(positions, heads):
+def rope_tables(seq, heads):
     half_dim = HEAD_DIM // 2
-    inverse = rope_base ** (-2.0 * jnp.arange(half_dim, dtype=jnp.float32) / HEAD_DIM)
-    angles = positions.astype(jnp.float32)[:, None] * inverse[None, :]
-    cosine, sine = jnp.cos(angles), jnp.sin(angles)
-    cosine = jnp.concatenate([cosine, cosine] * heads, axis=1)
-    sine = jnp.concatenate([-sine, sine] * heads, axis=1)
-    return (cosine, sine)
+    inverse = rope_base ** (-2.0 * np.arange(half_dim) / HEAD_DIM)
+    angles = np.arange(seq)[:, None] * inverse.astype(np.float32).astype(np.float64)[None, :]
+    angles = angles.astype(np.float32).astype(np.float64)
+    cosine, sine = np.cos(angles), np.sin(angles)
+    cosine = np.concatenate([cosine, cosine] * heads, axis=1)
+    sine = np.concatenate([-sine, sine] * heads, axis=1)
+    return jnp.asarray(cosine, jnp.float32), jnp.asarray(sine, jnp.float32)
 
 
 def half_turned(values):
@@ -73,10 +76,6 @@
     owner = jnp.sum(jnp.where(every == chosen[:, None], unit_owner, 0), axis=1)
     below = (every < chosen[:, None]) & (unit_owner == owner[:, None])
     return owner, jnp.sum(below.astype(jnp.int32), axis=1)
-
-
-def gated_gelu(upper_proj):
-    return jax.nn.gelu(upper_proj[:, :FF_WIDE], approximate=False) * upper_proj[:, FF_WIDE:]
 
 
 def adam_update(weight, gradient, first_old, second_old, step_rate, weight_decay):
@@ -129,6 +128,11 @@
         return values
     lane = lax.broadcasted_iota(jnp.int32, values.shape, 1)
     return jnp.where(lane // HEAD_DIM == head, values, jnp.zeros_like(values))
+
+
+def key_bias(length, seq):
+    position = lax.broadcasted_iota(jnp.int32, (1, seq), 1)
+    return jnp.where(position < length, 0.0, mask_fill).astype(jnp.float32)
 
 
 def attend_step(i, q_ref, k_ref, v_ref, bias, out_ref, wide_ref, lse_ref, chunk):
@@ -215,15 +219,15 @@
     attend_back_end(*args)
 
 
-def attend_kernel(slots, chunk, qkv_ref, bias_ref, out_ref, wide_ref, lse_ref):
+def attend_kernel(slots, chunk, qkv_ref, lengths_ref, out_ref, wide_ref, lse_ref):
     for s in range(slots):
         attend_slot(
-            qkv_ref.at[0, s], qkv_ref.at[1, s], qkv_ref.at[2, s], bias_ref[s],
+            qkv_ref.at[0, s], qkv_ref.at[1, s], qkv_ref.at[2, s], key_bias(lengths_ref[s], qkv_ref.shape[2]),
             out_ref.at[s], wide_ref.at[s], lse_ref.at[s], chunk,
         )
 
 
-def attend_call(qkv, bias):
+def attend_call(qkv, lengths):
     _, slots, seq, width = qkv.shape
     chunk = 256
     return pl.pallas_call(
@@ -233,30 +237,168 @@
             jax.ShapeDtypeStruct((slots, seq, width), jnp.float32),
             jax.ShapeDtypeStruct((slots, seq, width), jnp.float32),
         ),
+        in_specs=[pl.BlockSpec(memory_space=pltpu.VMEM), pl.BlockSpec(memory_space=pltpu.SMEM)],
         compiler_params=pltpu.CompilerParams(vmem_limit_bytes=VMEM_BYTES),
         name="attend",
-    )(qkv, bias)
-
-
-def attend_back_kernel(slots, chunk, qkv_ref, g_ref, wide_ref, lse_ref, bias_ref, cos_ref, sin_ref, out_ref, acc_k, acc_v):
+    )(qkv, lengths)
+
+
+def attend_back_kernel(slots, chunk, qkv_ref, g_ref, wide_ref, lse_ref, lengths_ref, cos_ref, sin_ref, out_ref, acc_k, acc_v):
     for s in range(slots):
         attend_back_slot(
             qkv_ref.at[0, s], qkv_ref.at[1, s], qkv_ref.at[2, s], g_ref.at[s],
-            wide_ref.at[s], lse_ref.at[s], bias_ref[s], cos_ref, sin_ref,
+            wide_ref.at[s], lse_ref.at[s], key_bias(lengths_ref[s], qkv_ref.shape[2]), cos_ref, sin_ref,
             out_ref.at[0, s], out_ref.at[1, s], out_ref.at[2, s], acc_k, acc_v, chunk,
         )
 
 
-def attend_back_call(qkv, grad_heads, wide, lse, bias, cosine, sine):
+def attend_back_call(qkv, grad_heads, wide, lse, lengths, cosine, sine):
     _, slots, seq, width = qkv.shape
     chunk = 256
     return pl.pallas_call(
         functools.partial(attend_back_kernel, slots, chunk),
         out_shape=jax.ShapeDtypeStruct(qkv.shape, jnp.bfloat16),
+        in_specs=[pl.BlockSpec(memory_space=pltpu.VMEM)] * 4
+        + [pl.BlockSpec(memory_space=pltpu.SMEM)]
+        + [pl.BlockSpec(memory_space=pltpu.VMEM)] * 2,
         scratch_shapes=[pltpu.VMEM((seq, width), jnp.float32)] * 2,
         compiler_params=pltpu.CompilerParams(vmem_limit_bytes=VMEM_BYTES),
         name="attend_back",
-    )(qkv, grad_heads, wide, lse, bias, cosine, sine)
+    )(qkv, grad_heads, wide, lse, lengths, cosine, sine)
+
+
+def middle_kernel(
+    tile, block_len, mixed_ref, tokens_ref, cot_ref, gains_ref, lengths_ref, w_ref,
+    out_ref, left_ref, right_ref, go_ref, back_ref, gain_ref,
+    w_out, w_one, w_two, w_down, x1, result, dnorm, sems
+):
+    rows_all, width = tokens_ref.shape
+    wide = w_one.shape[0] * tile
+    tiles = wide // tile
+    cols = 256
+    some = 64
+    start = lax.axis_index("ctx") * block_len
+
+    def live(i):
+        slot, inner = i * some // block_len, i * some % block_len
+        position = start + inner + lax.broadcasted_iota(jnp.int32, (some, 1), 0)
+        return (position < lengths_ref[slot]).astype(jnp.float32)
+
+    def copies(j):
+        rows = [pl.ds(width + k * wide + j * tile, tile) for k in range(3)]
+        return [
+            pltpu.make_async_copy(w_ref.at[r], to.at[j], sems.at[1 + j * 3 + k])
+            for k, (r, to) in enumerate(zip(rows, (w_one, w_two, w_down)))
+        ]
+
+    first = pltpu.make_async_copy(w_ref.at[pl.ds(0, width)], w_out, sems.at[0])
+    first.start()
+    for j in range(tiles):
+        for copy in copies(j):
+            copy.start()
+    right_ref[0] = mixed_ref[...]
+    first.wait()
+
+    def out_step(t, _):
+        at = pl.ds(pl.multiple_of(t * cols, cols), cols)
+        x1[:, at] = tokens_ref[:, at].astype(jnp.float32) + transposed(mixed_ref[...], w_out[at, :])
+        return 0
+
+    lax.fori_loop(0, width // cols, out_step, 0)
+
+    def normal(at):
+        values = x1[at, :]
+        mean = jnp.mean(values, axis=-1, keepdims=True)
+        centred = values - mean
+        scale = lax.rsqrt(jnp.mean(centred * centred, axis=-1, keepdims=True) + eps_norm)
+        return centred * scale, scale
+
+    def norm_step(i, _):
+        at = pl.ds(pl.multiple_of(i * some, some), some)
+        unit, _ = normal(at)
+        right_ref[1, at, :] = (unit * gains_ref[1:2, :]).astype(jnp.bfloat16)
+        right_ref[2, at, :] = (cot_ref[at, :].astype(jnp.float32) * live(i)).astype(jnp.bfloat16)
+        return 0
+
+    lax.fori_loop(0, rows_all // some, norm_step, 0)
+    result[...] = x1[...]
+    dnorm[...] = jnp.zeros_like(dnorm)
+    for j in range(tiles):
+        for copy in copies(j):
+            copy.wait()
+        norm, grad = right_ref[1], right_ref[2]
+        one = transposed(norm, w_one[j])
+        two = transposed(norm, w_two[j])
+        back = transposed(grad, w_down[j])
+        share = 0.5 * (1.0 + lax.erf(one * (0.5**0.5)))
+        gelu = one * share
+        slope = share + one * (jnp.exp(-0.5 * one * one) * (0.5 / math.pi) ** 0.5)
+        low = (gelu * two).astype(jnp.bfloat16)
+        d_one = (back * two * slope).astype(jnp.bfloat16)
+        d_two = (back * gelu).astype(jnp.bfloat16)
+        for k, part in enumerate((d_one, d_two, low)):
+            left_ref[:, pl.ds(width + k * wide + j * tile, tile)] = part
+        result[...] += jnp.dot(low, w_down[j], preferred_element_type=jnp.float32)
+        dnorm[...] += jnp.dot(d_one, w_one[j], preferred_element_type=jnp.float32) + jnp.dot(
+            d_two, w_two[j], preferred_element_type=jnp.float32
+        )
+    end = width + 3 * wide
+    if left_ref.shape[1] > end:
+        left_ref[:, end:] = jnp.zeros((rows_all, left_ref.shape[1] - end), left_ref.dtype)
+    out_ref[...] = result[...].astype(out_ref.dtype)
+    gain_ref[...] = jnp.zeros_like(gain_ref)
+
+    def back_step(i, _):
+        at = pl.ds(pl.multiple_of(i * some, some), some)
+        unit, scale = normal(at)
+        given = dnorm[at, :]
+        inner = given * gains_ref[1:2, :]
+        inner_mean = jnp.mean(inner, axis=-1, keepdims=True)
+        along = jnp.mean(inner * unit, axis=-1, keepdims=True)
+        grad = cot_ref[at, :].astype(jnp.float32) * live(i)
+        grad = grad + scale * (inner - inner_mean - unit * along)
+        back_ref[at, :] = grad
+        left_ref[at, 0:width] = grad.astype(jnp.bfloat16)
+        gain_ref[1:2, :] += jnp.sum(given * unit, axis=0, keepdims=True)
+        return 0
+
+    lax.fori_loop(0, rows_all // some, back_step, 0)
+
+    def go_step(t, _):
+        at = pl.ds(pl.multiple_of(t * cols, cols), cols)
+        go_ref[:, at] = jnp.dot(
+            left_ref[:, 0:width], w_out[:, at], preferred_element_type=jnp.float32
+        ).astype(jnp.bfloat16)
+        return 0
+
+    lax.fori_loop(0, width // cols, go_step, 0)
+
+
+def middle_call(mixed, tokens, cotangent, gains, lengths, stack_b, left_cols, block_len):
+    rows_all, width = tokens.shape
+    low = jnp.bfloat16
+    tile = 384
+    tiles = FF_WIDE // tile
+    vmem = pl.BlockSpec(memory_space=pltpu.VMEM)
+    return pl.pallas_call(
+        functools.partial(middle_kernel, tile, block_len),
+        out_shape=(
+            jax.ShapeDtypeStruct((rows_all, width), low),
+            jax.ShapeDtypeStruct((rows_all, left_cols), low),
+            jax.ShapeDtypeStruct((3, rows_all, width), low),
+            jax.ShapeDtypeStruct((rows_all, width), low),
+            jax.ShapeDtypeStruct((rows_all, width), jnp.float32),
+            jax.ShapeDtypeStruct((8, width), jnp.float32),
+        ),
+        in_specs=[vmem] * 4 + [pl.BlockSpec(memory_space=pltpu.SMEM), pl.BlockSpec(memory_space=pl.ANY)],
+        out_specs=(vmem,) * 6,
+        scratch_shapes=[pltpu.VMEM((width, width), low)]
+        + [pltpu.VMEM((tiles, tile, width), low)] * 3
+        + [pltpu.VMEM((rows_all, width), jnp.float32)] * 3
+        + [DMA((1 + 3 * tiles,))],
+        compiler_params=pltpu.CompilerParams(vmem_limit_bytes=VMEM_BYTES),
+        name="middle",
+    )(mixed, tokens, cotangent, gains, lengths, stack_b)
 
 
 def adam_kernel(per, unit_ref, a_ref, b_ref, *refs):
@@ -688,8 +830,8 @@
 
 
 def front_kernel(
-    given_ref, norm_ref, cos_ref, sin_ref, bias_ref,
-    oa_ref, ob_ref, heads, wide_ref, lse_ref, mixed_ref,
+    given_ref, tokens_ref, gains_ref, cos_ref, sin_ref, lengths_ref,
+    oa_ref, ob_ref, heads, wide_ref, lse_ref, mixed_ref, norm_ref,
     stack, rows, seen, low, mixed, got_a, got_b, new_a, new_b, own_a, own_b, send, recv, csem, ql, qsend, qrecv, ml, msend, mrecv, *sems
 ):
     n = 8
@@ -774,6 +916,20 @@
             3 * (1 - s),
         )[i]
 
+    def norm():
+        def step(i, _):
+            at = pl.ds(pl.multiple_of(i * 64, 64), 64)
+            values = layer_norm(tokens_ref[at, :].astype(jnp.float32), gains_ref[0:1, :])
+            norm_ref[at, :] = values.astype(jnp.bfloat16)
+            return 0
+
+        lax.fori_loop(0, slots * block_len // 64, step, 0)
+
+    def table(ref):
+        one = ref[block(ctx), :]
+        one = jnp.concatenate([one] * (cols // my_width), axis=1)
+        return jnp.concatenate([one] * slots, axis=0)
+
     def qkv(i):
         zb = region(i)
         ga.whole(zb, 1 - core).wait_recv()
@@ -785,8 +941,8 @@
             weight = stack[pl.ds(pl.multiple_of(tile * cols, cols), cols), :]
             values = transposed(norm_ref[...], weight)
             turn = (j < 2).astype(jnp.float32)
-            cos = cos_ref[...] * turn + (1.0 - turn)
-            values = values * cos + half_turned(values) * (sin_ref[...] * turn)
+            cos = table(cos_ref) * turn + (1.0 - turn)
+            values = values * cos + half_turned(values) * (table(sin_ref) * turn)
             rows[j, :, :, at] = values.astype(jnp.bfloat16).reshape(slots, block_len, cols)
             for q in range(cols // my_width):
                 owner = t * (cols // my_width) + q
@@ -803,12 +959,11 @@
 
         lax.fori_loop(0, per_z, tile_step, 0)
 
-    def heads_wait():
-        for j in range(3):
-            head_own(j).wait()
-            for d in range(1, n):
-                ref = seen.at[j, :, block(peer(d)), :]
-                remote(ref, ref, qsend.at[j, peer(d)], qrecv.at[j, peer(d)], (peer(d), shard)).wait_recv()
+    def heads_wait(j):
+        head_own(j).wait()
+        for d in range(1, n):
+            ref = seen.at[j, :, block(peer(d)), :]
+            remote(ref, ref, qsend.at[j, peer(d)], qrecv.at[j, peer(d)], (peer(d), shard)).wait_recv()
 
     def mixed_wait():
         for s in range(slots):
@@ -822,27 +977,35 @@
     spread(1)
     cross(0)
     ga.start()
+    norm()
     ga.line(-1), ga.line(1)
     ga.cross(0)
     ga.line(-2), ga.line(2)
+    cross(1)
+    gb.start()
     ga.cross(-1), ga.cross(1)
     ga.close(0)
-    cross(1)
     ga.line(-3), ga.line(3)
     ga.cross(-2), ga.cross(2)
     qkv(0)
+    gb.line(-1), gb.line(1)
     ga.close(-1), ga.close(1)
-    gb.start()
     ga.cross(-3), ga.cross(3)
     qkv(1)
+    gb.cross(0)
     ga.close(-2), ga.close(2)
-    gb.line(-1), gb.line(1)
     qkv(2)
     ga.close(-3), ga.close(3)
-    gb.cross(0)
+    gb.line(-2), gb.line(2)
     qkv(3)
-    gb.line(-2), gb.line(2)
-    heads_wait()
+    gb.cross(-1), gb.cross(1)
+    gb.close(0)
+    heads_wait(0)
+    gb.line(-3), gb.line(3)
+    gb.cross(-2), gb.cross(2)
+    gb.close(-1), gb.close(1)
+    heads_wait(1)
+    heads_wait(2)
     keep_a = pltpu.make_async_copy(stack, oa_ref, csem.at[0])
     keep_heads = pltpu.make_async_copy(seen, heads, csem.at[1])
     keep_a.start()
@@ -852,8 +1015,9 @@
 
     def attend_at(i, _):
         s, c = i // per_slot, i % per_slot
+        bias = key_bias(lengths_ref[s], seq)
         attend_step(
-            c, seen.at[0, s], seen.at[1, s], seen.at[2, s], bias_ref[s], low.at[s], wide_ref.at[s], lse_ref.at[s], chunk
+            c, seen.at[0, s], seen.at[1, s], seen.at[2, s], bias, low.at[s], wide_ref.at[s], lse_ref.at[s], chunk
         )
 
         @pl.when(c == per_slot - 1)
@@ -864,23 +1028,15 @@
 
         @pl.when(i == 0)
         def _():
-            gb.cross(-1), gb.cross(1)
-
-        @pl.when(i == 3)
+            gb.cross(-3), gb.cross(3)
+
+        @pl.when(i == 4)
         def _():
-            gb.close(0)
-
-        @pl.when(i == 5)
-        def _():
-            gb.line(-3), gb.line(3)
+            gb.close(-2), gb.close(2)
 
         return 0
 
     lax.fori_loop(0, slots * per_slot, attend_at, 0)
-    gb.cross(-2), gb.cross(2)
-    gb.close(-1), gb.close(1)
-    gb.cross(-3), gb.cross(3)
-    gb.close(-2), gb.close(2)
     gb.close(-3), gb.close(3)
     mixed_wait()
     mixed_ref[...] = mixed[...]
@@ -898,11 +1054,11 @@
     gb.finish()
 
 
-def front_call(given, rows_a, rows_b, norm_one, cosine, sine, bias, slots, block_len, collective_id):
+def front_call(given, rows_a, rows_b, tokens, gains, cosine, sine, lengths, slots, block_len, collective_id):
     vmem = pl.BlockSpec(memory_space=pltpu.VMEM)
     any_ = pl.BlockSpec(memory_space=pl.ANY)
     low = jnp.bfloat16
-    width = norm_one.shape[1]
+    width = tokens.shape[1]
     seq = block_len * 8
     my_width = width // 8
     stack_a, stack_b = (jax.ShapeDtypeStruct((64 * r, width), low) for r in (rows_a, rows_b))
@@ -925,9 +1081,10 @@
             jax.ShapeDtypeStruct((slots, seq, my_width), jnp.float32),
             jax.ShapeDtypeStruct((slots, seq, my_width), jnp.float32),
             jax.ShapeDtypeStruct((slots, block_len, width), low),
+            jax.ShapeDtypeStruct((slots * block_len, width), low),
         ),
-        in_specs=[vmem] * 5,
-        out_specs=(any_, any_, any_, vmem, vmem, vmem),
+        in_specs=[vmem] * 5 + [pl.BlockSpec(memory_space=pltpu.SMEM)],
+        out_specs=(any_, any_, any_, vmem, vmem, vmem, vmem),
         scratch_shapes=scratch
         + [DMA((4,)), DMA((4,)), DMA((2,)), DMA((3,)), DMA((3, 8)), DMA((3, 8)), DMA((slots,)), DMA((slots, 8)), DMA((slots, 8))]
         + GATHER_SEMS * 2,
@@ -935,7 +1092,7 @@
             collective_id=collective_id, has_side_effects=True, vmem_limit_bytes=VMEM_BYTES
         ),
         name="spread_and_attend",
-    )(given, norm_one, cosine, sine, bias)
+    )(given, tokens, gains, cosine, sine, lengths)
 
 
 GAIN_SEMS = [DMA((6,)), DMA((6,))]
@@ -978,8 +1135,8 @@
 
 
 def back_kernel(
-    g_ref, qkv_ref, wide_ref, lse_ref, bias_ref, cos_ref, sin_ref, norm_ref, tokens_ref, gains_ref, middle_ref, gain_ref,
-    left_ref, right_ref, w_ref,
+    g_ref, qkv_ref, wide_ref, lse_ref, cos_ref, sin_ref, norm_ref, tokens_ref, gains_ref, middle_ref, gain_ref,
+    left_ref, right_ref, w_ref, lengths_ref,
     oa_ref, ob_ref, og_ref, tok_ref,
     left_got, right_got, norm_got, rows_got, weight_ref, xsend, xrecv, heads, grad, rows, acc_k, acc_v, dnorm, gain, gain_got, gain_all, wsem, gl, gsend, grecv, dl, dsend, drecv, *refs
 ):
@@ -1036,7 +1193,8 @@
 
     right_copy = to_sib(right_ref, right_got, 4)
     norm_copy = to_sib(norm_ref, norm_got, 5)
-    rows_copy = to_sib(rows, rows_got, 6)
+    def rows_copy(s):
+        return to_sib(rows.at[:, s], rows_got.at[:, s], 6 + s)
 
     def given():
         left_copy(0, 1 - core).start()
@@ -1065,14 +1223,16 @@
     cols = 256
     tiles = width // cols
 
-    def rows_wait():
+    def rows_wait(s):
+        back_own(s).wait()
+        for d in range(1, n):
+            back_copy(s, d).wait_recv()
+        rows_copy(s).start()
+
+    def both():
+        norm_copy.wait_recv()
         for s in range(slots):
-            back_own(s).wait()
-            for d in range(1, n):
-                back_copy(s, d).wait_recv()
-        rows_copy.start()
-        norm_copy.wait_recv()
-        rows_copy.wait_recv()
+            rows_copy(s).wait_recv()
 
     def weight(t):
         zb = ra.zb(t)
@@ -1143,8 +1303,8 @@
     def attend_step(i, _):
         s, c = i // per_slot, i % per_slot
         slot = (
-            qkv_ref.at[0, s], qkv_ref.at[1, s], qkv_ref.at[2, s], grad.at[s], wide_ref.at[s], lse_ref.at[s], bias_ref[s],
-            cos_ref, sin_ref, heads.at[0, s], heads.at[1, s], heads.at[2, s], acc_k, acc_v, chunk,
+            qkv_ref.at[0, s], qkv_ref.at[1, s], qkv_ref.at[2, s], grad.at[s], wide_ref.at[s], lse_ref.at[s],
+            key_bias(lengths_ref[s], seq), cos_ref, sin_ref, heads.at[0, s], heads.at[1, s], heads.at[2, s], acc_k, acc_v, chunk,
         )
 
         @pl.when(c == 0)
@@ -1187,7 +1347,9 @@
     rb.one(3, 0)
     rb.one(3, 1)
     rb.tri(2)
-    rows_wait()
+    rows_wait(0)
+    rows_wait(1)
+    both()
     weight(0)
     ra.go1(0, 0)
     ra.go1(0, 1)
@@ -1256,13 +1418,13 @@
             back_copy(s, d).wait_send()
     for t in range(4):
         left_copy(t, 1 - core).wait_send()
-    for copy in (right_copy, norm_copy, rows_copy):
+    for copy in [right_copy, norm_copy] + [rows_copy(s) for s in range(slots)]:
         copy.wait_send()
     ra.finish(), rb.finish(), ga.finish(), gb.finish()
 
 
 def back_call(
-    grad_rows, qkv_heads, wide, lse, bias, cosine, sine, norm_one, tokens, gains, grad_middle, gain_part, left, right, w_qkv, collective_id
+    grad_rows, qkv_heads, wide, lse, cosine, sine, norm_one, tokens, gains, grad_middle, gain_part, left, right, w_qkv, lengths, collective_id
 ):
     any_ = pl.BlockSpec(memory_space=pl.ANY)
     vmem = pl.BlockSpec(memory_space=pltpu.VMEM)
@@ -1280,7 +1442,7 @@
             jax.ShapeDtypeStruct(gain, jnp.float32),
             jax.ShapeDtypeStruct((rows_all, width), low),
         ),
-        in_specs=[vmem] * 14 + [any_],
+        in_specs=[vmem] * 13 + [any_, pl.BlockSpec(memory_space=pltpu.SMEM)],
         out_specs=(any_, any_, vmem, vmem),
         scratch_shapes=[
             pltpu.VMEM((4, rows_all, 8 * rows_b), low),
@@ -1288,8 +1450,8 @@
             pltpu.VMEM((rows_all, width), low),
             pltpu.VMEM((3, slots, block_len, width), low),
             pltpu.VMEM(w_qkv.shape, low),
-            DMA((7,)),
-            DMA((7,)),
+            DMA((6 + slots,)),
+            DMA((6 + slots,)),
             pltpu.VMEM(qkv_heads.shape, low),
             pltpu.VMEM((slots, seq, my_width), low),
             pltpu.VMEM((3, slots, block_len, width), low),
@@ -1315,7 +1477,9 @@
             collective_id=collective_id, has_side_effects=True, vmem_limit_bytes=VMEM_BYTES
         ),
         name="back_and_sum",
-    )(grad_rows, qkv_heads, wide, lse, bias, cosine, sine, norm_one, tokens, gains, grad_middle, gain_part, left, right, w_qkv)
+    )(
+        grad_rows, qkv_heads, wide, lse, cosine, sine, norm_one, tokens, gains, grad_middle, gain_part, left, right, w_qkv, lengths
+    )
 
 
 def to_heads(values):
@@ -1387,17 +1551,9 @@
     def piece_rows(count, pieces):
         return -(-count // (pieces * part_rows)) * part_rows
 
-    positions = ctx * block_len + jnp.arange(block_len, dtype=jnp.int32)
-    tile_heads = 256 // HEAD_DIM
-    cos_rows, sin_rows = rope_tables(jnp.tile(positions, slots), tile_heads)
-    cos_seq, sin_seq = rope_tables(jnp.arange(seq, dtype=jnp.int32), my_width // HEAD_DIM)
-    live_rows = (positions[None, :] < lengths[:, None]).astype(jnp.float32)
-    bias = jnp.where(
-        jnp.arange(seq, dtype=jnp.int32)[None, :] < lengths[:, None], 0.0, mask_fill
-    ).astype(jnp.float32)[:, None, :]
-
-    inputs = tokens.astype(jnp.float32).reshape(rows_all, width)
-    norm_one = layer_norm(inputs, norm_gains[0]).astype(jnp.bfloat16)
+    cos_seq, sin_seq = rope_tables(seq, my_width // HEAD_DIM)
+    flat_tokens = tokens.reshape(rows_all, width)
+
     if fast:
         z, y, x, core = place()
         wanted = jnp.stack(
@@ -1409,8 +1565,8 @@
         per_a, per_b = piece_rows(rows_a, 64), piece_rows(rows_b, 64)
         at_pieces = [units_at(0, per_a, wanted), units_at(1, per_b, wanted)]
         given = pick(*(jnp.concatenate(both) for both in zip(*at_pieces)))
-        stack_a, stack_b, qkv_heads, wide, lse, mixed_low = front_call(
-            given, per_a, per_b, norm_one, cos_rows, sin_rows, bias, slots, block_len, 0
+        stack_a, stack_b, qkv_heads, wide, lse, mixed_low, norm_one = front_call(
+            given, per_a, per_b, flat_tokens, norm_gains, cos_seq, sin_seq, lengths, slots, block_len, 0
         )
     else:
         wanted = ctx * groups + jnp.arange(groups, dtype=jnp.int32)
@@ -1420,67 +1576,38 @@
             own = lax.psum_scatter(share, "shard", scatter_dimension=0, tiled=True)
             stacks.append(lax.all_gather(own, BOTH, axis=0, tiled=True))
         stack_a, stack_b = stacks
+        inputs = flat_tokens.astype(jnp.float32)
+        norm_one = layer_norm(inputs, norm_gains[0]).astype(low)
+        cos_rows, sin_rows = (
+            jnp.tile(lax.dynamic_slice_in_dim(table, ctx * block_len, block_len, 0), (slots, 256 // my_width))
+            for table in (cos_seq, sin_seq)
+        )
         qkv = qkv_call(norm_one, stack_a, cos_rows, sin_rows)
         qkv_heads = to_heads(qkv.reshape(3, slots, block_len, width))
-        mixed_heads, wide, lse = attend_call(qkv_heads, bias)
+        mixed_heads, wide, lse = attend_call(qkv_heads, lengths)
         mixed_low = to_rows(mixed_heads[None])
     mixed_low = mixed_low.reshape(rows_all, width)
-    w_out = stack_b[:width]
-    w_up = stack_b[width : width + 2 * FF_WIDE]
-    w_down = stack_b[width + 2 * FF_WIDE : rows_b]
-
-    middle = inputs + transposed(mixed_low, w_out)
-    norm_two = layer_norm(middle, norm_gains[1]).astype(jnp.bfloat16)
-    upper_proj = transposed(norm_two, w_up)
-    hidden_low = gated_gelu(upper_proj).astype(jnp.bfloat16)
-    result = middle + jnp.dot(hidden_low, w_down, preferred_element_type=jnp.float32)
-    output = result.astype(jnp.bfloat16).reshape(slots, block_len, width)
-
-    grad_result = cotangent.astype(jnp.float32).reshape(rows_all, width) * live_rows.reshape(
-        rows_all, 1
+    left_cols = 64 * piece_rows(rows_b, 64)
+    output, left, right, grad_heads_rows, grad_middle, gain_part = middle_call(
+        mixed_low, flat_tokens, cotangent.reshape(rows_all, width), norm_gains, lengths, stack_b, left_cols, block_len
     )
-    grad_down_low = grad_result.astype(jnp.bfloat16)
-    grad_hidden = transposed(grad_down_low, w_down)
-    _, gelu_back = jax.vjp(gated_gelu, upper_proj)
-    grad_upper_low = gelu_back(grad_hidden)[0].astype(jnp.bfloat16)
-    grad_norm_two = jnp.dot(grad_upper_low, w_up, preferred_element_type=jnp.float32)
-    _, norm_back_two = jax.vjp(layer_norm, middle, norm_gains[1])
-    grad_middle_part, grad_gain_two = norm_back_two(grad_norm_two)
-    grad_middle = grad_result + grad_middle_part
-    grad_attn_low = grad_middle.astype(jnp.bfloat16)
-    grad_heads_rows = jnp.dot(grad_attn_low, w_out, preferred_element_type=jnp.float32).astype(
-        jnp.bfloat16
-    )
+    output = output.reshape(slots, block_len, width)
     grad_heads_rows = grad_heads_rows.reshape(slots, block_len, width)
 
-    gain_part = jnp.zeros((8, width), jnp.float32).at[1].set(grad_gain_two)
     if fast:
-        left = jnp.concatenate(
-            [
-                grad_attn_low,
-                grad_upper_low,
-                hidden_low,
-                jnp.zeros((rows_all, stack_b.shape[0] - rows_b), low),
-            ],
-            axis=1,
-        )
-        right = jnp.stack([mixed_low, norm_two, grad_down_low])
         all_a, all_b, gain_grad, token_grad = back_call(
-            grad_heads_rows, qkv_heads, wide, lse, bias, cos_seq, sin_seq, norm_one, tokens.reshape(rows_all, width),
-            norm_gains, grad_middle, gain_part, left, right, stack_a, 1,
+            grad_heads_rows, qkv_heads, wide, lse, cos_seq, sin_seq, norm_one, flat_tokens,
+            norm_gains, grad_middle, gain_part, left, right, stack_a, lengths, 1,
         )
     else:
+        cuts = (0, width, width + 2 * FF_WIDE, rows_b)
         grads_b = jnp.concatenate(
-            [
-                leading(grad_attn_low, mixed_low).astype(low),
-                leading(grad_upper_low, norm_two).astype(low),
-                leading(hidden_low, grad_down_low).astype(low),
-                jnp.zeros((stack_b.shape[0] - rows_b, width), low),
-            ],
+            [leading(left[:, cuts[i] : cuts[i + 1]], right[i]).astype(low) for i in range(3)]
+            + [jnp.zeros((stack_b.shape[0] - rows_b, width), low)],
             axis=0,
         )
         grad_heads = to_heads(grad_heads_rows[None])[0]
-        grad_qkv_heads = attend_back_call(qkv_heads, grad_heads, wide, lse, bias, cos_seq, sin_seq)
+        grad_qkv_heads = attend_back_call(qkv_heads, grad_heads, wide, lse, lengths, cos_seq, sin_seq)
         grad_qkv_low = to_rows(grad_qkv_heads).reshape(3, rows_all, width)
         grad_norm_one = sum(
             jnp.dot(
@@ -1515,8 +1642,8 @@
     here = (unit_owner == shard) & (rank == jnp.arange(capacity, dtype=jnp.int32)[:, None])
     unit_of_slot = jnp.sum(jnp.where(here, every + 1, 0), axis=1) - 1
     kind = jnp.where(unit_of_slot < 0, -1, (unit_of_slot >= split).astype(jnp.int32))
-    at_a = jnp.maximum(lax.cummax(jnp.where(kind == 0, unit_of_slot, -1)), 0)
-    at_b = jnp.maximum(block_of(lax.cummax(jnp.where(kind == 1, unit_of_slot, -1))), 0)
+    at_a = jnp.where(kind == 0, unit_of_slot, 0)
+    at_b = jnp.where(kind == 1, block_of(unit_of_slot), 0)
     new_master, new_first, new_second = adam_call(
         kind, at_a, at_b, all_a, all_b, master, first_moment, second_moment
     )

time: 521 us -> 486 us (0.933)
  matrix products: 32.1 us -> 0 us
  Pallas kernels: 456 us -> 477 us
  other arithmetic: 26.8 us -> 7.19 us
    dot_general x6 -> x0, matrix products: 32.1 us -> none  [the longest x3 18 us: transposed(): lax.dot_general(left, right, (((1,), (1,)), ((), ())), preferred_element_...]
    pallas_call x0 -> x1, Pallas kernels: none -> 24.4 us  [middle_call(): pl.pallas_call(functools.partial(middle_kernel, tile, block_len), out_sha...]
where the time goes in v4:
time: 486 us
  Pallas kernels  477 us (98%)
  other arithmetic  7.19 us (1%)
    pallas_call x1, Pallas kernels, back_call(): pl.pallas_call(back_kernel, out_shape=(jax.ShapeDtypeStruct(w_qkv.shape,...  246 us
    pallas_call x1, Pallas kernels, front_call(): pl.pallas_call(front_kernel, out_shape=(stack_a, stack_b, jax.ShapeDtypeS...  154 us
    pallas_call x1, Pallas kernels, adam_call(): pl.pallas_call(functools.partial(adam_kernel, per), grid_spec=pltpu.Prefe...  46.1 us
    pallas_call x1, Pallas kernels, middle_call(): pl.pallas_call(functools.partial(middle_kernel, tile, block_len), out_sha...  24.4 us

profile of v4, /device:TPU:0, one launch (start us, length us, event | category | flops | bytes accessed | tf_op | source)
XLA Modules:
  0.0 486.1 jit_solution(3991402231525749599)
XLA Ops:
  0.7 0.1 add_bitcast_fusion.2
  0.7 0.1 add_bitcast_fusion.4
  0.8 0.7 broadcast_compare_fusion
  1.5 0.8 select_reduce_fusion
  2.3 0.9 convert_reduce_fusion
  3.2 0.1 select_reduce_fusion.2
  3.3 0.6 compare_select_fusion.2
  3.9 0.1 iota_add_fusion.1
  4.0 0.1 add.165
  4.1 0.1 iota_add_fusion
  4.1 0.1 add.169
  4.3 0.1 pad_add_fusion.1
  4.3 0.9 select_reduce_fusion.1
  5.2 0.9 convert_reduce_fusion.1
  6.1 0.6 and_select_fusion.3.part_ref
  6.7 6.5 %pick.1.given_ref = bf16[1536,1024]{1,0:T(8,128)(2,1)} custom-call(s32[96]{0:T(128)} %and_select_fusion.3.part_ref, f32[280,16,1024]{2,1,0:T(8,128)} %bitcast.43), custom_call_target="tpu_custom_call" | custom-call | tf_op jit(solution)/shard_map/pick/pallas_call | solution.py:479
  13.2 154.2 %spread_and_attend.1 = (bf16[3072,1024]{1,0:T(8,128)(2,1)}, bf16[9216,1024]{1,0:T(8,128)(2,1)}, bf16[3,2,1024,128]{3,2,1,0:T(8,128)(2,1)}, f32[2,1024,128]{2,1,0...) custom-call(bf16[1536,1024]{1,0:T(8,128)(2,1)} %pick.1.given_ref, ...), custom_call_target="tpu_custom_call" | custom-call | tf_op jit(solution)/shard_map/spread_and_attend/pallas_call | solution.py:1075
  167.4 0.0 copy-start.1
  167.4 0.0 copy-start.2
  167.4 0.0 copy-start.3
  167.4 24.4 %middle.1 = (bf16[256,1024]{1,0:T(8,128)(2,1)}, bf16[256,9216]{1,0:T(8,128)(2,1)}, bf16[3,256,1024]{2,1,0:T(8,128)(2,1)}, bf16[256,1024]{1,0:T(8,128)(2,1)}, f32[256,1024]{1,0:T(8,128)}, /*index=5*/f32[8,1024]{1,0:T(8,128)}) custom-call(bf16[256,1024]{1,0:T(8,128)(2,1)} %bitcast.49, bf16[256,1024]{1,0:T(8,128)(2,1)} %bitcast.45, bf16[256,1024]{1,0:T(8,128)(2,1)} %bitcast.47, ...), custom_call_target="tpu_custom_call" | custom-call | tf_op jit(solution)/shard_map/middle/pallas_call | solution.py:383
  191.8 245.9 %back_and_sum.1 = (bf16[3072,1024]{1,0:T(8,128)(2,1)}, bf16[9216,1024]{1,0:T(8,128)(2,1)}, f32[8,1024]{1,0:T(8,128)}, bf16[256,1024]{1,0:T(8,128)(2,1)}) custom-call(bf16[2,128,1024]{2,1,0:T(8,128)(2,1)} %bitcast.48, bf16[3,2,1024,128]{3,2,1,0:T(8,128)(2,1)} %get-tuple-element.32.qkv_ref, f32[2,1024,128]{2,1,0:T(8,128)} %get-tuple-element.33.wide_ref, ...), custom_call_target="tpu_custom_call" | custom-call | tf_op jit(solution)/shard_map/back_and_sum/pallas_call | solution.py:1437
  437.8 0.0 copy-done.1
  437.8 0.0 copy-done.2
  437.8 0.0 copy-done.3
  437.8 1.4 multiply_subtract_fusion
  439.2 0.0 copy-start
  439.2 46.1 %adamw.1 = (f32[70,64,1024]{2,1,0:T(8,128)}, f32[70,64,1024]{2,1,0:T(8,128)}, f32[70,64,1024]{2,1,0:T(8,128)}) custom-call(s32[70]{0:T(128)} %get-tuple-element.55.unit_ref, s32[70]{0:T(128)} %get-tuple-element.54.a_ref, s32[70]{0:T(128)} %get-tuple-element.53.b_ref, bf16[48,64,1024]{2,1,0:T(8,128)(2,1)} %bitcast.36, bf16[48,64,1024]{2,1,0:T(8,128)(2,1)} %bitcast.37, ...), custom_call_target="tpu_custom_call" | custom-call | tf_op jit(solution)/shard_map/adamw/pallas_call | solution.py:430
  485.3 0.0 copy-done
  485.3 0.8 copy.21
  (6 shorter events, 0.1 us)
Async XLA Ops:
  167.4 270.4 %copy-start.1 = (f32[2,1024]{1,0:T(2,128)S(1)}, f32[2,1024]{1,0:T(2,128)}, u32[]{:S(2)}) copy-start(f32[2,1024]{1,0:T(2,128)} %gains_ref.5) | copy-start | bytes 24580
  167.4 270.4 %copy-start.2 = (f32[2,1024]{1,0:T(2,128)S(1)}, f32[2,1024]{1,0:T(2,128)}, u32[]{:S(2)}) copy-start(f32[2,1024]{1,0:T(2,128)} %param.20) | copy-start | bytes 24580
  167.4 270.4 %copy-start.3 = (f32[2,1024]{1,0:T(2,128)S(1)}, f32[2,1024]{1,0:T(2,128)}, u32[]{:S(2)}) copy-start(f32[2,1024]{1,0:T(2,128)} %param.21) | copy-start | bytes 24580
  439.2 46.1 %copy-start = (bf16[256,1024]{1,0:T(8,128)(2,1)S(1)}, bf16[256,1024]{1,0:T(8,128)(2,1)}, u32[]{:S(2)}) copy-start(bf16[256,1024]{1,0:T(8,128)(2,1)} %get-tuple-element.41) | copy-start | bytes 1572868

commit v5 on v4

--- a/solution.py
+++ b/solution.py
@@ -71,11 +71,11 @@
     return jnp.where(lane % HEAD_DIM < half, ahead, behind)
 
 
-def unit_places(unit_owner, chosen):
+def own_places(unit_owner, owner, chosen):
     every = jnp.arange(unit_owner.shape[0], dtype=jnp.int32)
-    owner = jnp.sum(jnp.where(every == chosen[:, None], unit_owner, 0), axis=1)
-    below = (every < chosen[:, None]) & (unit_owner == owner[:, None])
-    return owner, jnp.sum(below.astype(jnp.int32), axis=1)
+    held = unit_owner == owner
+    mine = jnp.any((every == chosen[:, None]) & held, axis=1)
+    return mine, jnp.sum(((every < chosen[:, None]) & held).astype(jnp.int32), axis=1)
 
 
 def adam_update(weight, gradient, first_old, second_old, step_rate, weight_decay):
@@ -377,7 +377,7 @@
 def middle_call(mixed, tokens, cotangent, gains, lengths, stack_b, left_cols, block_len):
     rows_all, width = tokens.shape
     low = jnp.bfloat16
-    tile = 384
+    tile = 896 if FF_WIDE % 896 == 0 else 128
     tiles = FF_WIDE // tile
     vmem = pl.BlockSpec(memory_space=pltpu.VMEM)
     return pl.pallas_call(
@@ -403,7 +403,18 @@
 
 def adam_kernel(per, unit_ref, a_ref, b_ref, *refs):
     grads = (refs[:per], refs[per : 2 * per])
-    master, first, second, new_master, new_first, new_second = refs[2 * per :]
+    gain_grad, *gains = refs[2 * per : 2 * per + 4]
+    master, first, second, new_master, new_first, new_second, *new_gains = refs[2 * per + 4 :]
+
+    @pl.when(pl.program_id(0) == 0)
+    def _():
+        rows = gains[0].shape[0]
+        updated = adam_update(
+            gains[0][...], gain_grad[0:rows, :], gains[1][...], gains[2][...], rate_gain, 0.0
+        )
+        for ref, value in zip(new_gains, updated):
+            ref[...] = value
+
     for j in range(per):
         slot = pl.program_id(0) * per + j
         unit = unit_ref[slot]
@@ -417,7 +428,7 @@
         new_second[j] = two
 
 
-def adam_call(kind, at_a, at_b, grads_a, grads_b, master, first, second):
+def adam_call(kind, at_a, at_b, grads_a, grads_b, gain_grad, gains, master, first, second):
     capacity, rows, width = master.shape
     per = max(p for p in range(1, 8) if capacity % p == 0)
 
@@ -425,6 +436,9 @@
         return pl.BlockSpec(
             (1, rows, width), lambda i, kind, *at: (at[chunk][i * per + j], 0, 0)
         )
+
+    def whole(array):
+        return pl.BlockSpec(array.shape, lambda i, kind, *at: (0, 0))
 
     slot_spec = pl.BlockSpec((per, rows, width), lambda i, kind, *at: (i, 0, 0))
     return pl.pallas_call(
@@ -432,13 +446,15 @@
         grid_spec=pltpu.PrefetchScalarGridSpec(
             num_scalar_prefetch=3,
             grid=(capacity // per,),
-            in_specs=[unit_spec(j, c) for c in range(2) for j in range(per)] + [slot_spec] * 3,
-            out_specs=[slot_spec] * 3,
+            in_specs=[unit_spec(j, c) for c in range(2) for j in range(per)]
+            + [whole(a) for a in (gain_grad, *gains)]
+            + [slot_spec] * 3,
+            out_specs=[slot_spec] * 3 + [whole(a) for a in gains],
         ),
-        out_shape=[jax.ShapeDtypeStruct(master.shape, jnp.float32)] * 3,
+        out_shape=[jax.ShapeDtypeStruct(a.shape, jnp.float32) for a in (master, first, second, *gains)],
         compiler_params=pltpu.CompilerParams(vmem_limit_bytes=VMEM_BYTES),
         name="adamw",
-    )(kind, at_a, at_b, *([grads_a] * per), *([grads_b] * per), master, first, second)
+    )(kind, at_a, at_b, *([grads_a] * per), *([grads_b] * per), gain_grad, *gains, master, first, second)
 
 
 def pick_kernel(part_ref, master_ref, out_ref, got, sems):
@@ -755,15 +771,13 @@
         self.add(self.base(zb) + h * 4 + a * 2 + b, self.got3, slot * 2 + h, 1)
 
     def add(self, at, ref, start, count):
-        step = 48
-
         def body(i, _):
-            to = pl.ds(pl.multiple_of(at * self.rows + i * step, 16), step)
-            given = pl.ds(pl.multiple_of(start * self.rows + i * step, 16), step)
+            to = pl.ds(pl.multiple_of((at + i) * self.rows, 16), self.rows)
+            given = pl.ds(pl.multiple_of((start + i) * self.rows, 16), self.rows)
             self.acc[to, :] = self.acc[to, :] + ref[given, :]
             return 0
 
-        lax.fori_loop(0, count * self.rows // step, body, 0)
+        lax.fori_loop(0, count, body, 0)
 
     def go1(self, t, q):
         for h in range(2):
@@ -786,20 +800,24 @@
             self.send2(t, h).wait_recv()
             self.add(self.base(zb) + h * 4 + a * 2 + b, self.got2, zb * 2 + h, 1)
 
-    def tri(self, t):
+    def tri(self, t, first):
         zb = self.zb(t)
         z = self.z
+        inner = ((zb > z) & (z > 0)) | ((zb < z) & (z < 3))
         for h in range(2):
-
-            @pl.when(((zb > z) & (z > 0)) | ((zb < z) & (z < 3)))
-            def _():
-                self.come3(zb, h)
-
-            @pl.when(zb > z)
+            if not first:
+
+                @pl.when(inner)
+                def _():
+                    self.come3(zb, h)
+
+            now = jnp.logical_not(inner) if first else inner
+
+            @pl.when((zb > z) & now)
             def _():
                 self.send3(t, h, True).start()
 
-            @pl.when(zb < z)
+            @pl.when((zb < z) & now)
             def _():
                 self.send3(t, h, False).start()
 
@@ -829,10 +847,171 @@
                     remote(ref, ref, self.s3.at[t, h], self.r3.at[0, h], self.xn).wait_send()
 
 
+LATE_GATHER_SEMS = [DMA] + [DMA((3, 4))] * 2 + [DMA((3,))] * 2 + [DMA((4,))] * 2
+
+
+class LateGather:
+    def __init__(self, own, buf, rows, sems):
+        self.own, self.buf, self.rows = own, buf, rows
+        self.lsem, self.zs, self.zr, self.fs, self.fr, self.ss, self.sr = sems
+        self.meet()
+
+    def meet(self):
+        self.z, self.y, self.x, self.core = z, y, x, core = place()
+        self.xn = device_at(z, y, 1 - x, core)
+        self.yn = device_at(z, 1 - y, x, core)
+        self.sib = device_at(z, y, x, 1 - core)
+
+    def one_of(self, y, x):
+        return rows_at(self.buf, ((self.z * 2 + self.core) * 2 + y) * 2 + x, 1, self.rows)
+
+    def block(self, zb, c):
+        return rows_at(self.buf, (zb * 2 + c) * 4, 4, self.rows)
+
+    def hand(self, i, mine):
+        y, x = self.y, self.x
+        at = ((y, x) if mine else (1 - y, x), (y, x) if mine else (y, 1 - x), (1 - y, x if mine else 1 - x))[i]
+        ref = self.one_of(*at)
+        src = self.own() if mine and i < 2 else ref
+        return remote(src, ref, self.fs.at[i], self.fr.at[i], self.yn if i == 0 else self.xn)
+
+    def keep(self):
+        return pltpu.make_async_copy(self.own(), self.one_of(self.y, self.x), self.lsem)
+
+    def start(self):
+        self.keep().start()
+        self.hand(0, True).start()
+        self.hand(1, True).start()
+        self.keep().wait()
+
+    def pass_on(self):
+        self.hand(0, False).wait_recv()
+        self.hand(2, True).start()
+
+    def far_copy(self, d, i, zb):
+        ref = rows_at(self.buf, (zb * 2 + self.core) * 4 + i, 1, self.rows)
+        to = device_at((self.z + d) % 4, self.y, self.x, self.core)
+        return remote(ref, ref, self.zs.at[d - 1, i], self.zr.at[d - 1, i], to)
+
+    def far(self, d, i):
+        self.far_copy(d, i, self.z).start()
+
+    def whole(self, zb, c):
+        ref = self.block(zb, c)
+        return remote(ref, ref, self.ss.at[zb], self.sr.at[zb], self.sib)
+
+    def ready(self):
+        self.hand(1, False).wait_recv()
+        self.hand(2, False).wait_recv()
+        self.whole(self.z, self.core).start()
+
+    def come(self, d):
+        zb = (self.z - d) % 4
+        for i in range(4):
+            self.far_copy(d, i, zb).wait_recv()
+        self.whole(zb, self.core).start()
+
+    def finish(self):
+        for i in range(3):
+            self.hand(i, True).wait_send()
+            for k in range(4):
+                self.far_copy(i + 1, k, self.z).wait_send()
+        for zb in range(4):
+            self.whole(zb, self.core).wait_send()
+            self.whole(zb, 1 - self.core).wait_recv()
+
+
+LATE_REDUCE_REFS = 8
+ROWS_C = 32
+
+
+def late_reduce_scratch(rows, width):
+    def buf(n):
+        return pltpu.VMEM((n * rows, width), jnp.bfloat16)
+
+    return [buf(16), buf(2), buf(1), buf(12), DMA((3,)), DMA((3,)), DMA((3, 4)), DMA((3, 4))]
+
+
+class LateReduce:
+    def __init__(self, rows, refs):
+        self.acc, self.got1, self.got2, self.got3 = refs[:4]
+        self.s1, self.r1, self.s3, self.r3 = refs[4:]
+        self.rows = rows
+        self.meet()
+
+    def meet(self):
+        self.z, self.y, self.x, self.core = z, y, x, core = place()
+        self.xn = device_at(z, y, 1 - x, core)
+        self.yn = device_at(z, 1 - y, x, core)
+        self.sib = device_at(z, y, x, 1 - core)
+    def add(self, to, given):
+        rows = self.rows
+
+        def body(i, _):
+            at = pl.ds(pl.multiple_of(i * rows, 16), rows)
+            to[at, :] = to[at, :] + given[at, :]
+            return 0
+
+        lax.fori_loop(0, to.shape[0] // rows, body, 0)
+
+    def part(self, zb, at, count=1):
+        return rows_at(self.acc, zb * 4 + at, count, self.rows)
+
+    def far_copy(self, d, i):
+        zb = (self.z + d) % 4
+        return remote(
+            self.part(zb, i),
+            rows_at(self.got3, (d - 1) * 4 + i, 1, self.rows),
+            self.s3.at[d - 1, i],
+            self.r3.at[d - 1, i],
+            device_at(zb, self.y, self.x, self.core),
+        )
+
+    def far(self, d, i):
+        self.far_copy(d, i).start()
+
+    def to_x(self, yb):
+        src = self.part(self.z, yb * 2 + 1 - self.x)
+        return remote(src, rows_at(self.got1, yb, 1, self.rows), self.s1.at[yb], self.r1.at[yb], self.xn)
+
+    def to_y(self):
+        src = self.part(self.z, (1 - self.y) * 2 + self.x)
+        return remote(src, self.got2, self.s1.at[2], self.r1.at[2], self.yn)
+
+    def three(self):
+        for d in (1, 2, 3):
+            for i in range(4):
+                self.far_copy(d, i).wait_recv()
+            self.add(self.part(self.z, 0, 4), rows_at(self.got3, (d - 1) * 4, 4, self.rows))
+        for yb in range(2):
+            self.to_x(yb).start()
+
+    def one(self):
+        for yb in range(2):
+            self.to_x(yb).wait_recv()
+            self.add(self.part(self.z, yb * 2 + self.x), rows_at(self.got1, yb, 1, self.rows))
+        self.to_y().start()
+
+    def two(self):
+        self.to_y().wait_recv()
+        self.add(self.own(), self.got2)
+
+    def own(self):
+        return self.part(self.z, self.y * 2 + self.x)
+
+    def finish(self):
+        for yb in range(2):
+            self.to_x(yb).wait_send()
+        self.to_y().wait_send()
+        for d in (1, 2, 3):
+            for i in range(4):
+                self.far_copy(d, i).wait_send()
+
+
 def front_kernel(
     given_ref, tokens_ref, gains_ref, cos_ref, sin_ref, lengths_ref,
     oa_ref, ob_ref, heads, wide_ref, lse_ref, mixed_ref, norm_ref,
-    stack, rows, seen, low, mixed, got_a, got_b, new_a, new_b, own_a, own_b, send, recv, csem, ql, qsend, qrecv, ml, msend, mrecv, *sems
+    stack, rows, seen, low, mixed, got_a, got_b, new_a, new_b, own_a, own_b, got_c, new_c, own_c, send, recv, csem, ql, qsend, qrecv, ml, msend, mrecv, *sems
 ):
     n = 8
     z, y, x, core = place()
@@ -840,11 +1019,18 @@
     m = len(GATHER_SEMS)
     rows_a, rows_b = own_a.shape[0] // 2, own_b.shape[0] // 2
     ga = Gather(lambda h: rows_at(own_a, h, 1, rows_a), stack, rows_a, sems[:m])
-    gb = Gather(lambda h: rows_at(own_b, h, 1, rows_b), ob_ref, rows_b, sems[m:])
+    rows_c = own_c.shape[0]
+    start_c = 64 * rows_b
+    gb = Gather(lambda h: rows_at(own_b, h, 1, rows_b), ob_ref.at[pl.ds(0, start_c)], rows_b, sems[m : 2 * m])
+    gc = LateGather(lambda: own_c, ob_ref.at[pl.ds(start_c, 32 * rows_c)], rows_c, sems[2 * m :])
     _, slots, block_len, width = rows.shape
     seq, my_width = seen.shape[2:]
     greet([ga.xn, ga.sib] + [(lax.rem(ctx + d, n), shard) for d in range(1, n)])
-    jobs = ((0, got_a, new_a, own_a), (8 * rows_a, got_b, new_b, own_b))
+    jobs = (
+        (0, got_a, new_a, own_a),
+        (8 * rows_a, got_b, new_b, own_b),
+        (8 * (rows_a + rows_b), got_c, new_c, own_c),
+    )
 
     def share(i, c, xb):
         start, got, new, own = jobs[i]
@@ -863,7 +1049,7 @@
 
     def to_x(i):
         start, got, new, own = jobs[i]
-        return remote(got.at[held(i, 1 - x)], new, send.at[2 + i], recv.at[2 + i], ga.xn)
+        return remote(got.at[held(i, 1 - x)], new, send.at[3 + i], recv.at[3 + i], ga.xn)
 
     def spread(i):
         start, got, new, own = jobs[i]
@@ -971,19 +1157,23 @@
             for d in range(1, n):
                 mixed_copy(s, d).wait_recv()
 
-    for i in range(2):
+    for i in range(3):
         to_core(i).start()
     spread(0)
     spread(1)
+    spread(2)
     cross(0)
     ga.start()
     norm()
     ga.line(-1), ga.line(1)
     ga.cross(0)
+    cross(2)
+    gc.start()
     ga.line(-2), ga.line(2)
     cross(1)
     gb.start()
     ga.cross(-1), ga.cross(1)
+    gc.pass_on()
     ga.close(0)
     ga.line(-3), ga.line(3)
     ga.cross(-2), ga.cross(2)
@@ -992,16 +1182,29 @@
     ga.close(-1), ga.close(1)
     ga.cross(-3), ga.cross(3)
     qkv(1)
+    gc.ready()
+    gc.far(2, 0)
+    gc.far(1, 0)
     gb.cross(0)
+    gc.far(3, 0)
+    gc.far(2, 1)
     ga.close(-2), ga.close(2)
     qkv(2)
     ga.close(-3), ga.close(3)
     gb.line(-2), gb.line(2)
+    gc.far(1, 1)
+    gc.far(3, 1)
     qkv(3)
     gb.cross(-1), gb.cross(1)
+    gc.far(2, 2)
+    gc.far(1, 2)
     gb.close(0)
+    gc.far(3, 2)
+    gc.far(2, 3)
     heads_wait(0)
     gb.line(-3), gb.line(3)
+    gc.far(1, 3)
+    gc.far(3, 3)
     gb.cross(-2), gb.cross(2)
     gb.close(-1), gb.close(1)
     heads_wait(1)
@@ -1029,20 +1232,23 @@
         @pl.when(i == 0)
         def _():
             gb.cross(-3), gb.cross(3)
+            gc.come(1)
 
         @pl.when(i == 4)
         def _():
             gb.close(-2), gb.close(2)
+            gc.come(3)
 
         return 0
 
     lax.fori_loop(0, slots * per_slot, attend_at, 0)
     gb.close(-3), gb.close(3)
+    gc.come(2)
     mixed_wait()
     mixed_ref[...] = mixed[...]
     keep_a.wait()
     keep_heads.wait()
-    for i in range(2):
+    for i in range(3):
         to_core(i).wait_send()
         to_x(i).wait_send()
     for d in range(1, n):
@@ -1052,16 +1258,19 @@
             mixed_copy(s, d).wait_send()
     ga.finish(False)
     gb.finish()
-
-
-def front_call(given, rows_a, rows_b, tokens, gains, cosine, sine, lengths, slots, block_len, collective_id):
+    gc.finish()
+
+
+def front_call(given, rows_a, rows_b, rows_c, tokens, gains, cosine, sine, lengths, slots, block_len, collective_id):
     vmem = pl.BlockSpec(memory_space=pltpu.VMEM)
     any_ = pl.BlockSpec(memory_space=pl.ANY)
     low = jnp.bfloat16
     width = tokens.shape[1]
     seq = block_len * 8
     my_width = width // 8
-    stack_a, stack_b = (jax.ShapeDtypeStruct((64 * r, width), low) for r in (rows_a, rows_b))
+    stack_a, stack_b = (
+        jax.ShapeDtypeStruct((r, width), low) for r in (64 * rows_a, 64 * rows_b + 32 * rows_c)
+    )
     scratch = [
         pltpu.VMEM(stack_a.shape, low),
         pltpu.VMEM((3, slots, block_len, width), low),
@@ -1072,6 +1281,7 @@
     for pieces in (4, 2, 2):
         for r in (rows_a, rows_b):
             scratch.append(pltpu.VMEM((pieces * r, width), low))
+    scratch += [pltpu.VMEM((pieces * rows_c, width), low) for pieces in (2, 1, 1)]
     return pl.pallas_call(
         front_kernel,
         out_shape=(
@@ -1086,8 +1296,9 @@
         in_specs=[vmem] * 5 + [pl.BlockSpec(memory_space=pltpu.SMEM)],
         out_specs=(any_, any_, any_, vmem, vmem, vmem, vmem),
         scratch_shapes=scratch
-        + [DMA((4,)), DMA((4,)), DMA((2,)), DMA((3,)), DMA((3, 8)), DMA((3, 8)), DMA((slots,)), DMA((slots, 8)), DMA((slots, 8))]
-        + GATHER_SEMS * 2,
+        + [DMA((6,)), DMA((6,)), DMA((2,)), DMA((3,)), DMA((3, 8)), DMA((3, 8)), DMA((slots,)), DMA((slots, 8)), DMA((slots, 8))]
+        + GATHER_SEMS * 2
+        + LATE_GATHER_SEMS,
         compiler_params=pltpu.CompilerParams(
             collective_id=collective_id, has_side_effects=True, vmem_limit_bytes=VMEM_BYTES
         ),
@@ -1138,7 +1349,7 @@
     g_ref, qkv_ref, wide_ref, lse_ref, cos_ref, sin_ref, norm_ref, tokens_ref, gains_ref, middle_ref, gain_ref,
     left_ref, right_ref, w_ref, lengths_ref,
     oa_ref, ob_ref, og_ref, tok_ref,
-    left_got, right_got, norm_got, rows_got, weight_ref, xsend, xrecv, heads, grad, rows, acc_k, acc_v, dnorm, gain, gain_got, gain_all, wsem, gl, gsend, grecv, dl, dsend, drecv, *refs
+    left_got, late_got, right_got, norm_got, rows_got, weight_ref, xsend, xrecv, heads, grad, rows, acc_k, acc_v, dnorm, gain, gain_got, gain_all, wsem, gl, gsend, grecv, dl, dsend, drecv, *refs
 ):
     n = 8
     slots, block_len, width = g_ref.shape
@@ -1146,13 +1357,18 @@
     chunk = 256
     per_slot = seq // chunk
     m = len(GATHER_SEMS)
-    rows_a, rows_b = oa_ref.shape[0] // 64, ob_ref.shape[0] // 64
+    rows_a, rows_b, rows_c = oa_ref.shape[0] // 64, left_got.shape[2] // 8, late_got.shape[2] // 4
+    start_c = 64 * rows_b
     ra = Reduce(rows_a, refs[:REDUCE_REFS])
     rb = Reduce(rows_b, refs[REDUCE_REFS : 2 * REDUCE_REFS])
     refs = refs[2 * REDUCE_REFS :]
+    rc = LateReduce(rows_c, refs[:LATE_REDUCE_REFS])
+    refs = refs[LATE_REDUCE_REFS:]
     ga = Gather(ra.own, oa_ref, rows_a, refs[:m])
-    gb = Gather(rb.own, ob_ref, rows_b, refs[m : 2 * m])
-    gs = GainSum(gain, gain_got, gain_all, refs[2 * m :])
+    gb = Gather(rb.own, ob_ref.at[pl.ds(0, start_c)], rows_b, refs[m : 2 * m])
+    refs = refs[2 * m :]
+    gc = LateGather(rc.own, ob_ref.at[pl.ds(start_c, 32 * rows_c)], rows_c, refs[: len(LATE_GATHER_SEMS)])
+    gs = GainSum(gain, gain_got, gain_all, refs[len(LATE_GATHER_SEMS) :])
     z, y, x, core = place()
     ctx, shard = lax.axis_index("ctx"), lax.axis_index("shard")
     greet([ra.xn, ra.sib] + [(lax.rem(ctx + d, n), shard) for d in range(1, n)])
@@ -1187,9 +1403,15 @@
     def to_sib(src, dst, i):
         return remote(src, dst, xsend.at[i], xrecv.at[i], ra.sib)
 
+    region_b, region_c = 8 * rows_b, 4 * rows_c
+
     def left_copy(t, c):
-        lane = pl.ds(pl.multiple_of((rb.zb(t) * 2 + c) * 8 * rows_b, cut), 8 * rows_b)
+        lane = pl.ds(pl.multiple_of((rb.zb(t) * 2 + c) * region_b, cut), region_b)
         return to_sib(left_ref.at[:, lane], left_got.at[rb.zb(t)], t)
+
+    def late_copy(zb, c):
+        lane = pl.ds(pl.multiple_of(start_c + (zb * 2 + c) * region_c, cut), region_c)
+        return to_sib(left_ref.at[:, lane], late_got.at[zb], 6 + slots + zb)
 
     right_copy = to_sib(right_ref, right_got, 4)
     norm_copy = to_sib(norm_ref, norm_got, 5)
@@ -1197,29 +1419,44 @@
         return to_sib(rows.at[:, s], rows_got.at[:, s], 6 + s)
 
     def given():
+        right_copy.start()
         left_copy(0, 1 - core).start()
-        right_copy.start()
+        for t in range(4):
+            late_copy(t, 1 - core).start()
         for t in range(1, 4):
             left_copy(t, 1 - core).start()
         norm_copy.start()
         right_copy.wait_recv()
 
-    def fill(t):
-        zb = rb.zb(t)
-        left_copy(t, core).wait_recv()
-        count = 8 * rows_b // cut
+    def product(zb, start, region, got, acc):
+        count = region // cut
 
         def step(i, _):
-            g = (zb * 2 + core) * count + i
+            g = start // cut + (zb * 2 + core) * count + i
             kind = (g >= width // cut).astype(jnp.int32) + (g >= (width + 2 * FF_WIDE) // cut).astype(jnp.int32)
             mine = left_ref[:, pl.ds(pl.multiple_of(g * cut, cut), cut)]
-            other = left_got[zb, :, pl.ds(pl.multiple_of(i * cut, cut), cut)]
+            other = got[zb, :, pl.ds(pl.multiple_of(i * cut, cut), cut)]
             total = leading(mine, right_ref[kind]) + leading(other, right_got[kind])
-            at = pl.ds(pl.multiple_of(zb * 8 * rows_b + i * cut, cut), cut)
-            rb.acc[at, :] = total.astype(jnp.bfloat16)
+            at = pl.ds(pl.multiple_of((zb * count + i) * cut, cut), cut)
+            acc[at, :] = total.astype(jnp.bfloat16)
             return 0
 
         lax.fori_loop(0, count, step, 0)
+
+    def fill(t):
+        left_copy(t, core).wait_recv()
+        product(rb.zb(t), 0, region_b, left_got, rb.acc)
+
+    def late():
+        for zb in range(4):
+            late_copy(zb, core).wait_recv()
+
+        def step(zb, _):
+            product(zb, start_c, region_c, late_got, rc.acc)
+            return 0
+
+        lax.fori_loop(0, 4, step, 0)
+
     cols = 256
     tiles = width // cols
 
@@ -1295,6 +1532,7 @@
     fill(1)
     fill(2)
     fill(3)
+    late()
     w_copy.start()
     go_own.wait()
     for d in range(1, n):
@@ -1336,17 +1574,26 @@
     rb.go1(2, 0)
     rb.one(1, 1)
     rb.go1(2, 1)
-    rb.tri(0)
+    rc.far(2, 0)
+    rc.far(1, 0)
+    rb.tri(0, 1)
+    rb.tri(0, 0)
     rb.two(1)
     rb.one(2, 0)
     rb.go1(3, 0)
     rb.one(2, 1)
     rb.go1(3, 1)
-    rb.tri(1)
+    rc.far(3, 0)
+    rc.far(2, 1)
+    rb.tri(1, 1)
+    rb.tri(1, 0)
     rb.two(2)
     rb.one(3, 0)
     rb.one(3, 1)
-    rb.tri(2)
+    rc.far(1, 1)
+    rc.far(3, 1)
+    rb.tri(2, 1)
+    rb.tri(2, 0)
     rows_wait(0)
     rows_wait(1)
     both()
@@ -1356,6 +1603,9 @@
     weight(1)
     ra.go1(1, 0)
     ra.go1(1, 1)
+    rc.far(2, 2)
+    rc.far(1, 2)
+    rc.far(3, 2)
     rb.two(3)
     weight(2)
     ra.go1(2, 0)
@@ -1363,6 +1613,9 @@
     weight(3)
     ra.go1(3, 0)
     ra.go1(3, 1)
+    rc.far(2, 3)
+    rc.far(1, 3)
+    rc.far(3, 3)
     ra.one(0, 0)
     ra.one(0, 1)
     rb.three()
@@ -1371,39 +1624,62 @@
     ra.one(1, 0)
     ra.one(1, 1)
     ra.two(0)
+    rc.three()
     ra.one(2, 0)
     ra.one(2, 1)
-    ra.tri(0)
+    ra.tri(0, 1)
+    ra.tri(0, 0)
     ra.two(1)
+    rc.one()
     gb.line(-1), gb.line(1)
     ra.one(3, 0)
     ra.one(3, 1)
-    ra.tri(1)
+    ra.tri(1, 1)
+    ra.tri(1, 0)
     ra.two(2)
     gb.cross(0)
+    rc.two()
+    gc.start()
     gs.end(0)
     gs.begin(1)
-    ra.tri(2)
+    ra.tri(2, 1)
+    ra.tri(2, 0)
     ra.two(3)
     gb.line(-2), gb.line(2)
+    gc.pass_on()
     ra.three()
     ga.start()
+    gc.ready()
+    gc.far(2, 0)
+    gc.far(1, 0)
+    gc.far(3, 0)
     gb.cross(-1), gb.cross(1)
     gs.end(1)
     gs.begin(2)
     gb.close(0)
+    gc.far(2, 1)
+    gc.far(1, 1)
+    gc.far(3, 1)
     gb.line(-3), gb.line(3)
+    gc.far(2, 2)
+    gc.far(1, 2)
+    gc.far(3, 2)
     ga.line(-1), ga.line(1)
     gb.cross(-2), gb.cross(2)
+    gc.far(2, 3)
+    gc.far(1, 3)
+    gc.far(3, 3)
     gs.end(2)
     gs.begin_far()
     ga.cross(0)
     gb.close(-1), gb.close(1)
     ga.line(-2), ga.line(2)
     gb.cross(-3), gb.cross(3)
+    gc.come(1)
     ga.cross(-1), ga.cross(1)
     ga.close(0)
     gb.close(-2), gb.close(2)
+    gc.come(3)
     ga.line(-3), ga.line(3)
     ga.cross(-2), ga.cross(2)
     ga.close(-1), ga.close(1)
@@ -1411,6 +1687,7 @@
     ga.cross(-3), ga.cross(3)
     ga.close(-2), ga.close(2)
     ga.close(-3), ga.close(3)
+    gc.come(2)
     gs.end_far(og_ref)
     for d in range(1, n):
         go_copy(d).wait_send()
@@ -1418,9 +1695,11 @@
             back_copy(s, d).wait_send()
     for t in range(4):
         left_copy(t, 1 - core).wait_send()
+        late_copy(t, 1 - core).wait_send()
     for copy in [right_copy, norm_copy] + [rows_copy(s) for s in range(slots)]:
         copy.wait_send()
-    ra.finish(), rb.finish(), ga.finish(), gb.finish()
+    ra.finish(), rb.finish(), rc.finish()
+    ga.finish(), gb.finish(), gc.finish()
 
 
 def back_call(
@@ -1433,12 +1712,13 @@
     seq, my_width = qkv_heads.shape[2:]
     rows_all = slots * block_len
     gain = gain_part.shape
-    rows_a, rows_b = w_qkv.shape[0] // 64, left.shape[1] // 64
+    rows_a, rows_c = w_qkv.shape[0] // 64, ROWS_C
+    rows_b = left.shape[1] // 64 - rows_c // 2
     return pl.pallas_call(
         back_kernel,
         out_shape=(
             jax.ShapeDtypeStruct(w_qkv.shape, low),
-            jax.ShapeDtypeStruct((64 * rows_b, width), low),
+            jax.ShapeDtypeStruct((left.shape[1], width), low),
             jax.ShapeDtypeStruct(gain, jnp.float32),
             jax.ShapeDtypeStruct((rows_all, width), low),
         ),
@@ -1446,12 +1726,13 @@
         out_specs=(any_, any_, vmem, vmem),
         scratch_shapes=[
             pltpu.VMEM((4, rows_all, 8 * rows_b), low),
+            pltpu.VMEM((4, rows_all, 4 * rows_c), low),
             pltpu.VMEM(right.shape, low),
             pltpu.VMEM((rows_all, width), low),
             pltpu.VMEM((3, slots, block_len, width), low),
             pltpu.VMEM(w_qkv.shape, low),
-            DMA((6 + slots,)),
-            DMA((6 + slots,)),
+            DMA((10 + slots,)),
+            DMA((10 + slots,)),
             pltpu.VMEM(qkv_heads.shape, low),
             pltpu.VMEM((slots, seq, my_width), low),
             pltpu.VMEM((3, slots, block_len, width), low),
@@ -1471,7 +1752,9 @@
         ]
         + reduce_scratch(rows_a, width)
         + reduce_scratch(rows_b, width)
+        + late_reduce_scratch(rows_c, width)
         + GATHER_SEMS * 2
+        + LATE_GATHER_SEMS
         + GAIN_SEMS,
         compiler_params=pltpu.CompilerParams(
             collective_id=collective_id, has_side_effects=True, vmem_limit_bytes=VMEM_BYTES
@@ -1538,14 +1821,14 @@
     per_unit = unit_rows // part_rows
     parts = master.reshape(capacity * per_unit, part_rows, width)
 
-    def units_at(chunk, per, wanted):
+    def units_at(chunk, per, wanted, start=0):
         at = wanted[..., None] * (per // part_rows) + jnp.arange(per // part_rows, dtype=jnp.int32)
+        at = at + start // part_rows
         at = at.reshape(-1)
         return unit_of(at // per_unit, chunk), at % per_unit
 
     def pick(unit, inner):
-        owner, rank = unit_places(unit_owner, unit)
-        mine = (owner == shard) & (unit >= 0)
+        mine, rank = own_places(unit_owner, shard, unit)
         return pick_call(jnp.where(mine, rank * per_unit + inner, -1), parts)
 
     def piece_rows(count, pieces):
@@ -1562,11 +1845,16 @@
                 for c in range(2)
             ]
         )
-        per_a, per_b = piece_rows(rows_a, 64), piece_rows(rows_b, 64)
-        at_pieces = [units_at(0, per_a, wanted), units_at(1, per_b, wanted)]
+        late = jnp.stack([jnp.stack([((z * 2 + c) * 2 + y) * 2 + q for q in range(2)]) for c in range(2)])
+        per_a, per_b = piece_rows(rows_a, 64), piece_rows(rows_b, 64) - ROWS_C // 2
+        at_pieces = [
+            units_at(0, per_a, wanted),
+            units_at(1, per_b, wanted),
+            units_at(1, ROWS_C, late, 64 * per_b),
+        ]
         given = pick(*(jnp.concatenate(both) for both in zip(*at_pieces)))
         stack_a, stack_b, qkv_heads, wide, lse, mixed_low, norm_one = front_call(
-            given, per_a, per_b, flat_tokens, norm_gains, cos_seq, sin_seq, lengths, slots, block_len, 0
+            given, per_a, per_b, ROWS_C, flat_tokens, norm_gains, cos_seq, sin_seq, lengths, slots, block_len, 0
         )
     else:
         wanted = ctx * groups + jnp.arange(groups, dtype=jnp.int32)
@@ -1633,22 +1921,18 @@
         )
         gain_grad = lax.psum(gain_part.at[0].set(grad_gain_one), BOTH)
     token_grad = token_grad.reshape(slots, block_len, width)
-    gain_grad = gain_grad[:2]
     all_a = all_a.reshape(-1, unit_rows, width)
     all_b = all_b.reshape(-1, unit_rows, width)
 
     every = jnp.arange(units, dtype=jnp.int32)
-    rank = unit_places(unit_owner, every)[1]
+    rank = own_places(unit_owner, shard, every)[1]
     here = (unit_owner == shard) & (rank == jnp.arange(capacity, dtype=jnp.int32)[:, None])
     unit_of_slot = jnp.sum(jnp.where(here, every + 1, 0), axis=1) - 1
     kind = jnp.where(unit_of_slot < 0, -1, (unit_of_slot >= split).astype(jnp.int32))
     at_a = jnp.where(kind == 0, unit_of_slot, 0)
     at_b = jnp.where(kind == 1, block_of(unit_of_slot), 0)
-    new_master, new_first, new_second = adam_call(
-        kind, at_a, at_b, all_a, all_b, master, first_moment, second_moment
-    )
-    new_gains, new_gain_first, new_gain_second = adam_update(
-        norm_gains, gain_grad, gain_first, gain_second, rate_gain, 0.0
+    new_master, new_first, new_second, new_gains, new_gain_first, new_gain_second = adam_call(
+        kind, at_a, at_b, all_a, all_b, gain_grad, (norm_gains, gain_first, gain_second), master, first_moment, second_moment
     )
     return (
         output,

time: 486 us -> 458 us (0.942)
  Pallas kernels: 477 us -> 453 us
    pallas_call x1, Pallas kernels: 246 us -> 237 us  [back_call(): pl.pallas_call(back_kernel, out_shape=(jax.ShapeDtypeStruct(w_qkv.shape,...]
    pallas_call x1, Pallas kernels: 154 us -> 148 us  [front_call(): pl.pallas_call(front_kernel, out_shape=(stack_a, stack_b, jax.ShapeDtypeS...]
    pallas_call x1, Pallas kernels: 46.1 us -> 39.7 us  [adam_call(): pl.pallas_call(functools.partial(adam_kernel, per), grid_spec=pltpu.Prefe...]
where the time goes in v5:
time: 458 us
  Pallas kernels  453 us (99%)
    pallas_call x1, Pallas kernels, back_call(): pl.pallas_call(back_kernel, out_shape=(jax.ShapeDtypeStruct(w_qkv.shape,...  237 us
    pallas_call x1, Pallas kernels, front_call(): pl.pallas_call(front_kernel, out_shape=(stack_a, stack_b, jax.ShapeDtypeS...  148 us
    pallas_call x1, Pallas kernels, adam_call(): pl.pallas_call(functools.partial(adam_kernel, per), grid_spec=pltpu.Prefe...  39.7 us
    pallas_call x1, Pallas kernels, middle_call(): pl.pallas_call(functools.partial(middle_kernel, tile, block_len), out_sha...  22 us

profile of v5, /device:TPU:0, one launch (start us, length us, event | category | flops | bytes accessed | tf_op | source)
XLA Modules:
  0.0 457.8 jit_solution(5471355159603581274)
XLA Ops:
  0.7 0.1 add_bitcast_fusion.2
  0.8 0.1 add_bitcast_fusion.6
  0.8 0.1 add_bitcast_fusion.4
  1.0 0.7 broadcast_compare_fusion
  1.6 0.1 convert_reduce_fusion
  1.8 0.1 add_add_fusion
  1.8 0.1 add.223
  2.0 0.1 select_reduce_fusion
  2.1 0.6 compare_select_fusion.3
  2.7 0.1 iota_add_fusion.1
  2.7 0.1 add.206
  2.8 0.1 iota_add_fusion
  2.9 0.1 add.210
  3.0 0.1 pad_add_fusion.1
  3.1 0.2 convert_reduce_fusion.1
  3.3 0.2 fusion.2
  3.5 0.6 fusion.9.part_ref
  4.1 6.5 %pick.1.given_ref = bf16[1536,1024]{1,0:T(8,128)(2,1)} custom-call(s32[96]{0:T(128)} %fusion.9.part_ref, f32[280,16,1024]{2,1,0:T(8,128)} %bitcast.51), custom_call_target="tpu_custom_call" | custom-call | tf_op jit(solution)/shard_map/pick/pallas_call | solution.py:495
  10.6 147.5 %spread_and_attend.1 = (bf16[3072,1024]{1,0:T(8,128)(2,1)}, bf16[9216,1024]{1,0:T(8,128)(2,1)}, bf16[3,2,1024,128]{3,2,1,0:T(8,128)(2,1)}, f32[2,1024,128]{2,1,0...) custom-call(bf16[1536,1024]{1,0:T(8,128)(2,1)} %pick.1.given_ref, ...), custom_call_target="tpu_custom_call" | custom-call | tf_op jit(solution)/shard_map/spread_and_attend/pallas_call | solution.py:1285
  158.2 22.0 %middle.1 = (bf16[256,1024]{1,0:T(8,128)(2,1)}, bf16[256,9216]{1,0:T(8,128)(2,1)}, bf16[3,256,1024]{2,1,0:T(8,128)(2,1)}, bf16[256,1024]{1,0:T(8,128)(2,1)}, f32[256,1024]{1,0:T(8,128)}, /*index=5*/f32[8,1024]{1,0:T(8,128)}) custom-call(bf16[256,1024]{1,0:T(8,128)(2,1)} %bitcast.57, bf16[256,1024]{1,0:T(8,128)(2,1)} %bitcast.53, bf16[256,1024]{1,0:T(8,128)(2,1)} %bitcast.55, ...), custom_call_target="tpu_custom_call" | custom-call | tf_op jit(solution)/shard_map/middle/pallas_call | solution.py:383
  180.1 237.1 %back_and_sum.1 = (bf16[3072,1024]{1,0:T(8,128)(2,1)}, bf16[9216,1024]{1,0:T(8,128)(2,1)}, f32[8,1024]{1,0:T(8,128)}, bf16[256,1024]{1,0:T(8,128)(2,1)}) custom-call(bf16[2,128,1024]{2,1,0:T(8,128)(2,1)} %bitcast.56, bf16[3,2,1024,128]{3,2,1,0:T(8,128)(2,1)} %get-tuple-element.35.qkv_ref, f32[2,1024,128]{2,1,0:T(8,128)} %get-tuple-element.36.wide_ref, ...), custom_call_target="tpu_custom_call" | custom-call | tf_op jit(solution)/shard_map/back_and_sum/pallas_call | solution.py:1717
  417.3 0.0 copy-start
  417.3 39.7 %adamw.1 = (f32[70,64,1024]{2,1,0:T(8,128)}, f32[70,64,1024]{2,1,0:T(8,128)}, f32[70,64,1024]{2,1,0:T(8,128)}, f32[2,1024]{1,0:T(2,128)}, f32[2,1024]{1,0:T(2,128)}, /*index=5*/f32[2,1024]{1,0:T(2,128)}) custom-call(s32[70]{0:T(128)} %get-tuple-element.58.unit_ref, s32[70]{0:T(128)} %get-tuple-element.57.a_ref, s32[70]{0:T(128)} %get-tuple-element.56.b_ref, ...), custom_call_target="tpu_custom_call" | custom-call | tf_op jit(solution)/shard_map/adamw/pallas_call | solution.py:444
  457.0 0.0 copy-done
  457.0 0.8 copy.21
  (8 shorter events, 0.1 us)
Async XLA Ops:
  417.3 39.7 %copy-start = (bf16[256,1024]{1,0:T(8,128)(2,1)S(1)}, bf16[256,1024]{1,0:T(8,128)(2,1)}, u32[]{:S(2)}) copy-start(bf16[256,1024]{1,0:T(8,128)(2,1)} %get-tuple-element.44) | copy-start | bytes 1572868

commit v6 on v5

--- a/solution.py
+++ b/solution.py
@@ -479,14 +479,12 @@
             copy(p).wait()
             out_ref[at(p), :] = got[p].astype(out_ref.dtype)
 
-        @pl.when(part_ref[p] < 0)
-        def _():
-            out_ref[at(p), :] = jnp.zeros((rows, out_ref.shape[1]), out_ref.dtype)
-
         return 0
 
-    lax.fori_loop(0, count, start, 0)
-    lax.fori_loop(0, count, end, 0)
+    unroll = max(u for u in (1, 2, 4, 8) if count % u == 0)
+    lax.fori_loop(0, count, start, 0, unroll=unroll)
+    out_ref[...] = jnp.zeros_like(out_ref)
+    lax.fori_loop(0, count, end, 0, unroll=unroll)
 
 
 def pick_call(part, parts):

time: 458 us -> 458 us (level)
  no operation moved by 1% of the time
where the time goes in v6:
time: 458 us
  Pallas kernels  453 us (99%)
    pallas_call x1, Pallas kernels, back_call(): pl.pallas_call(back_kernel, out_shape=(jax.ShapeDtypeStruct(w_qkv.shape,...  237 us
    pallas_call x1, Pallas kernels, front_call(): pl.pallas_call(front_kernel, out_shape=(stack_a, stack_b, jax.ShapeDtypeS...  148 us
    pallas_call x1, Pallas kernels, adam_call(): pl.pallas_call(functools.partial(adam_kernel, per), grid_spec=pltpu.Prefe...  40.6 us
    pallas_call x1, Pallas kernels, middle_call(): pl.pallas_call(functools.partial(middle_kernel, tile, block_len), out_sha...  22 us

profile of v6, /device:TPU:0, one launch (start us, length us, event | category | flops | bytes accessed | tf_op | source)
XLA Modules:
  0.0 457.5 jit_solution(8941019081451718962)
XLA Ops:
  0.7 0.1 add_bitcast_fusion.2
  0.8 0.1 add_bitcast_fusion.6
  0.8 0.1 add_bitcast_fusion.4
  1.0 0.7 broadcast_compare_fusion
  1.6 0.1 convert_reduce_fusion
  1.8 0.1 add_add_fusion
  1.8 0.1 add.223
  2.0 0.1 select_reduce_fusion
  2.1 0.6 compare_select_fusion.3
  2.7 0.1 iota_add_fusion.1
  2.7 0.1 add.206
  2.8 0.1 iota_add_fusion
  2.9 0.1 add.210
  3.0 0.1 pad_add_fusion.1
  3.1 0.2 convert_reduce_fusion.1
  3.3 0.2 fusion.2
  3.5 0.6 fusion.9.part_ref
  4.1 5.1 %pick.1.given_ref = bf16[1536,1024]{1,0:T(8,128)(2,1)} custom-call(s32[96]{0:T(128)} %fusion.9.part_ref, f32[280,16,1024]{2,1,0:T(8,128)} %bitcast.51), custom_call_target="tpu_custom_call" | custom-call | tf_op jit(solution)/shard_map/pick/pallas_call | solution.py:493
  9.2 147.7 %spread_and_attend.1 = (bf16[3072,1024]{1,0:T(8,128)(2,1)}, bf16[9216,1024]{1,0:T(8,128)(2,1)}, bf16[3,2,1024,128]{3,2,1,0:T(8,128)(2,1)}, f32[2,1024,128]{2,1,0...) custom-call(bf16[1536,1024]{1,0:T(8,128)(2,1)} %pick.1.given_ref, ...), custom_call_target="tpu_custom_call" | custom-call | tf_op jit(solution)/shard_map/spread_and_attend/pallas_call | solution.py:1283
  156.9 22.0 %middle.1 = (bf16[256,1024]{1,0:T(8,128)(2,1)}, bf16[256,9216]{1,0:T(8,128)(2,1)}, bf16[3,256,1024]{2,1,0:T(8,128)(2,1)}, bf16[256,1024]{1,0:T(8,128)(2,1)}, f32[256,1024]{1,0:T(8,128)}, /*index=5*/f32[8,1024]{1,0:T(8,128)}) custom-call(bf16[256,1024]{1,0:T(8,128)(2,1)} %bitcast.57, bf16[256,1024]{1,0:T(8,128)(2,1)} %bitcast.53, bf16[256,1024]{1,0:T(8,128)(2,1)} %bitcast.55, ...), custom_call_target="tpu_custom_call" | custom-call | tf_op jit(solution)/shard_map/middle/pallas_call | solution.py:383
  178.9 237.2 %back_and_sum.1 = (bf16[3072,1024]{1,0:T(8,128)(2,1)}, bf16[9216,1024]{1,0:T(8,128)(2,1)}, f32[8,1024]{1,0:T(8,128)}, bf16[256,1024]{1,0:T(8,128)(2,1)}) custom-call(bf16[2,128,1024]{2,1,0:T(8,128)(2,1)} %bitcast.56, bf16[3,2,1024,128]{3,2,1,0:T(8,128)(2,1)} %get-tuple-element.35.qkv_ref, f32[2,1024,128]{2,1,0:T(8,128)} %get-tuple-element.36.wide_ref, ...), custom_call_target="tpu_custom_call" | custom-call | tf_op jit(solution)/shard_map/back_and_sum/pallas_call | solution.py:1715
  416.1 0.0 copy-start
  416.1 40.6 %adamw.1 = (f32[70,64,1024]{2,1,0:T(8,128)}, f32[70,64,1024]{2,1,0:T(8,128)}, f32[70,64,1024]{2,1,0:T(8,128)}, f32[2,1024]{1,0:T(2,128)}, f32[2,1024]{1,0:T(2,128)}, /*index=5*/f32[2,1024]{1,0:T(2,128)}) custom-call(s32[70]{0:T(128)} %get-tuple-element.58.unit_ref, s32[70]{0:T(128)} %get-tuple-element.57.a_ref, s32[70]{0:T(128)} %get-tuple-element.56.b_ref, ...), custom_call_target="tpu_custom_call" | custom-call | tf_op jit(solution)/shard_map/adamw/pallas_call | solution.py:444
  456.7 0.0 copy-done
  456.7 0.8 copy.21
  (8 shorter events, 0.1 us)
Async XLA Ops:
  416.1 40.6 %copy-start = (bf16[256,1024]{1,0:T(8,128)(2,1)S(1)}, bf16[256,1024]{1,0:T(8,128)(2,1)}, u32[]{:S(2)}) copy-start(bf16[256,1024]{1,0:T(8,128)(2,1)} %get-tuple-element.44) | copy-start | bytes 1572868
